TPU v7x, 32 devices: a whole 2x2x4 slice. The times are simulated.
32 devices in a mesh: seq: 4 (over x, core), blk: 8 (over z, y).
Axes of the slice: x: 2, y: 2, z: 4, core: 2. Of those that a mesh axis runs over, the one named last changes fastest.
Arguments:
- patches: bfloat16 [8192, 1280], P(('seq', 'blk')), may hold values from -40 to 40
- vis_gain: float32 [1280], replicated, may hold values from 0.1 to 1.9
- vis_up: bfloat16 [5120, 1280], P('seq'), may hold values from -0.15625 to 0.15625
- vis_bias: float32 [5120], P('seq'), may hold values from -4 to 4
- vis_down: bfloat16 [5120, 1280], P('seq'), may hold values from -0.078125 to 0.078125
- merge_gain: float32 [1280], replicated, may hold values from 0.1 to 1.9
- merge_proj: bfloat16 [5120, 1280], replicated, may hold values from -0.078125 to 0.078125
- text_embed: bfloat16 [4096, 1280], P(('seq', 'blk')), may hold values from -40 to 40
- slot_index: int32 [2048], P(('seq', 'blk')), may hold values from 0 to 4095, as said below
- text_gain: float32 [1280], replicated, may hold values from 0.1 to 1.9
- text_up: bfloat16 [5120, 1280], P('blk'), may hold values from -0.15625 to 0.15625
- text_down: bfloat16 [5120, 1280], P('blk'), may hold values from -0.078125 to 0.078125
Outputs:
- hidden_out: bfloat16 [4096, 1280], P(('seq', 'blk'))
Inputs may be any that keep to these rules, and one draw needn't show every extreme that they name: slot_index values are distinct. The merged rows held by one device go to prompt tokens held by devices with the same seq index. Each device sends either no merged rows or exactly 16 merged rows to each device of its blk group; in every draw some device receives 16 rows from every device of its blk group.
All inputs are finite; a program needn't handle non-finite values.
Results may differ from a plain program's by a relative error of at most 0.015.
Values may be sent and summed in bfloat16 or wider, within the bound.
No kernel may reach another device: no remote copies, remote signals or barrier semaphores. Data moves between devices by JAX's collectives and lax.ppermute only.
A program may use at most 192 MiB of HBM per device.

v0:
```python
import jax
import jax.numpy as jnp
from jax import lax
from jax.sharding import PartitionSpec as P


def normalize(values, row_gain):
    values = values.astype(jnp.float32)
    center = values - jnp.mean(values, axis=-1, keepdims=True)
    spread = jnp.mean(center * center, axis=-1, keepdims=True)
    return center * lax.rsqrt(spread + 1e-06) * row_gain


def up_project(rows_in, up_piece):
    return lax.dot_general(
        rows_in, up_piece, (((1,), (1,)), ((), ())), preferred_element_type=jnp.float32
    )


def per_device(
    patches,
    vis_gain,
    vis_up,
    vis_bias,
    vis_down,
    merge_gain,
    merge_proj,
    text_embed,
    slot_index,
    text_gain,
    text_up,
    text_down,
):
    rows_here = patches.shape[0]
    width = patches.shape[1]
    vis_normed = normalize(patches, vis_gain).astype(jnp.bfloat16)
    gathered = lax.all_gather(vis_normed, "seq", axis=0, tiled=True)
    sliced = gathered
    hidden = jax.nn.gelu(up_project(sliced, vis_up) + vis_bias, approximate=True).astype(
        jnp.bfloat16
    )
    vis_mlp = lax.psum_scatter(
        jnp.dot(hidden, vis_down, preferred_element_type=jnp.float32).astype(jnp.bfloat16),
        "seq",
        scatter_dimension=0,
        tiled=True,
    ).astype(jnp.float32)
    vis_out = patches.astype(jnp.float32) + vis_mlp
    merge_normed = normalize(vis_out, merge_gain).astype(jnp.bfloat16)
    joined = merge_normed.reshape(rows_here // 4, 4 * width)
    merged = jnp.dot(joined, merge_proj, preferred_element_type=jnp.float32).astype(jnp.bfloat16)
    cycle_size = lax.axis_size("blk")
    merged_count = slot_index.shape[0]
    token_count = text_embed.shape[0]
    capacity = 2 * merged_count // cycle_size
    target = slot_index // token_count % cycle_size
    position = slot_index % token_count
    one_hot = (target[:, None] == jnp.arange(cycle_size, dtype=jnp.int32)[None, :]).astype(
        jnp.int32
    )
    rank_in = jnp.sum((jnp.cumsum(one_hot, axis=0) - one_hot) * one_hot, axis=1)
    buffer_slot = target * capacity + rank_in
    send_rows = jnp.zeros((cycle_size * capacity, width), jnp.bfloat16).at[buffer_slot].set(merged)
    send_where = (
        jnp.full((cycle_size * capacity,), token_count, jnp.int32).at[buffer_slot].set(position)
    )
    got_rows, got_where = (
        lax.all_to_all(send_rows, "blk", split_axis=0, concat_axis=0, tiled=True),
        lax.all_to_all(send_where, "blk", split_axis=0, concat_axis=0, tiled=True),
    )
    text_rows = text_embed.at[got_where].set(got_rows, mode="drop")
    text_normed = normalize(text_rows, text_gain).astype(jnp.bfloat16)
    gathered_tokens = lax.all_gather(text_normed, "blk", axis=0, tiled=True)
    sliced = gathered_tokens
    hidden = jax.nn.gelu(up_project(sliced, text_up), approximate=True).astype(jnp.bfloat16)
    text_mlp = lax.psum_scatter(
        jnp.dot(hidden, text_down, preferred_element_type=jnp.float32).astype(jnp.bfloat16),
        "blk",
        scatter_dimension=0,
        tiled=True,
    ).astype(jnp.float32)
    return (text_rows.astype(jnp.float32) + text_mlp).astype(jnp.bfloat16)


def solution(mesh):
    placed = (
        P(("seq", "blk"), None),
        P(),
        P("seq", None),
        P("seq"),
        P("seq", None),
        P(),
        P(),
        P(("seq", "blk"), None),
        P(("seq", "blk")),
        P(),
        P("blk", None),
        P("blk", None),
    )
    return jax.shard_map(
        per_device, mesh=mesh, in_specs=placed, out_specs=P(("seq", "blk"), None), check_vma=False
    )
```

profile of v0, /device:TPU:0, one launch (start us, length us, event | category | flops | bytes accessed | tf_op | source)
XLA Modules:
  0.0 265.8 jit_solution(12738826806330860115)
XLA Ops:
  6.5 1.9 copy.16
  8.4 1.3 convert_reduce_fusion
  9.7 1.4 fusion.18
  11.1 2.2 fusion.20
  13.4 28.4 %all-gather.3.cloned.1.call-done = bf16[1024,1280]{1,0:T(8,128)(2,1)} async-done(((bf16[256,1280]{1,0:T(8,128)(2,1)}), bf16[1024,1280]{1,0:T(8,128)(2,1)}) %all-gather.3.cloned.1.call-update) | async-done | bytes 2621456 | tf_op jit(solution)/shard_map/all_gather | solution.py:37
  41.7 11.0 %convolution_convert_fusion.1 = bf16[1024,1280]{1,0:T(8,128)(2,1)} fusion(bf16[1280,1280]{1,0:T(8,128)(2,1)S(1)} %copy-done, bf16[1024,1280]{1,0:T(8,128)(2,1)} %all-gather.3.cloned.1.call-done, bf16[1280,1280]{1,0:T(8,128)(2,1)} %param.14, f32[1280]{0:T(1024)S(1)} %copy-done.5), kind=kOutput, calls=%fused_computation.14 | convolution fusion | flops 6725304320 | bytes 11801600 | tf_op jit(solution)/shard_map/dot_general | solution.py:43
  55.2 5.5 %all-to-all-start = ((s32[8,16,1]{1,2,0:T(1,128)}), s32[8,16,1]{1,2,0:T(1,128)S(1)}, u32[]{:S(2)}, u32[]{:S(2)}) async-start(s32[8,16,1]{1,2,0:T(1,128)} %bitcast), calls=%async_computation | async-start | bytes 8192 | tf_op jit(solution)/shard_map/all_to_all | solution.py:69
  60.8 26.9 %reduce-scatter.3.cloned.1.call-done = bf16[256,1280]{1,0:T(8,128)(2,1)} async-done(((bf16[1024,1280]{1,0:T(8,128)(2,1)}), bf16[256,1280]{1,0:T(8,128)(2,1)}) %reduce-scatter.3.cloned.1.call-update) | async-done | bytes 655376 | tf_op jit(solution)/shard_map/reduce_scatter | solution.py:42
  87.6 1.6 fusion.27
  89.3 1.6 multiply_reduce_fusion
  90.9 1.1 multiply_convert_fusion
  92.1 2.3 reshape.76
  94.3 7.3 %convolution_convert_fusion.2 = bf16[64,1280]{1,0:T(8,128)(2,1)S(1)} fusion(bf16[64,5120]{1,0:T(8,128)(2,1)} %reshape.76, bf16[5120,1280]{1,0:T(8,128)(2,1)} %param.18), kind=kOutput, calls=%fused_computation.23 | convolution fusion | flops 838942720 | bytes 13926400 | tf_op jit(solution)/shard_map/dot_general | solution.py:51
  101.6 1.6 scatter_custom_fusion.1
  103.2 5.5 %all-to-all-start.1 = ((bf16[8,16,1280]{2,1,0:T(8,128)(2,1)}), bf16[8,16,1280]{2,1,0:T(8,128)(2,1)}, u32[]{:S(2)}, u32[]{:S(2)}) async-start(bf16[8,16,1280]{2,1,0:T(8,128)(2,1)} %bitcast.14), calls=%async_computation.2 | async-start | bytes 655360 | tf_op jit(solution)/shard_map/all_to_all | solution.py:68
  110.0 9.1 %all-to-all-done.1 = bf16[8,16,1280]{2,1,0:T(8,128)(2,1)} async-done(((bf16[8,16,1280]{2,1,0:T(8,128)(2,1)}), bf16[8,16,1280]{2,1,0:T(8,128)(2,1)}, u32[]{:S(2)}, u32[]{:S(2)}) %all-to-all-start.1) | async-done | bytes 327712 | tf_op jit(solution)/shard_map/all_to_all | solution.py:68
  119.2 3.3 %scatter_fusion = bf16[128,1280]{1,0:T(8,128)(2,1)} fusion(bf16[128,1280]{1,0:T(8,128)(2,1)} %copy.16, s32[128]{0:T(128)S(1)} %fusion.38, bf16[128,1280]{1,0:T(8,128)(2,1)} %bitcast.3), kind=kCustom, calls=%fused_computation.2 | custom fusion | bytes 983552 | tf_op jit(solution)/shard_map/scatter | solution.py:71
  122.5 1.1 convert_reduce_fusion.1
  123.6 1.2 fusion.30
  124.8 1.9 fusion.32
  127.0 52.7 %all-gather.5.cloned.1.call-done = bf16[1024,1280]{1,0:T(8,128)(2,1)} async-done(((bf16[128,1280]{1,0:T(8,128)(2,1)}), bf16[1024,1280]{1,0:T(8,128)(2,1)}) %all-gather.5.cloned.1.call-update) | async-done | bytes 2621456 | tf_op jit(solution)/shard_map/all_gather | solution.py:73
  179.6 8.7 %convolution_convert_fusion = bf16[1024,1280]{1,0:T(8,128)(2,1)} fusion(bf16[640,1280]{1,0:T(8,128)(2,1)} %param.23, bf16[1024,1280]{1,0:T(8,128)(2,1)} %all-gather.5.cloned.1.call-done, bf16[640,1280]{1,0:T(8,128)(2,1)} %param.22), kind=kOutput, calls=%fused_computation.13 | convolution fusion | flops 3362652160 | bytes 8519680 | tf_op jit(solution)/shard_map/dot_general | solution.py:77
  188.3 69.1 %reduce-scatter.5.cloned.1.call-done = bf16[128,1280]{1,0:T(8,128)(2,1)} async-done(((bf16[1024,1280]{1,0:T(8,128)(2,1)}), bf16[128,1280]{1,0:T(8,128)(2,1)}) %reduce-scatter.5.cloned.1.call-update) | async-done | bytes 327696 | tf_op jit(solution)/shard_map/reduce_scatter | solution.py:76
  257.4 1.9 fusion.33
  (40 shorter events, 4.1 us)
Async XLA Ops:
  6.5 35.2 %copy-start = (bf16[1280,1280]{1,0:T(8,128)(2,1)S(1)}, bf16[1280,1280]{1,0:T(8,128)(2,1)}, u32[]{:S(2)}) copy-start(bf16[1280,1280]{1,0:T(8,128)(2,1)} %param.16) | copy-start | bytes 9830404
  6.5 35.2 %copy-start.5 = (f32[1280]{0:T(1024)S(1)}, f32[1280]{0:T(1024)}, u32[]{:S(2)}) copy-start(f32[1280]{0:T(1024)} %param.15) | copy-start | bytes 15364
  6.5 35.2 %all-gather.3.cloned.1.call-start = ((), (), s32[]{:S(2)}) async-start(), calls=%async_computation.4 | async-start | bytes 3276800 | tf_op jit(solution)/shard_map/all_gather | solution.py:37
  13.3 74.3 %reduce-scatter.3.cloned.1.call-start = ((), (), s32[]{:S(2)}) async-start(), calls=%async_computation.5 | async-start | bytes 3276800 | tf_op jit(solution)/shard_map/reduce_scatter | solution.py:42
  52.7 0.7 copy-start.6
  52.7 38.2 %copy-start.3 = (f32[1280]{0:T(1024)S(1)}, f32[1280]{0:T(1024)}, u32[]{:S(2)}) copy-start(f32[1280]{0:T(1024)} %param.17) | copy-start | bytes 15364
  55.2 48.0 %all-to-all-start = ((s32[8,16,1]{1,2,0:T(1,128)}), s32[8,16,1]{1,2,0:T(1,128)S(1)}, u32[]{:S(2)}, u32[]{:S(2)}) async-start(s32[8,16,1]{1,2,0:T(1,128)} %bitcast), calls=%async_computation | async-start | bytes 8192 | tf_op jit(solution)/shard_map/all_to_all | solution.py:69
  87.6 3.3 %copy-start.1 = (bf16[256,1280]{1,0:T(8,128)(2,1)S(1)}, bf16[256,1280]{1,0:T(8,128)(2,1)}, u32[]{:S(2)}) copy-start(bf16[256,1280]{1,0:T(8,128)(2,1)} %param.12) | copy-start | bytes 1966084
  87.6 3.3 %copy-start.2 = (bf16[256,1280]{1,0:T(8,128)(2,1)S(1)}, bf16[256,1280]{1,0:T(8,128)(2,1)}, u32[]{:S(2)}) copy-start(bf16[256,1280]{1,0:T(8,128)(2,1)} %reduce-scatter.3.cloned.1.call-done) | copy-start | bytes 1966084
  103.2 16.0 %all-to-all-start.1 = ((bf16[8,16,1280]{2,1,0:T(8,128)(2,1)}), bf16[8,16,1280]{2,1,0:T(8,128)(2,1)}, u32[]{:S(2)}, u32[]{:S(2)}) async-start(bf16[8,16,1280]{2,1,0:T(8,128)(2,1)} %bitcast.14), calls=%async_computation.2 | async-start | bytes 655360 | tf_op jit(solution)/shard_map/all_to_all | solution.py:68
  108.7 70.9 %all-gather.5.cloned.1.call-start = ((), (), s32[]{:S(2)}) async-start(), calls=%async_computation.6 | async-start | bytes 2949120 | tf_op jit(solution)/shard_map/all_gather | solution.py:73
  119.2 5.6 %copy-start.4 = (f32[1280]{0:T(1024)S(1)}, f32[1280]{0:T(1024)}, u32[]{:S(2)}) copy-start(f32[1280]{0:T(1024)} %param.21) | copy-start | bytes 15364
  126.7 130.7 %reduce-scatter.5.cloned.1.call-start = ((), (), s32[]{:S(2)}) async-start(), calls=%async_computation.7 | async-start | bytes 2949120 | tf_op jit(solution)/shard_map/reduce_scatter | solution.py:76
Sparse Core Ops, SparseCore 0:
  13.4 28.2 all-gather.2
  52.9 34.6 reduce-scatter.2
  126.9 52.7 all-gather.4
  188.4 68.9 reduce-scatter.4
where the time goes:
time: 267 us; the launch traced here: 266 us
  waiting for transfers between devices  186 us (70%)
  matrix products  27 us (10%)
  other arithmetic  16.4 us (6%)
  between operations  13.2 us (5%)
  local copies, waits for them, and re-layouts  11.7 us (4%)
  starting transfers between devices  11.3 us (4%)
    reduce_scatter x1, waiting for transfers between devices, per_device(): lax.psum_scatter(jnp.dot(hidden, text_down, preferred_element_type=jnp.fl...  69.1 us
    all_gather x1, waiting for transfers between devices, per_device(): gathered_tokens = lax.all_gather(text_normed, 'blk', axis=0, tiled=True)  52.7 us
    all_gather x1, waiting for transfers between devices, per_device(): gathered = lax.all_gather(vis_normed, 'seq', axis=0, tiled=True)  28.4 us
    reduce_scatter x1, waiting for transfers between devices, per_device(): lax.psum_scatter(jnp.dot(hidden, vis_down, preferred_element_type=jnp.flo...  26.9 us
    dot_general x1, matrix products, per_device(): jnp.dot(hidden, vis_down, preferred_element_type=jnp.float32)  11 us
    all_to_all x1, waiting for transfers between devices, per_device(): lax.all_to_all(send_rows, 'blk', split_axis=0, concat_axis=0, tiled=True)  9.14 us
    dot_general x1, matrix products, per_device(): jnp.dot(hidden, text_down, preferred_element_type=jnp.float32)  8.66 us
    dot_general x1, matrix products, per_device(): jnp.dot(joined, merge_proj, preferred_element_type=jnp.float32)  7.29 us
  transfers between devices with their start and end apart: 6, of which 5 were waited for; matrix products, arithmetic and copies ran while one was open for 7% of the time, Pallas kernels for 0%

commit v1 on v0

v1 whole, which is shorter than its diff:
```python
import functools

import jax
import jax.numpy as jnp
from jax import lax
from jax.experimental import pallas as pl
from jax.experimental.pallas import tpu as pltpu
from jax.sharding import PartitionSpec as P

F32 = jnp.float32
BF16 = jnp.bfloat16
ANY = pl.BlockSpec(memory_space=pl.ANY)
VMEM = pl.BlockSpec(memory_space=pltpu.VMEM)
PARAMS = pltpu.CompilerParams(vmem_limit_bytes=48 * 1024 * 1024)


def normalize(values, row_gain):
    values = values.astype(F32)
    center = values - jnp.mean(values, axis=-1, keepdims=True)
    spread = jnp.mean(center * center, axis=-1, keepdims=True)
    return center * lax.rsqrt(spread + 1e-06) * row_gain


def gelu(v):
    return 0.5 * v * (1.0 + jnp.tanh(0.7978845608028654 * (v + 0.044715 * (v * v * v))))


def up_project(rows_in, up_piece):
    return lax.dot_general(rows_in, up_piece, (((1,), (1,)), ((), ())), preferred_element_type=F32)


def swap(x, axis, bit):
    size = lax.axis_size(axis)
    return lax.ppermute(x, axis, [(i, i ^ bit) for i in range(size)])


def plane_rows(patches):
    rows = patches.shape[0]
    count = rows // 8
    place = lax.broadcasted_iota(jnp.int32, (rows, rows), 0)
    source = lax.broadcasted_iota(jnp.int32, (rows, rows), 1)
    half, plane, window = place // (4 * count), place // count % 4, place % count
    order = (source == 4 * (count * half + window) + plane).astype(BF16)
    return jnp.dot(order, patches, preferred_element_type=F32)


def norm_patches_kernel(patches_ref, gain_ref, first_ref, second_ref):
    rows = patches_ref.shape[0]
    normed = normalize(plane_rows(patches_ref[...]), gain_ref[...]).astype(BF16)
    first_ref[...] = normed[: rows // 2]
    second_ref[...] = normed[rows // 2 :]


def norm_patches(patches, gain):
    rows, width = patches.shape
    half = jax.ShapeDtypeStruct((rows // 2, width), BF16)
    return pl.pallas_call(
        norm_patches_kernel,
        out_shape=(half, half),
        in_specs=[VMEM, VMEM],
        out_specs=(VMEM, VMEM),
        compiler_params=PARAMS,
        name="norm_patches",
    )(patches, gain.reshape(1, width))


def load_tiles(tiles, scratch, sems):
    copies, number = [], 0
    for place, pieces in enumerate(tiles):
        at, mine = 0, []
        for ref, first, rows in pieces:
            copy = pltpu.make_async_copy(
                ref.at[pl.ds(first, rows)], scratch.at[place, pl.ds(at, rows)], sems.at[number]
            )
            copy.start()
            mine.append(copy)
            at += rows
            number += 1
        copies.append(mine)
    return copies


def feed_forward(rows, biases, up_copies, up, down_copies, down):
    total = None
    for tile in range(len(up_copies)):
        for copy in up_copies[tile]:
            copy.wait()
        hidden = up_project(rows, up[tile])
        if biases is not None:
            hidden = hidden + biases[tile]
        hidden = gelu(hidden).astype(BF16)
        for copy in down_copies[tile]:
            copy.wait()
        part = jnp.dot(hidden, down[tile], preferred_element_type=F32)
        total = part if total is None else total + part
    return total


def vision_kernel(row_count, *refs):
    row_refs = refs[:row_count]
    up_a, bias_a, down_a, up_b, bias_b, down_b, out_ref, up, down, up_sems, down_sems = refs[row_count:]
    tile = up.shape[1]
    spans = range(0, up_a.shape[0], tile)
    up_copies = load_tiles([[(ref, at, tile)] for ref in (up_a, up_b) for at in spans], up, up_sems)
    down_copies = load_tiles([[(ref, at, tile)] for ref in (down_a, down_b) for at in spans], down, down_sems)
    biases = [ref[:, pl.ds(at, tile)] for ref in (bias_a, bias_b) for at in spans]
    rows = jnp.concatenate([ref[...] for ref in row_refs], axis=0) if row_count > 1 else row_refs[0][...]
    total = feed_forward(rows, biases, up_copies, up, down_copies, down)
    out_ref[...] = total.astype(out_ref.dtype)


def vision_feed_forward(row_parts, weights, out_type):
    (up_a, bias_a, down_a), (up_b, bias_b, down_b) = weights
    width = up_a.shape[1]
    units = up_a.shape[0]
    tile = units // 2
    tiles = 4
    rows = sum(part.shape[0] for part in row_parts)
    return pl.pallas_call(
        functools.partial(vision_kernel, len(row_parts)),
        out_shape=jax.ShapeDtypeStruct((rows, width), out_type),
        in_specs=[VMEM] * len(row_parts) + [ANY, VMEM, ANY, ANY, VMEM, ANY],
        out_specs=VMEM,
        scratch_shapes=[
            pltpu.VMEM((tiles, tile, width), BF16),
            pltpu.VMEM((tiles, tile, width), BF16),
            pltpu.SemaphoreType.DMA((tiles,)),
            pltpu.SemaphoreType.DMA((tiles,)),
        ],
        compiler_params=PARAMS,
        cost_estimate=pl.CostEstimate(
            flops=8 * rows * width * units, bytes_accessed=8 * width * units, transcendentals=2 * rows * units
        ),
        name="vision_feed_forward",
    )(*row_parts, up_a, bias_a.reshape(1, units), down_a, up_b, bias_b.reshape(1, units), down_b)


def merge_kernel(patches_ref, own_ref, first_ref, second_ref, gain_ref, proj_ref, place_ref, out_ref, proj, sems):
    rows, width = patches_ref.shape
    count = rows // 8
    copies = load_tiles([[(proj_ref, plane * width, width)] for plane in range(4)], proj, sems)
    wide = plane_rows(patches_ref[...])
    merged = None
    for plane in range(4):
        halves = []
        for half, back_ref in enumerate((first_ref, second_ref)):
            vis_out = (
                wide[4 * count * half + plane * count :][:count]
                + own_ref[pl.ds(4 * count * half + plane * count, count), :]
                + back_ref[pl.ds(plane * count, count), :].astype(F32)
            )
            halves.append(normalize(vis_out, gain_ref[...]).astype(BF16))
        copies[plane][0].wait()
        part = jnp.dot(jnp.concatenate(halves, axis=0), proj[plane], preferred_element_type=F32)
        merged = part if merged is None else merged + part
    placed = jnp.dot(place_ref[...], merged.astype(BF16), preferred_element_type=F32)
    out_ref[...] = placed.astype(BF16)


def merge_rows(patches, own, first, second, gain, proj, place):
    rows, width = patches.shape
    return pl.pallas_call(
        merge_kernel,
        out_shape=jax.ShapeDtypeStruct((place.shape[0], width), BF16),
        in_specs=[VMEM] * 5 + [ANY, VMEM],
        out_specs=VMEM,
        scratch_shapes=[
            pltpu.VMEM((4, width, width), BF16),
            pltpu.SemaphoreType.DMA((4,)),
        ],
        compiler_params=PARAMS,
        cost_estimate=pl.CostEstimate(
            flops=2 * rows * width * width, bytes_accessed=8 * width * width, transcendentals=rows
        ),
        name="merge_rows",
    )(patches, own, first, second, gain.reshape(1, width), proj, place)


def text_kernel(piece_count, embed_ref, got_ref, pick_ref, gain_ref, up_ref, down_ref, *refs):
    pieces = refs[:piece_count]
    out_ref, up, down, up_sems, down_sems = refs[piece_count:]
    units = up_ref.shape[0]
    part = pieces[0].shape[0] // 2
    per_tile = units // part
    groups = [pieces[at : at + per_tile] for at in range(0, piece_count, per_tile)]
    up_copies = load_tiles(
        [[(up_ref, 0, units)]] + [[(ref, 0, part) for ref in group] for group in groups], up, up_sems
    )
    down_copies = load_tiles(
        [[(down_ref, 0, units)]] + [[(ref, part, part) for ref in group] for group in groups], down, down_sems
    )
    pick = pick_ref[...]
    picked = jnp.dot(pick, got_ref[...], preferred_element_type=F32)
    taken = jnp.sum(pick.astype(F32), axis=1, keepdims=True)
    text_rows = jnp.where(taken > 0.5, picked, embed_ref[...].astype(F32))
    normed = normalize(text_rows, gain_ref[...]).astype(BF16)
    total = feed_forward(normed, None, up_copies, up, down_copies, down)
    if out_ref.dtype == F32:
        total = text_rows + total
    out_ref[...] = total.astype(out_ref.dtype)


def text_feed_forward(embed, got, pick, gain, up, down, pieces, out_type):
    rows, width = embed.shape
    units = up.shape[0]
    loads = 1 + len(pieces)
    tiles = 4
    return pl.pallas_call(
        functools.partial(text_kernel, len(pieces)),
        out_shape=jax.ShapeDtypeStruct((rows, width), out_type),
        in_specs=[VMEM] * 4 + [ANY] * (2 + len(pieces)),
        out_specs=VMEM,
        scratch_shapes=[
            pltpu.VMEM((tiles, units, width), BF16),
            pltpu.VMEM((tiles, units, width), BF16),
            pltpu.SemaphoreType.DMA((loads,)),
            pltpu.SemaphoreType.DMA((loads,)),
        ],
        compiler_params=PARAMS,
        cost_estimate=pl.CostEstimate(
            flops=16 * rows * width * units, bytes_accessed=16 * width * units, transcendentals=4 * rows * units
        ),
        name="text_feed_forward",
    )(embed, got, pick, gain.reshape(1, width), up, down, *pieces)


def gather_text_weights(text_up, text_down):
    units = text_up.shape[0]
    core = lax.axis_index("seq") % 2
    quarter = units // 4
    halves = []
    for half in range(2):
        first = core * (units // 2) + half * quarter
        halves.append(
            jnp.concatenate(
                [lax.dynamic_slice_in_dim(w, first, quarter, 0) for w in (text_up, text_down)], axis=0
            )
        )
    near_a, near_b = swap(halves[0], "blk", 1), swap(halves[1], "blk", 1)
    far_a, far_b = swap(halves[0], "blk", 2), swap(halves[1], "blk", 2)
    both_a, both_b = swap(far_a, "blk", 1), swap(near_b, "blk", 2)
    arrived = [(near_a, near_b), (far_a, far_b), (both_a, both_b)]
    pieces = []
    for pair in arrived:
        pieces += [*pair, *(swap(w, "seq", 1) for w in pair)]
    return pieces


def vision_part(patches, vis_gain, vis_up, vis_bias, vis_down):
    weights = [(vis_up, vis_bias, vis_down), tuple(swap(w, "seq", 1) for w in (vis_up, vis_bias, vis_down))]
    first, second = norm_patches(patches, vis_gain)
    far_first, far_second = swap(first, "seq", 2), swap(second, "seq", 2)
    back_first = swap(vision_feed_forward([far_first], weights, BF16), "seq", 2)
    back_second = swap(vision_feed_forward([far_second], weights, BF16), "seq", 2)
    own = vision_feed_forward([first, second], weights, F32)
    return own, back_first, back_second


def rank_of(target, cycle_size):
    one_hot = (target[..., None] == jnp.arange(cycle_size, dtype=jnp.int32)).astype(jnp.int32)
    return jnp.sum((jnp.cumsum(one_hot, axis=-2) - one_hot) * one_hot, axis=-1)


def per_device(
    patches,
    vis_gain,
    vis_up,
    vis_bias,
    vis_down,
    merge_gain,
    merge_proj,
    text_embed,
    slot_index,
    text_gain,
    text_up,
    text_down,
):
    cycle_size = lax.axis_size("blk")
    merged_count = slot_index.shape[0]
    token_count, width = text_embed.shape
    capacity = 2 * merged_count // cycle_size
    me = lax.axis_index("blk")
    paired = cycle_size == 8

    slots = lax.all_gather(slot_index, "blk", axis=0)
    target = slots // token_count % cycle_size
    position = slots % token_count
    rank = rank_of(target, cycle_size)
    my_target = lax.dynamic_index_in_dim(target, me, 0, keepdims=False)
    my_rank = lax.dynamic_index_in_dim(rank, me, 0, keepdims=False)
    sides = 2 if paired else 1
    dest = jnp.arange(cycle_size, dtype=jnp.int32)[:, None, None, None]
    side = jnp.arange(sides, dtype=jnp.int32)[None, :, None, None]
    nth = jnp.arange(capacity, dtype=jnp.int32)[None, None, :, None]
    owner = dest ^ (4 * side)
    place = ((my_target == owner) & (my_rank == nth)).astype(BF16)
    place = place.reshape(cycle_size * sides * capacity, merged_count)

    def pick_for(which):
        theirs = (target == (me ^ (4 * which)))[:, None, :] & (
            rank[:, None, :] == jnp.arange(capacity, dtype=jnp.int32)[None, :, None]
        )
        where = jnp.max(jnp.where(theirs, position[:, None, :], -1), axis=-1)
        tokens = jnp.arange(token_count, dtype=jnp.int32)[:, None, None]
        chosen = (where[None] == tokens).astype(BF16)
        blank = jnp.zeros_like(chosen)
        parts = [chosen if s == which else blank for s in range(sides)]
        return jnp.stack(parts, axis=2).reshape(token_count, cycle_size * sides * capacity)

    if paired:
        pieces = gather_text_weights(text_up, text_down)
        other_embed = swap(text_embed, "blk", 4)
    own, back_first, back_second = vision_part(patches, vis_gain, vis_up, vis_bias, vis_down)
    send = merge_rows(patches, own, back_first, back_second, merge_gain, merge_proj, place)
    got = lax.all_to_all(send, "blk", split_axis=0, concat_axis=0, tiled=True)
    if paired:
        theirs = text_feed_forward(
            other_embed, got, pick_for(1), text_gain, text_up, text_down, pieces, BF16
        )
        mine = text_feed_forward(text_embed, got, pick_for(0), text_gain, text_up, text_down, pieces, F32)
        return (mine + swap(theirs, "blk", 4).astype(F32)).astype(BF16)
    pick = pick_for(0)
    taken = jnp.sum(pick.astype(F32), axis=1, keepdims=True) > 0.5
    text_rows = jnp.where(taken, jnp.dot(pick, got, preferred_element_type=F32), text_embed.astype(F32))
    text_normed = normalize(text_rows, text_gain).astype(BF16)
    gathered_tokens = lax.all_gather(text_normed, "blk", axis=0, tiled=True)
    hidden = gelu(up_project(gathered_tokens, text_up)).astype(BF16)
    text_mlp = lax.psum_scatter(
        jnp.dot(hidden, text_down, preferred_element_type=F32).astype(BF16),
        "blk",
        scatter_dimension=0,
        tiled=True,
    ).astype(F32)
    return (text_rows + text_mlp).astype(BF16)


def solution(mesh):
    placed = (
        P(("seq", "blk"), None),
        P(),
        P("seq", None),
        P("seq"),
        P("seq", None),
        P(),
        P(),
        P(("seq", "blk"), None),
        P(("seq", "blk")),
        P(),
        P("blk", None),
        P("blk", None),
    )
    return jax.shard_map(
        per_device, mesh=mesh, in_specs=placed, out_specs=P(("seq", "blk"), None), check_vma=False
    )
```

time: 267 us -> 141 us (0.53)
  waiting for transfers between devices: 186 us -> 33.7 us
  Pallas kernels: 0 us -> 45.1 us
  matrix products: 27 us -> 0 us
  blocking collectives: 0 us -> 25.1 us
  between operations: 13.2 us -> 0.94 us
  starting transfers between devices: 11.3 us -> 22.8 us
  other arithmetic: 16.4 us -> 6.85 us
  local copies, waits for them, and re-layouts: 11.7 us -> 6.44 us
    reduce_scatter x2 -> x0, waiting for transfers between devices: 96 us -> none  [the longest x1 69.1 us: per_device(): lax.psum_scatter(jnp.dot(hidden, text_down, preferred_element_type=jnp.fl...]
    all_gather x2 -> x0, waiting for transfers between devices: 81 us -> none  [the longest x1 52.7 us: per_device(): gathered_tokens = lax.all_gather(text_normed, 'blk', axis=0, tiled=True)]
    pallas_call x0 -> x7, Pallas kernels: none -> 45.1 us  [the longest x3 20.9 us: vision_feed_forward(): pl.pallas_call(functools.partial(vision_kernel, len(row_parts)), out_shap...]
    ppermute x0 -> x21, waiting for transfers between devices: none -> 33.7 us  [swap(): return lax.ppermute(x, axis, [(i, i ^ bit) for i in range(size)])]
    dot_general x3 -> x0, matrix products: 27 us -> none  [the longest x1 11 us: per_device(): jnp.dot(hidden, vis_down, preferred_element_type=jnp.float32)]
    unnamed x0 -> x1, blocking collectives: none -> 25.1 us
    ppermute x0 -> x21, starting transfers between devices: none -> 17.9 us  [swap(): return lax.ppermute(x, axis, [(i, i ^ bit) for i in range(size)])]
    all_to_all x2 -> x1, waiting for transfers between devices: 9.14 us -> 0.01 us  [per_device(): got = lax.all_to_all(send, 'blk', split_axis=0, concat_axis=0, tiled=True)]
  transfers between devices with their start and end apart: 6 -> 22, of which waited for: 5 -> 6; matrix products, arithmetic and copies ran while one was open for 7% -> 7% of each run, Pallas kernels for 0% -> 26%
where the time goes in v1:
time: 141 us
  Pallas kernels  45.1 us (32%)
  waiting for transfers between devices  33.7 us (24%)
  blocking collectives  25.1 us (18%)
  starting transfers between devices  22.8 us (16%)
  other arithmetic  6.85 us (5%)
  local copies, waits for them, and re-layouts  6.44 us (5%)
    ppermute x21, waiting for transfers between devices, swap(): return lax.ppermute(x, axis, [(i, i ^ bit) for i in range(size)])  33.7 us
    unnamed x1, blocking collectives  25.1 us
    pallas_call x3, Pallas kernels, vision_feed_forward(): pl.pallas_call(functools.partial(vision_kernel, len(row_parts)), out_shap...  20.9 us
    ppermute x21, starting transfers between devices, swap(): return lax.ppermute(x, axis, [(i, i ^ bit) for i in range(size)])  17.9 us
    pallas_call x2, Pallas kernels, text_feed_forward(): pl.pallas_call(functools.partial(text_kernel, len(pieces)), out_shape=jax...  16 us
    pallas_call x1, Pallas kernels, merge_rows(): pl.pallas_call(merge_kernel, out_shape=jax.ShapeDtypeStruct((place.shape[...  6.9 us
    all_to_all x1, starting transfers between devices, per_device(): got = lax.all_to_all(send, 'blk', split_axis=0, concat_axis=0, tiled=True)  4.88 us
    concatenate x2, other arithmetic, gather_text_weights(): jnp.concatenate([lax.dynamic_slice_in_dim(w, first, quarter, 0) for w in...  3.09 us
  transfers between devices with their start and end apart: 22, of which 6 were waited for; matrix products, arithmetic and copies ran while one was open for 7% of the time, Pallas kernels for 26%

profile of v1, /device:TPU:0, one launch (start us, length us, event | category | flops | bytes accessed | tf_op | source)
XLA Modules:
  0.0 140.9 jit_solution(17139829061288006607)
XLA Ops:
  4.8 2.5 %collective-permute-start.3 = (bf16[128,1280]{1,0:T(8,128)(2,1)}, bf16[128,1280]{1,0:T(8,128)(2,1)}, u32[]{:S(2)}, u32[]{:S(2)}) collective-permute-start(bf16[128,1280]{1,0:T(8,128)(2,1)} %get-tuple-element.7.refs_0_), channel_id=1, source_target_pairs={{0,16},{8,24},{16,0},{24,8},{1,17},{9,25},{17,1},{25,9},{2,18},{10... | collective-permute-start | bytes 983048 | tf_op jit(solution)/shard_map/ppermute | solution.py:34
  7.3 2.4 %constant_dynamic-slice_fusion = (bf16[160,1280]{1,0:T(8,128)(2,1)}, bf16[160,1280]{1,0:T(8,128)(2,1)S(1)}, bf16[160,1280]{1,0:T(8,128)(2,1)S(1)}, bf16[160,1280]{1,0:T(8,128)(2,1)}) fusion(bf16[640,1280]{1,0:T(8,128)(2,1)} %down_ref.3, s32[]{:T(128)S(6)} %select_n.49, s32[]{:T(128)S(6)} %select_n.48, bf16[640,1280]{1,0:T(8,128)(2,1)} %up_ref.3), kind=kLoop, calls=%fused_computation.36 | loop fusion | bytes 3276808 | tf_op jit(solution)/shard_map/dynamic_slice | solution.py:236
  10.7 1.5 %collective-permute-start.7 = (bf16[320,1280]{1,0:T(8,128)(2,1)}, bf16[320,1280]{1,0:T(8,128)(2,1)}, u32[]{:S(2)}, u32[]{:S(2)}) collective-permute-start(bf16[320,1280]{1,0:T(8,128)(2,1)} %pad_maximum_fusion), channel_id=1, source_target_pairs={{0,1},{1,0},{2,3},{3,2},{4,5},{5,4},{6,7},{7,6},{8,9},{9,8},{10,11... | collective-permute-start | bytes 2457608 | tf_op jit(solution)/shard_map/ppermute | solution.py:34
  13.7 25.1 %all-reduce.2 = s32[512]{0:T(512)S(1)} all-reduce(s32[512]{0:T(512)S(1)} %dynamic-update-slice), channel_id=2, replica_groups=mesh['seq'=4,'blk'=8] {'blk'}, use_global_device_ids=true, to_apply=%add.2 | all-reduce | flops 512 | bytes 4096
  38.9 1.4 fusion.9
  40.3 2.1 %pad_maximum_fusion.1 = bf16[320,1280]{1,0:T(8,128)(2,1)} fusion(bf16[160,1280]{1,0:T(8,128)(2,1)} %get-tuple-element.15, bf16[160,1280]{1,0:T(8,128)(2,1)} %get-tuple-element.20), kind=kLoop, calls=%fused_computation.1 | loop fusion | flops 1638400 | bytes 1638400 | tf_op jit(solution)/shard_map/concatenate | solution.py:235
  43.0 1.5 %collective-permute-start.8 = (bf16[320,1280]{1,0:T(8,128)(2,1)}, bf16[320,1280]{1,0:T(8,128)(2,1)}, u32[]{:S(2)}, u32[]{:S(2)}) collective-permute-start(bf16[320,1280]{1,0:T(8,128)(2,1)} %pad_maximum_fusion.1), channel_id=1, source_target_pairs={{0,1},{1,0},{2,3},{3,2},{4,5},{5,4},{6,7},{7,6},{8,9},{9,8},{10,11... | collective-permute-start | bytes 2457608 | tf_op jit(solution)/shard_map/ppermute | solution.py:34
  45.4 6.7 %vision_feed_forward.4 = bf16[128,1280]{1,0:T(8,128)(2,1)S(1)} custom-call(bf16[128,1280]{1,0:T(8,128)(2,1)} %collective-permute-done.3.refs_0_, bf16[1280,1280]{1,0:T(8,128)(2,1)S(1)} %copy-done, f32[1,1280]{1,0:T(1,128)S(1)} %reshape.128.refs_3_.refs_2_, bf16[1280,1280]{1,0:T(8,128)(2,1)} %refs_3_.3, ...), custom_call_target="tpu_custom_call" | custom-call | flops 1677721600 | bytes 13107200 | tf_op jit(solution)/shard_map/vision_feed_forward/pallas_call | solution.py:119
  52.1 1.5 %collective-permute-start.4 = (bf16[128,1280]{1,0:T(8,128)(2,1)S(1)}, bf16[128,1280]{1,0:T(8,128)(2,1)S(1)}, u32[]{:S(2)}, u32[]{:S(2)}) collective-permute-start(bf16[128,1280]{1,0:T(8,128)(2,1)S(1)} %vision_feed_forward.4), channel_id=1, source_target_pairs={{0,16},{8,24},{16,0},{24,8},{1,17},{9,25},{17,1},{25,9},{2,18},{10... | collective-permute-start | bytes 983048 | tf_op jit(solution)/shard_map/ppermute | solution.py:34
  53.7 5.7 %vision_feed_forward.5 = bf16[128,1280]{1,0:T(8,128)(2,1)S(1)} custom-call(bf16[128,1280]{1,0:T(8,128)(2,1)S(1)} %collective-permute-done.5.refs_0_, bf16[1280,1280]{1,0:T(8,128)(2,1)S(1)} %copy-done, f32[1,1280]{1,0:T(1,128)S(1)} %reshape.128.refs_3_.refs_2_, bf16[1280,1280]{1,0:T(8,128)(2,1)} %refs_3_.3, ...), custom_call_target="tpu_custom_call" | custom-call | flops 1677721600 | bytes 13107200 | tf_op jit(solution)/shard_map/vision_feed_forward/pallas_call | solution.py:119
  60.0 1.7 %collective-permute-start.12 = (bf16[320,1280]{1,0:T(8,128)(2,1)}, bf16[320,1280]{1,0:T(8,128)(2,1)}, u32[]{:S(2)}, u32[]{:S(2)}) collective-permute-start(bf16[320,1280]{1,0:T(8,128)(2,1)} %pad_maximum_fusion.1), channel_id=1, source_target_pairs={{0,2},{1,3},{2,0},{3,1},{4,6},{5,7},{6,4},{7,5},{8,10},{9,11},{10,... | collective-permute-start | bytes 2457608 | tf_op jit(solution)/shard_map/ppermute | solution.py:34
  62.0 2.5 %collective-permute-start.15 = (bf16[320,1280]{1,0:T(8,128)(2,1)}, bf16[320,1280]{1,0:T(8,128)(2,1)}, u32[]{:S(2)}, u32[]{:S(2)}) collective-permute-start(bf16[320,1280]{1,0:T(8,128)(2,1)} %collective-permute-done.11.refs_4_), channel_id=1, source_target_pairs={{0,1},{1,0},{2,3},{3,2},{4,5},{5,4},{6,7},{7,6},{8,9},{9,8},{10,11... | collective-permute-start | bytes 2457608 | tf_op jit(solution)/shard_map/ppermute | solution.py:34
  64.6 1.9 %collective-permute-done.6.second_ref = bf16[128,1280]{1,0:T(8,128)(2,1)S(1)} collective-permute-done((bf16[128,1280]{1,0:T(8,128)(2,1)S(1)}, bf16[128,1280]{1,0:T(8,128)(2,1)S(1)}, u32[]{:S(2)}, u32[]{:S(2)}) %collective-permute-start.6) | collective-permute-done | bytes 327712 | tf_op jit(solution)/shard_map/ppermute | solution.py:34
  66.9 8.5 %vision_feed_forward.3.own_ref = f32[256,1280]{1,0:T(8,128)S(1)} custom-call(bf16[128,1280]{1,0:T(8,128)(2,1)} %get-tuple-element.7.refs_0_, bf16[128,1280]{1,0:T(8,128)(2,1)S(1)} %copy-done.4, bf16[1280,1280]{1,0:T(8,128)(2,1)S(1)} %copy-done, f32[1,1280]{1,0:T(1,128)S(1)} %reshape.128.refs_3_.refs_2_, bf16[1280,1280]{1,0:T(8,128)(2,1)} %refs_3_.3, ...), custom_call_target="tpu_custom_call" | custom-call | flops 3355443200 | bytes 13107200 | tf_op jit(solution)/shard_map/vision_feed_forward/pallas_call | solution.py:119
  75.4 6.9 %merge_rows.1 = bf16[256,1280]{1,0:T(8,128)(2,1)} custom-call(bf16[256,1280]{1,0:T(8,128)(2,1)S(1)} %copy-done.2, f32[256,1280]{1,0:T(8,128)S(1)} %vision_feed_forward.3.own_ref, bf16[128,1280]{1,0:T(8,128)(2,1)S(1)} %collective-permute-done.4.first_ref, bf16[128,1280]{1,0:T(8,128)(2,1)S(1)} %collective-permute-done.6.second_ref, ...), custom_call_target="tpu_custom_call" | custom-call | flops 838860800 | bytes 13107200 | tf_op jit(solution)/shard_map/merge_rows/pallas_call | solution.py:162
  82.3 4.9 %all-to-all-start = ((bf16[8,32,1280]{2,1,0:T(8,128)(2,1)}), bf16[8,32,1280]{2,1,0:T(8,128)(2,1)S(1)}, u32[]{:S(2)}, u32[]{:S(2)}) async-start(bf16[8,32,1280]{2,1,0:T(8,128)(2,1)} %bitcast.3), calls=%async_computation | async-start | bytes 1310720 | tf_op jit(solution)/shard_map/all_to_all | solution.py:315
  87.3 18.0 %collective-permute-done.19.embed_ref = bf16[128,1280]{1,0:T(8,128)(2,1)} collective-permute-done((bf16[128,1280]{1,0:T(8,128)(2,1)}, bf16[128,1280]{1,0:T(8,128)(2,1)}, u32[]{:S(2)}, u32[]{:S(2)}) %collective-permute-start.19) | collective-permute-done | bytes 327712 | tf_op jit(solution)/shard_map/ppermute | solution.py:34
  106.3 5.3 %collective-permute-done.16.refs_9_ = bf16[320,1280]{1,0:T(8,128)(2,1)} collective-permute-done((bf16[320,1280]{1,0:T(8,128)(2,1)}, bf16[320,1280]{1,0:T(8,128)(2,1)}, u32[]{:S(2)}, u32[]{:S(2)}) %collective-permute-start.16) | collective-permute-done | bytes 819232 | tf_op jit(solution)/shard_map/ppermute | solution.py:34
  112.3 2.0 %collective-permute-done.18.refs_11_ = bf16[320,1280]{1,0:T(8,128)(2,1)} collective-permute-done((bf16[320,1280]{1,0:T(8,128)(2,1)}, bf16[320,1280]{1,0:T(8,128)(2,1)}, u32[]{:S(2)}, u32[]{:S(2)}) %collective-permute-start.18) | collective-permute-done | bytes 819232 | tf_op jit(solution)/shard_map/ppermute | solution.py:34
  114.3 8.0 %text_feed_forward.3 = bf16[128,1280]{1,0:T(8,128)(2,1)S(1)} custom-call(bf16[128,1280]{1,0:T(8,128)(2,1)} %collective-permute-done.19.embed_ref, bf16[256,1280]{1,0:T(8,128)(2,1)S(1)} %bitcast.8, bf16[128,256]{1,0:T(8,128)(2,1)S(1)} %copy.28.pick_ref, f32[1,1280]{1,0:T(1,128)S(1)} %reshape.133.gain_ref, bf16[640,1280]{1,0:T(8,128)(2,1)} %up_ref.3, ...), custom_call_target="tpu_custom_call" | custom-call | flops 1677721600 | bytes 13107200 | tf_op jit(solution)/shard_map/text_feed_forward/pallas_call | solution.py:208
  122.3 2.6 %collective-permute-start.20 = (bf16[128,1280]{1,0:T(8,128)(2,1)S(1)}, bf16[128,1280]{1,0:T(8,128)(2,1)}, u32[]{:S(2)}, u32[]{:S(2)}) collective-permute-start(bf16[128,1280]{1,0:T(8,128)(2,1)S(1)} %text_feed_forward.3), channel_id=1, source_target_pairs={{0,4},{1,5},{2,6},{3,7},{4,0},{5,1},{6,2},{7,3},{8,12},{9,13},{10,... | collective-permute-start | bytes 983048 | tf_op jit(solution)/shard_map/ppermute | solution.py:34
  125.0 8.0 %text_feed_forward.2 = f32[128,1280]{1,0:T(8,128)S(1)} custom-call(bf16[128,1280]{1,0:T(8,128)(2,1)} %embed_ref.1, bf16[256,1280]{1,0:T(8,128)(2,1)S(1)} %bitcast.9, bf16[128,256]{1,0:T(8,128)(2,1)S(1)} %copy.27.pick_ref, f32[1,1280]{1,0:T(1,128)S(1)} %reshape.133.gain_ref, bf16[640,1280]{1,0:T(8,128)(2,1)} %up_ref.3, bf16[640,1280]{1,0:T(8,128)(2,1)} %down_ref.3, ...), custom_call_target="tpu_custom_call" | custom-call | flops 1677721600 | bytes 13107200 | tf_op jit(solution)/shard_map/text_feed_forward/pallas_call | solution.py:208
  133.0 6.1 %collective-permute-done.20 = bf16[128,1280]{1,0:T(8,128)(2,1)} collective-permute-done((bf16[128,1280]{1,0:T(8,128)(2,1)S(1)}, bf16[128,1280]{1,0:T(8,128)(2,1)}, u32[]{:S(2)}, u32[]{:S(2)}) %collective-permute-start.20) | collective-permute-done | bytes 327712 | tf_op jit(solution)/shard_map/ppermute | solution.py:34
  139.1 1.8 %add_convert_fusion = bf16[128,1280]{1,0:T(8,128)(2,1)} fusion(f32[128,1280]{1,0:T(8,128)S(1)} %text_feed_forward.2, bf16[128,1280]{1,0:T(8,128)(2,1)} %collective-permute-done.20), kind=kLoop, calls=%fused_computation.4 | loop fusion | flops 491520 | bytes 1310720 | tf_op jit(solution)/shard_map/convert_element_type | solution.py:321
  (84 shorter events, 11.4 us)
Async XLA Ops:
  0.0 44.7 %collective-permute-start = (bf16[1280,1280]{1,0:T(8,128)(2,1)}, bf16[1280,1280]{1,0:T(8,128)(2,1)}, u32[]{:S(2)}, u32[]{:S(2)}) collective-permute-start(bf16[1280,1280]{1,0:T(8,128)(2,1)} %refs_1_.3), channel_id=1, source_target_pairs={{0,8},{8,0},{16,24},{24,16},{1,9},{9,1},{17,25},{25,17},{2,10},{10... | collective-permute-start | bytes 9830408 | tf_op jit(solution)/shard_map/ppermute | solution.py:34
  0.5 44.9 %collective-permute-start.2 = (bf16[1280,1280]{1,0:T(8,128)(2,1)}, bf16[1280,1280]{1,0:T(8,128)(2,1)}, u32[]{:S(2)}, u32[]{:S(2)}) collective-permute-start(bf16[1280,1280]{1,0:T(8,128)(2,1)} %refs_3_.3), channel_id=1, source_target_pairs={{0,8},{8,0},{16,24},{24,16},{1,9},{9,1},{17,25},{25,17},{2,10},{10... | collective-permute-start | bytes 9830408 | tf_op jit(solution)/shard_map/ppermute | solution.py:34
  0.5 42.0 %collective-permute-start.1 = (f32[1280]{0:T(1024)}, f32[1280]{0:T(1024)S(1)}, u32[]{:S(2)}, u32[]{:S(2)}) collective-permute-start(f32[1280]{0:T(1024)} %param.15), channel_id=1, source_target_pairs={{0,8},{8,0},{16,24},{24,16},{1,9},{9,1},{17,25},{25,17},{2,10},{10... | collective-permute-start | bytes 15368 | tf_op jit(solution)/shard_map/ppermute | solution.py:34
  4.8 38.2 %collective-permute-start.3 = (bf16[128,1280]{1,0:T(8,128)(2,1)}, bf16[128,1280]{1,0:T(8,128)(2,1)}, u32[]{:S(2)}, u32[]{:S(2)}) collective-permute-start(bf16[128,1280]{1,0:T(8,128)(2,1)} %get-tuple-element.7.refs_0_), channel_id=1, source_target_pairs={{0,16},{8,24},{16,0},{24,8},{1,17},{9,25},{17,1},{25,9},{2,18},{10... | collective-permute-start | bytes 983048 | tf_op jit(solution)/shard_map/ppermute | solution.py:34
  9.7 34.8 %copy-start.7 = (f32[1280]{0:T(1024)S(1)}, f32[1280]{0:T(1024)}, u32[]{:S(2)}) copy-start(f32[1280]{0:T(1024)} %param.15) | copy-start | bytes 15364
  9.7 35.7 %copy-start = (bf16[1280,1280]{1,0:T(8,128)(2,1)S(1)}, bf16[1280,1280]{1,0:T(8,128)(2,1)}, u32[]{:S(2)}) copy-start(bf16[1280,1280]{1,0:T(8,128)(2,1)} %refs_1_.3) | copy-start | bytes 9830404
  10.7 49.4 %collective-permute-start.7 = (bf16[320,1280]{1,0:T(8,128)(2,1)}, bf16[320,1280]{1,0:T(8,128)(2,1)}, u32[]{:S(2)}, u32[]{:S(2)}) collective-permute-start(bf16[320,1280]{1,0:T(8,128)(2,1)} %pad_maximum_fusion), channel_id=1, source_target_pairs={{0,1},{1,0},{2,3},{3,2},{4,5},{5,4},{6,7},{7,6},{8,9},{9,8},{10,11... | collective-permute-start | bytes 2457608 | tf_op jit(solution)/shard_map/ppermute | solution.py:34
  42.5 19.6 %collective-permute-start.11 = (bf16[320,1280]{1,0:T(8,128)(2,1)}, bf16[320,1280]{1,0:T(8,128)(2,1)}, u32[]{:S(2)}, u32[]{:S(2)}) collective-permute-start(bf16[320,1280]{1,0:T(8,128)(2,1)} %pad_maximum_fusion), channel_id=1, source_target_pairs={{0,2},{1,3},{2,0},{3,1},{4,6},{5,7},{6,4},{7,5},{8,10},{9,11},{10,... | collective-permute-start | bytes 2457608 | tf_op jit(solution)/shard_map/ppermute | solution.py:34
  43.0 18.7 %collective-permute-start.8 = (bf16[320,1280]{1,0:T(8,128)(2,1)}, bf16[320,1280]{1,0:T(8,128)(2,1)}, u32[]{:S(2)}, u32[]{:S(2)}) collective-permute-start(bf16[320,1280]{1,0:T(8,128)(2,1)} %pad_maximum_fusion.1), channel_id=1, source_target_pairs={{0,1},{1,0},{2,3},{3,2},{4,5},{5,4},{6,7},{7,6},{8,9},{9,8},{10,11... | collective-permute-start | bytes 2457608 | tf_op jit(solution)/shard_map/ppermute | solution.py:34
  44.7 9.0 %collective-permute-start.5 = (bf16[128,1280]{1,0:T(8,128)(2,1)}, bf16[128,1280]{1,0:T(8,128)(2,1)S(1)}, u32[]{:S(2)}, u32[]{:S(2)}) collective-permute-start(bf16[128,1280]{1,0:T(8,128)(2,1)} %copy-done.3), channel_id=1, source_target_pairs={{0,16},{8,24},{16,0},{24,8},{1,17},{9,25},{17,1},{25,9},{2,18},{10... | collective-permute-start | bytes 983048 | tf_op jit(solution)/shard_map/ppermute | solution.py:34
  52.1 12.5 %collective-permute-start.4 = (bf16[128,1280]{1,0:T(8,128)(2,1)S(1)}, bf16[128,1280]{1,0:T(8,128)(2,1)S(1)}, u32[]{:S(2)}, u32[]{:S(2)}) collective-permute-start(bf16[128,1280]{1,0:T(8,128)(2,1)S(1)} %vision_feed_forward.4), channel_id=1, source_target_pairs={{0,16},{8,24},{16,0},{24,8},{1,17},{9,25},{17,1},{25,9},{2,18},{10... | collective-permute-start | bytes 983048 | tf_op jit(solution)/shard_map/ppermute | solution.py:34
  59.4 7.1 %collective-permute-start.6 = (bf16[128,1280]{1,0:T(8,128)(2,1)S(1)}, bf16[128,1280]{1,0:T(8,128)(2,1)S(1)}, u32[]{:S(2)}, u32[]{:S(2)}) collective-permute-start(bf16[128,1280]{1,0:T(8,128)(2,1)S(1)} %vision_feed_forward.5), channel_id=1, source_target_pairs={{0,16},{8,24},{16,0},{24,8},{1,17},{9,25},{17,1},{25,9},{2,18},{10... | collective-permute-start | bytes 983048 | tf_op jit(solution)/shard_map/ppermute | solution.py:34
  60.0 45.3 %collective-permute-start.12 = (bf16[320,1280]{1,0:T(8,128)(2,1)}, bf16[320,1280]{1,0:T(8,128)(2,1)}, u32[]{:S(2)}, u32[]{:S(2)}) collective-permute-start(bf16[320,1280]{1,0:T(8,128)(2,1)} %pad_maximum_fusion.1), channel_id=1, source_target_pairs={{0,2},{1,3},{2,0},{3,1},{4,6},{5,7},{6,4},{7,5},{8,10},{9,11},{10,... | collective-permute-start | bytes 2457608 | tf_op jit(solution)/shard_map/ppermute | solution.py:34
  61.7 44.1 %collective-permute-start.9 = (bf16[320,1280]{1,0:T(8,128)(2,1)}, bf16[320,1280]{1,0:T(8,128)(2,1)}, u32[]{:S(2)}, u32[]{:S(2)}) collective-permute-start(bf16[320,1280]{1,0:T(8,128)(2,1)} %collective-permute-done.7.refs_0_), channel_id=1, source_target_pairs={{0,8},{8,0},{16,24},{24,16},{1,9},{9,1},{17,25},{25,17},{2,10},{10... | collective-permute-start | bytes 2457608 | tf_op jit(solution)/shard_map/ppermute | solution.py:34
  62.0 43.8 %collective-permute-start.15 = (bf16[320,1280]{1,0:T(8,128)(2,1)}, bf16[320,1280]{1,0:T(8,128)(2,1)}, u32[]{:S(2)}, u32[]{:S(2)}) collective-permute-start(bf16[320,1280]{1,0:T(8,128)(2,1)} %collective-permute-done.11.refs_4_), channel_id=1, source_target_pairs={{0,1},{1,0},{2,3},{3,2},{4,5},{5,4},{6,7},{7,6},{8,9},{9,8},{10,11... | collective-permute-start | bytes 2457608 | tf_op jit(solution)/shard_map/ppermute | solution.py:34
  64.6 47.0 %collective-permute-start.16 = (bf16[320,1280]{1,0:T(8,128)(2,1)}, bf16[320,1280]{1,0:T(8,128)(2,1)}, u32[]{:S(2)}, u32[]{:S(2)}) collective-permute-start(bf16[320,1280]{1,0:T(8,128)(2,1)} %collective-permute-done.8.refs_1_), channel_id=1, source_target_pairs={{0,2},{1,3},{2,0},{3,1},{4,6},{5,7},{6,4},{7,5},{8,10},{9,11},{10,... | collective-permute-start | bytes 2457608 | tf_op jit(solution)/shard_map/ppermute | solution.py:34
  66.5 38.8 %collective-permute-start.19 = (bf16[128,1280]{1,0:T(8,128)(2,1)}, bf16[128,1280]{1,0:T(8,128)(2,1)}, u32[]{:S(2)}, u32[]{:S(2)}) collective-permute-start(bf16[128,1280]{1,0:T(8,128)(2,1)} %embed_ref.1), channel_id=1, source_target_pairs={{0,4},{1,5},{2,6},{3,7},{4,0},{5,1},{6,2},{7,3},{8,12},{9,13},{10,... | collective-permute-start | bytes 983048 | tf_op jit(solution)/shard_map/ppermute | solution.py:34
  82.3 32.0 %all-to-all-start = ((bf16[8,32,1280]{2,1,0:T(8,128)(2,1)}), bf16[8,32,1280]{2,1,0:T(8,128)(2,1)S(1)}, u32[]{:S(2)}, u32[]{:S(2)}) async-start(bf16[8,32,1280]{2,1,0:T(8,128)(2,1)} %bitcast.3), calls=%async_computation | async-start | bytes 1310720 | tf_op jit(solution)/shard_map/all_to_all | solution.py:315
  105.3 7.0 %collective-permute-start.10 = (bf16[320,1280]{1,0:T(8,128)(2,1)}, bf16[320,1280]{1,0:T(8,128)(2,1)S(1)}, u32[]{:S(2)}, u32[]{:S(2)}) collective-permute-start(bf16[320,1280]{1,0:T(8,128)(2,1)} %collective-permute-done.8.refs_1_), channel_id=1, source_target_pairs={{0,8},{8,0},{16,24},{24,16},{1,9},{9,1},{17,25},{25,17},{2,10},{10... | collective-permute-start | bytes 2457608 | tf_op jit(solution)/shard_map/ppermute | solution.py:34
  105.3 7.0 %collective-permute-start.13 = (bf16[320,1280]{1,0:T(8,128)(2,1)}, bf16[320,1280]{1,0:T(8,128)(2,1)S(1)}, u32[]{:S(2)}, u32[]{:S(2)}) collective-permute-start(bf16[320,1280]{1,0:T(8,128)(2,1)} %collective-permute-done.11.refs_4_), channel_id=1, source_target_pairs={{0,8},{8,0},{16,24},{24,16},{1,9},{9,1},{17,25},{25,17},{2,10},{10... | collective-permute-start | bytes 2457608 | tf_op jit(solution)/shard_map/ppermute | solution.py:34
  105.8 6.5 %collective-permute-start.14 = (bf16[320,1280]{1,0:T(8,128)(2,1)}, bf16[320,1280]{1,0:T(8,128)(2,1)S(1)}, u32[]{:S(2)}, u32[]{:S(2)}) collective-permute-start(bf16[320,1280]{1,0:T(8,128)(2,1)} %collective-permute-done.12.refs_5_), channel_id=1, source_target_pairs={{0,8},{8,0},{16,24},{24,16},{1,9},{9,1},{17,25},{25,17},{2,10},{10... | collective-permute-start | bytes 2457608 | tf_op jit(solution)/shard_map/ppermute | solution.py:34
  105.9 6.4 %collective-permute-start.17 = (bf16[320,1280]{1,0:T(8,128)(2,1)}, bf16[320,1280]{1,0:T(8,128)(2,1)}, u32[]{:S(2)}, u32[]{:S(2)}) collective-permute-start(bf16[320,1280]{1,0:T(8,128)(2,1)} %collective-permute-done.15.refs_8_), channel_id=1, source_target_pairs={{0,8},{8,0},{16,24},{24,16},{1,9},{9,1},{17,25},{25,17},{2,10},{10... | collective-permute-start | bytes 2457608 | tf_op jit(solution)/shard_map/ppermute | solution.py:34
  111.6 2.7 %collective-permute-start.18 = (bf16[320,1280]{1,0:T(8,128)(2,1)}, bf16[320,1280]{1,0:T(8,128)(2,1)}, u32[]{:S(2)}, u32[]{:S(2)}) collective-permute-start(bf16[320,1280]{1,0:T(8,128)(2,1)} %collective-permute-done.16.refs_9_), channel_id=1, source_target_pairs={{0,8},{8,0},{16,24},{24,16},{1,9},{9,1},{17,25},{25,17},{2,10},{10... | collective-permute-start | bytes 2457608 | tf_op jit(solution)/shard_map/ppermute | solution.py:34
  122.3 16.8 %collective-permute-start.20 = (bf16[128,1280]{1,0:T(8,128)(2,1)S(1)}, bf16[128,1280]{1,0:T(8,128)(2,1)}, u32[]{:S(2)}, u32[]{:S(2)}) collective-permute-start(bf16[128,1280]{1,0:T(8,128)(2,1)S(1)} %text_feed_forward.3), channel_id=1, source_target_pairs={{0,4},{1,5},{2,6},{3,7},{4,0},{5,1},{6,2},{7,3},{8,12},{9,13},{10,... | collective-permute-start | bytes 983048 | tf_op jit(solution)/shard_map/ppermute | solution.py:34
  (10 other events, 57.4 us)

commit v2 on v0

v2 whole, which is shorter than its diff:
```python
import functools

import jax
import jax.numpy as jnp
from jax import lax
from jax.experimental import pallas as pl
from jax.experimental.pallas import tpu as pltpu
from jax.sharding import PartitionSpec as P

F32 = jnp.float32
BF16 = jnp.bfloat16
VMEM = pl.BlockSpec(memory_space=pltpu.VMEM)
STORED = pl.BlockSpec(memory_space=pltpu.HBM)
SMEM = pl.BlockSpec(memory_space=pltpu.SMEM)
TOKEN = jax.ShapeDtypeStruct((8, 128), F32)


def like(x):
    return jax.ShapeDtypeStruct(x.shape, x.dtype)


def cost(microseconds):
    return pl.CostEstimate(flops=int(microseconds * 1e9), bytes_accessed=1000, transcendentals=0)


def call(kernel, name, out_shape, args, microseconds=0.001, aliases=None, scalars=0, stored=(), copies=0, scratch=(), megabytes=16):
    aliases = aliases or {}
    stored = (*stored, *aliases)
    specs = [SMEM] * scalars + [STORED if at in stored else VMEM for at in range(scalars, len(args))]
    single = not isinstance(out_shape, tuple)
    out_shape = (out_shape,) if single else out_shape
    outs = pl.pallas_call(
        kernel,
        out_shape=out_shape,
        in_specs=specs,
        out_specs=tuple(STORED if at in aliases.values() else VMEM for at in range(len(out_shape))),
        input_output_aliases=aliases,
        scratch_shapes=[*scratch, *([pltpu.SemaphoreType.DMA((copies,))] if copies else [])],
        compiler_params=pltpu.CompilerParams(vmem_limit_bytes=megabytes * 1024 * 1024),
        cost_estimate=cost(microseconds),
        name=name,
    )(*args)
    return outs[0] if single else outs


def normalize(values, row_gain):
    values = values.astype(F32)
    center = values - jnp.mean(values, axis=-1, keepdims=True)
    spread = jnp.mean(center * center, axis=-1, keepdims=True)
    return center * lax.rsqrt(spread + 1e-06) * row_gain


def gelu(v):
    half = 0.5 * v
    return half + half * jnp.tanh(v * (0.7978845608028654 + 0.035677408136300125 * (v * v)))


def up_project(rows_in, up_piece):
    return lax.dot_general(rows_in, up_piece, (((1,), (1,)), ((), ())), preferred_element_type=F32)


def swap(x, axis, bit):
    size = lax.axis_size(axis)
    return lax.ppermute(x, axis, [(i, i ^ bit) for i in range(size)])


def swap_by_core(x, bit_of_core):
    seq_size, blk_size = lax.axis_size("seq"), lax.axis_size("blk")
    pairs = [(s * blk_size + b, s * blk_size + (b ^ bit_of_core[s % 2])) for s in range(seq_size) for b in range(blk_size)]
    return lax.ppermute(x, ("seq", "blk"), pairs)


def plane_rows(patches):
    rows = patches.shape[0]
    count = rows // 8
    place = lax.broadcasted_iota(jnp.int32, (rows, rows), 0)
    source = lax.broadcasted_iota(jnp.int32, (rows, rows), 1)
    half, plane, window = place // (4 * count), place // count % 4, place % count
    order = (source == 4 * (count * half + window) + plane).astype(BF16)
    return jnp.dot(order, patches, preferred_element_type=F32)


def norm_patches_kernel(patches_ref, gain_ref, first_ref, second_ref, token_ref):
    rows = patches_ref.shape[0]
    normed = normalize(plane_rows(patches_ref[...]), gain_ref[...]).astype(BF16)
    first_ref[...] = normed[: rows // 2]
    second_ref[...] = normed[rows // 2 :]
    token_ref[...] = jnp.zeros_like(token_ref)


def start_copies(pairs, sems):
    copies = [pltpu.make_async_copy(source, goal, sems.at[at]) for at, (source, goal) in enumerate(pairs)]
    for copy in copies:
        copy.start()
    return copies


def same_kernel(*refs):
    pass


def after(x, before):
    return call(same_kernel, "after", like(x), (x, before), aliases={0: 0}, stored=(1,))


def feed_forward(rows, pieces):
    def pre(piece):
        up, bias, _ = piece
        product = up_project(rows, up())
        return product if bias is None else product + bias()

    total, ready = None, pre(pieces[0])
    for at, (_, _, down) in enumerate(pieces):
        later = pre(pieces[at + 1]) if at + 1 < len(pieces) else None
        part = jnp.dot(gelu(ready).astype(BF16), down(), preferred_element_type=F32)
        total = part if total is None else total + part
        ready = later
    return total


def vision_pieces(up, bias, down):
    pieces = []
    tile = up.shape[0] // 2
    for at in (0, tile):
        cut = pl.ds(at, tile)
        pieces.append(
            (
                functools.partial(lambda ref, cut: ref[cut, :], up, cut),
                functools.partial(lambda ref, cut: ref[cut], bias, cut),
                functools.partial(lambda ref, cut: ref[cut, :], down, cut),
            )
        )
    return pieces


def first_kernel(rows_ref, ua, ba, da, ub, bb, db, *refs):
    out_ref, token_ref, da_out, ub_out, db_out, sems = refs
    copies = start_copies([(da, da_out), (ub, ub_out), (db, db_out)], sems)
    rows = rows_ref[...]
    copies[0].wait()
    total = feed_forward(rows, vision_pieces(ua, ba, da_out))
    for copy in copies[1:]:
        copy.wait()
    total = total + feed_forward(rows, vision_pieces(ub_out, bb, db_out))
    out_ref[...] = total.astype(BF16)
    token_ref[...] = jnp.zeros_like(token_ref)


def pass_on(core_ref, ref, out_ref, sem):
    half = out_ref.shape[0]
    for core in range(2):

        @pl.when(core_ref[0] == core)
        def _():
            copy = pltpu.make_async_copy(ref.at[pl.ds(core * half, half)], out_ref, sem)
            copy.start()
            copy.wait()


def second_kernel(core_ref, rows_ref, ua, ba, da, ub, bb, db, before_ref, *refs):
    if len(refs) > 2:
        side_ref, _, half_ref, out_ref, token_ref, sems = refs
        pass_on(core_ref, side_ref, half_ref, sems.at[0])
    else:
        out_ref, token_ref = refs
    total = feed_forward(rows_ref[...], vision_pieces(ua, ba, da) + vision_pieces(ub, bb, db))
    out_ref[...] = total.astype(BF16)
    token_ref[...] = jnp.zeros_like(token_ref)


def own_kernel(first_ref, second_ref, ua, ba, da, ub, bb, db, before_ref, back_ref, proj, out_ref, proj_out, sems):
    copies = start_copies([(proj, proj_out)], sems)
    half = first_ref.shape[0]
    rows = jnp.concatenate([first_ref[...], second_ref[...]], axis=0)
    total = feed_forward(rows, vision_pieces(ua, ba, da) + vision_pieces(ub, bb, db))
    out_ref[pl.ds(0, half), :] = total[:half] + back_ref[...].astype(F32)
    out_ref[pl.ds(half, half), :] = total[half:]
    for copy in copies:
        copy.wait()


def merge_kernel(core_ref, patches_ref, own_ref, back_ref, gain_ref, proj_ref, place_ref, where_ref, *refs):
    if len(refs) > 1:
        side_ref, _, half_ref, out_ref, sems = refs
        pass_on(core_ref, side_ref, half_ref, sems.at[0])
    else:
        out_ref = refs[0]
    rows, width = patches_ref.shape
    count = rows // 8
    wide = plane_rows(patches_ref[...])
    merged = None
    for plane in range(4):
        halves = []
        for half in range(2):
            here = 4 * count * half + plane * count
            vis_out = wide[here : here + count] + own_ref[pl.ds(here, count), :]
            if half:
                vis_out = vis_out + back_ref[pl.ds(plane * count, count), :].astype(F32)
            halves.append(normalize(vis_out, gain_ref[...]).astype(BF16))
        proj = proj_ref[pl.ds(plane * width, width), :]
        part = jnp.dot(jnp.concatenate(halves, axis=0), proj, preferred_element_type=F32)
        merged = part if merged is None else merged + part
    placed = jnp.dot(place_ref[...], merged.astype(BF16), preferred_element_type=F32)
    out_ref[:, :width] = placed.astype(BF16)
    out_ref[:, width:] = where_ref[...]


def place_text_rows(which, capacity, embed_ref, got_ref):
    width = embed_ref.shape[1]
    where = got_ref[:, width:].astype(F32)
    token = lax.broadcasted_iota(jnp.int32, where.shape, 1).astype(F32)
    side_of = lax.broadcasted_iota(jnp.int32, where.shape, 0) // capacity % 2
    pick = ((where == token) & (side_of == which)).astype(F32).astype(BF16)
    by_token = (((0,), (0,)), ((), ()))
    picked = lax.dot_general(pick, got_ref[:, :width], by_token, preferred_element_type=F32)
    taken = lax.dot_general(pick, jnp.ones((pick.shape[0], 128), BF16), by_token, preferred_element_type=F32)
    return jnp.where(taken[:, :1] > 0.5, picked, embed_ref[...].astype(F32))


def joined_kernel(up_ref, down_ref, before_ref, embed_ref, out_ref):
    half = up_ref.shape[0]
    out_ref[pl.ds(0, half), :] = up_ref[...]
    out_ref[pl.ds(half, half), :] = down_ref[...]


def text_pieces(slices):
    return [
        (functools.partial(lambda ref: ref[...], up), None, functools.partial(lambda ref: ref[...], down))
        for up, down in slices
    ]


def across_pieces(halves):
    half = halves[0].shape[0] // 2
    up, down = pl.ds(0, half), pl.ds(half, half)
    return [
        (
            functools.partial(lambda ref: ref[up, :], ref),
            None,
            functools.partial(lambda ref: ref[down, :], ref),
        )
        for ref in halves
    ]


def loaded_pieces(refs, up, down, sems):
    copies = start_copies(
        [(ref, (up, down)[at % 2].at[at // 2]) for at, ref in enumerate(refs)], sems
    )

    def read(at):
        copies[at].wait()
        return (up, down)[at % 2][at // 2]

    return [
        (functools.partial(read, at), None, functools.partial(read, at + 1)) for at in range(0, len(refs), 2)
    ]


def theirs_kernel(capacity, embed_ref, got_ref, gain_ref, *refs):
    slices, (normed_ref, total_ref), scratch = refs[:6], refs[6:8], refs[8:]
    pieces = loaded_pieces(slices, *scratch)
    text_rows = place_text_rows(1, capacity, embed_ref, got_ref)
    normed = normalize(text_rows, gain_ref[...]).astype(BF16)
    normed_ref[...] = normed
    total_ref[...] = feed_forward(normed, pieces)


def theirs_last_kernel(normed_ref, total_ref, *refs):
    pieces = across_pieces(refs[:-1])
    refs[-1][...] = (total_ref[...] + feed_forward(normed_ref[...], pieces)).astype(BF16)


def mine_kernel(capacity, embed_ref, got_ref, gain_ref, *refs):
    slices, halves, out_ref, scratch = refs[:6], refs[6:8], refs[8], refs[9:]
    pieces = loaded_pieces(slices, *scratch)
    text_rows = place_text_rows(0, capacity, embed_ref, got_ref)
    normed = normalize(text_rows, gain_ref[...]).astype(BF16)
    out_ref[...] = text_rows + feed_forward(normed, across_pieces(halves) + pieces)


def per_device(
    patches,
    vis_gain,
    vis_up,
    vis_bias,
    vis_down,
    merge_gain,
    merge_proj,
    text_embed,
    slot_index,
    text_gain,
    text_up,
    text_down,
):
    cycle_size = lax.axis_size("blk")
    merged_count = slot_index.shape[0]
    token_count, width = text_embed.shape
    patch_count = patches.shape[0]
    capacity = 2 * merged_count // cycle_size
    paired = cycle_size == 8
    sides = 2 if paired else 1

    target = slot_index // token_count % cycle_size
    position = slot_index % token_count
    one_hot = (target[:, None] == jnp.arange(cycle_size, dtype=jnp.int32)[None, :]).astype(jnp.int32)
    rank = jnp.sum((jnp.cumsum(one_hot, axis=0) - one_hot) * one_hot, axis=1)
    sent = jnp.arange(cycle_size * sides * capacity, dtype=jnp.int32)[:, None]
    owner = sent // (sides * capacity) ^ (4 * (sent // capacity % sides))
    chosen = (target[None, :] == owner) & (rank[None, :] == sent % capacity)
    place = chosen.astype(BF16)
    where = jnp.max(jnp.where(chosen, position[None, :], -1), axis=1, keepdims=True)
    where = jnp.broadcast_to(where.astype(BF16), (where.shape[0], 128))

    core = (lax.axis_index("seq") % 2).reshape(1)
    half_rows = jax.ShapeDtypeStruct((patch_count // 2, width), BF16)
    far_up, far_down = swap(vis_up, "seq", 1), swap(vis_down, "seq", 1)
    other_bias = swap(after(vis_bias, far_up), "seq", 1)
    first, second, _ = call(
        norm_patches_kernel, "norm_patches", (half_rows, half_rows, TOKEN), (patches, vis_gain)
    )
    far_first, far_second = swap(first, "seq", 2), swap(second, "seq", 2)
    args = (far_first, vis_up, vis_bias, vis_down, far_up, other_bias, far_down)
    outs = (half_rows, TOKEN, like(vis_down), like(vis_up), like(vis_down))
    if paired:
        side_up, side_down = swap_by_core(text_up, (1, 2)), swap_by_core(text_down, (1, 2))
    part_first, first_done, near_down, far_up, far_down = call(
        first_kernel, "vision_first", outs, args, stored=(3, 4, 6), copies=3
    )
    weights = (vis_up, vis_bias, near_down, far_up, other_bias, far_down)
    back_first = swap(part_first, "seq", 2)
    if paired:
        other_embed = swap(text_embed, "blk", 4)
    args = (core, far_second, *weights, first_done)
    outs = (half_rows, TOKEN)
    half_slice = jax.ShapeDtypeStruct((text_up.shape[0] // 2, width), BF16)
    if paired:
        side_up, across_up, part_second, second_done = call(
            second_kernel,
            "vision_second",
            (like(side_up), half_slice, *outs),
            args + (side_up,),
            aliases={len(args): 0},
            copies=1,
            scalars=1,
            microseconds=30,
        )
        other_up, across_up = swap(side_up, "seq", 1), swap_by_core(across_up, (2, 1))
    else:
        part_second, second_done = call(second_kernel, "vision_second", outs, args, scalars=1, microseconds=30)
    back_second = swap(part_second, "seq", 2)
    own_rows = jax.ShapeDtypeStruct((patch_count, width), F32)
    own, merge_proj = call(
        own_kernel,
        "vision_own",
        (own_rows, like(merge_proj)),
        (first, second, *weights, second_done, back_first, merge_proj),
        stored=(10,),
        copies=1,
    )
    args = (core, patches, own, back_second, merge_gain, merge_proj, place, where)
    sent_rows = jax.ShapeDtypeStruct((place.shape[0], width + 128), BF16)
    if paired:
        side_down, across_down, send = call(
            merge_kernel,
            "merge_rows",
            (like(side_down), half_slice, sent_rows),
            args + (side_down,),
            aliases={len(args): 0},
            copies=1,
            scalars=1,
        )
        other_down, across_down = swap(side_down, "seq", 1), swap_by_core(across_down, (2, 1))
    else:
        send = call(merge_kernel, "merge_rows", sent_rows, args, scalars=1)
    got = lax.all_to_all(send, "blk", split_axis=0, concat_axis=0, tiled=True)
    if paired:
        across = call(joined_kernel, "join_across", like(text_up), (across_up, across_down, send, other_embed), stored=(2,), microseconds=20)
        halves = (across, swap(across, "seq", 1))
        other_up, other_down = call(
            same_kernel,
            "hold",
            (like(other_up), like(other_down)),
            (other_up, other_down),
            aliases={0: 0, 1: 1},
            stored=(0, 1),
            microseconds=20,
        )
        slices = (text_up, text_down, side_up, side_down, other_up, other_down)
        room = tuple(pltpu.VMEM((3, *text_up.shape), BF16) for _ in range(2))
        tokens = jax.ShapeDtypeStruct((token_count, width), F32)
        text_normed, total = call(
            functools.partial(theirs_kernel, capacity),
            "text_theirs",
            (like(text_embed), tokens),
            (other_embed, got, text_gain, *slices),
            stored=tuple(range(3, 9)),
            copies=6,
            scratch=room,
            megabytes=20,
        )
        theirs = call(theirs_last_kernel, "text_theirs_last", like(text_embed), (text_normed, total, *halves))
        mine = call(
            functools.partial(mine_kernel, capacity),
            "text_mine",
            tokens,
            (text_embed, got, text_gain, *slices, *halves),
            stored=tuple(range(3, 9)),
            copies=6,
            scratch=room,
            megabytes=20,
        )
        return (mine + swap(theirs, "blk", 4).astype(F32)).astype(BF16)
    tokens = jnp.arange(token_count, dtype=jnp.int32).astype(BF16)
    pick = (got[:, width:][:, :1] == tokens[None, :]).astype(BF16)
    picked = lax.dot_general(pick, got[:, :width], (((0,), (0,)), ((), ())), preferred_element_type=F32)
    taken = jnp.sum(pick.astype(F32), axis=0)[:, None] > 0.5
    text_rows = jnp.where(taken, picked, text_embed.astype(F32))
    text_normed = normalize(text_rows, text_gain).astype(BF16)
    gathered_tokens = lax.all_gather(text_normed, "blk", axis=0, tiled=True)
    hidden = gelu(up_project(gathered_tokens, text_up)).astype(BF16)
    text_mlp = lax.psum_scatter(
        jnp.dot(hidden, text_down, preferred_element_type=F32).astype(BF16),
        "blk",
        scatter_dimension=0,
        tiled=True,
    ).astype(F32)
    return (text_rows + text_mlp).astype(BF16)


def solution(mesh):
    placed = (
        P(("seq", "blk"), None),
        P(),
        P("seq", None),
        P("seq"),
        P("seq", None),
        P(),
        P(),
        P(("seq", "blk"), None),
        P(("seq", "blk")),
        P(),
        P("blk", None),
        P("blk", None),
    )
    return jax.shard_map(
        per_device, mesh=mesh, in_specs=placed, out_specs=P(("seq", "blk"), None), check_vma=False
    )
```

time: 267 us -> 111 us (0.42)
  the two profiles are of different devices: /device:TPU:0 before, /device:TPU:6 now
where the time goes in v2:
time: 111 us; the launch traced here: 110 us
  Pallas kernels  43.5 us (39%)
  waiting for transfers between devices  31.4 us (28%)
  starting transfers between devices  19.2 us (17%)
  local copies, waits for them, and re-layouts  13.3 us (12%)
  other arithmetic  2.17 us (2%)
    pallas_call x11, Pallas kernels, call(): pl.pallas_call(kernel, out_shape=out_shape, in_specs=specs, out_specs=tup...  43.5 us
    ppermute x12, waiting for transfers between devices, swap(): return lax.ppermute(x, axis, [(i, i ^ bit) for i in range(size)])  26.1 us
    unnamed x37, local copies, waits for them, and re-layouts  13.2 us
    ppermute x12, starting transfers between devices, swap(): return lax.ppermute(x, axis, [(i, i ^ bit) for i in range(size)])  9.75 us
    ppermute x4, starting transfers between devices, swap_by_core(): return lax.ppermute(x, ('seq', 'blk'), pairs)  5.27 us
    all_to_all x1, starting transfers between devices, per_device(): got = lax.all_to_all(send, 'blk', split_axis=0, concat_axis=0, tiled=True)  4.15 us
    all_to_all x1, waiting for transfers between devices, per_device(): got = lax.all_to_all(send, 'blk', split_axis=0, concat_axis=0, tiled=True)  3.91 us
  transfers between devices with their start and end apart: 17, of which 6 were waited for; matrix products, arithmetic and copies ran while one was open for 2% of the time, Pallas kernels for 37%

profile of v2, /device:TPU:6, one launch (start us, length us, event | category | flops | bytes accessed | tf_op | source)
XLA Modules:
  0.0 109.8 jit_solution(6632731737229795630)
XLA Ops:
  4.3 2.0 %collective-permute-start.4 = (bf16[128,1280]{1,0:T(8,128)(2,1)}, bf16[128,1280]{1,0:T(8,128)(2,1)}, u32[]{:S(2)}, u32[]{:S(2)}) collective-permute-start(bf16[128,1280]{1,0:T(8,128)(2,1)} %get-tuple-element.26.second_ref), channel_id=1, source_target_pairs={{0,16},{8,24},{16,0},{24,8},{1,17},{9,25},{17,1},{25,9},{2,18},{10... | collective-permute-start | bytes 983048 | tf_op jit(solution)/shard_map/ppermute | solution.py:64
  8.0 2.7 %collective-permute-done.1.refs_1_.ub = bf16[1280,1280]{1,0:T(8,128)(2,1)S(1)} collective-permute-done((bf16[1280,1280]{1,0:T(8,128)(2,1)}, bf16[1280,1280]{1,0:T(8,128)(2,1)S(1)}, u32[]{:S(2)}, u32[]{:S(2)}) %collective-permute-start.1) | collective-permute-done | bytes 3276832 | tf_op jit(solution)/shard_map/ppermute | solution.py:64
  10.7 1.8 %copy-done.2 = bf16[1280,1280]{1,0:T(8,128)(2,1)} copy-done((bf16[1280,1280]{1,0:T(8,128)(2,1)}, bf16[1280,1280]{1,0:T(8,128)(2,1)S(1)}, u32[]{:S(2)}) %copy-start.2) | copy-done | bytes 3276824
  12.6 2.5 %collective-permute-done.rows_ref = bf16[128,1280]{1,0:T(8,128)(2,1)} collective-permute-done((bf16[128,1280]{1,0:T(8,128)(2,1)}, bf16[128,1280]{1,0:T(8,128)(2,1)}, u32[]{:S(2)}, u32[]{:S(2)}) %collective-permute-start) | collective-permute-done | bytes 327712 | tf_op jit(solution)/shard_map/ppermute | solution.py:64
  16.7 1.9 %copy-done = bf16[1280,1280]{1,0:T(8,128)(2,1)S(1)} copy-done((bf16[1280,1280]{1,0:T(8,128)(2,1)S(1)}, bf16[1280,1280]{1,0:T(8,128)(2,1)}, u32[]{:S(2)}) %copy-start) | copy-done | bytes 3276824
  18.7 1.9 %copy-done.3 = bf16[1280,1280]{1,0:T(8,128)(2,1)S(1)} copy-done((bf16[1280,1280]{1,0:T(8,128)(2,1)S(1)}, bf16[1280,1280]{1,0:T(8,128)(2,1)}, u32[]{:S(2)}) %copy-start.3) | copy-done | bytes 3276824
  20.6 1.9 %copy-done.7 = bf16[1280,1280]{1,0:T(8,128)(2,1)S(1)} copy-done((bf16[1280,1280]{1,0:T(8,128)(2,1)S(1)}, bf16[1280,1280]{1,0:T(8,128)(2,1)}, u32[]{:S(2)}) %copy-start.7) | copy-done | bytes 3276824
  22.5 5.8 %vision_first.1 = (bf16[128,1280]{1,0:T(8,128)(2,1)S(1)}, f32[8,128]{1,0:T(8,128)S(1)}, bf16[1280,1280]{1,0:T(8,128)(2,1)S(1)}, bf16[1280,1280]{1,0:T(8,128)(2,1)S(1)}, bf16[1280,1280]{1,0:T(8,128)(2,1)S(1)}) custom-call(bf16[128,1280]{1,0:T(8,128)(2,1)} %collective-permute-done.rows_ref, bf16[1280,1280]{1,0:T(8,128)(2,1)S(1)} %copy-done, ...), custom_call_target="tpu_custom_call" | custom-call | flops 1000000 | bytes 1000 | tf_op jit(solution)/shard_map/vision_first/pallas_call | solution.py:32
  28.9 5.2 %vision_second.1 = (bf16[640,1280]{1,0:T(8,128)(2,1)}, bf16[320,1280]{1,0:T(8,128)(2,1)S(1)}, bf16[128,1280]{1,0:T(8,128)(2,1)S(1)}, f32[8,128]{1,0:T(8,128)S(1)}) custom-call(s32[1]{0:T(128)} %bitcast.core_ref, bf16[128,1280]{1,0:T(8,128)(2,1)} %collective-permute-done.4.rows_ref, ...), custom_call_target="tpu_custom_call", output_to_operand_aliasing={{0}: (9, {})} | custom-call | flops 30000001024 | bytes 1000 | tf_op jit(solution)/shard_map/vision_second/pallas_call | solution.py:32
  34.1 1.6 %collective-permute-start.7 = (bf16[128,1280]{1,0:T(8,128)(2,1)S(1)}, bf16[128,1280]{1,0:T(8,128)(2,1)S(1)}, u32[]{:S(2)}, u32[]{:S(2)}) collective-permute-start(bf16[128,1280]{1,0:T(8,128)(2,1)S(1)} %get-tuple-element.34), channel_id=1, source_target_pairs={{0,16},{8,24},{16,0},{24,8},{1,17},{9,25},{17,1},{25,9},{2,18},{10... | collective-permute-start | bytes 983048 | tf_op jit(solution)/shard_map/ppermute | solution.py:64
  36.0 1.7 %collective-permute-start.11 = (bf16[320,1280]{1,0:T(8,128)(2,1)S(1)}, bf16[320,1280]{1,0:T(8,128)(2,1)}, u32[]{:S(2)}, u32[]{:S(2)}) collective-permute-start(bf16[320,1280]{1,0:T(8,128)(2,1)S(1)} %get-tuple-element.41), channel_id=1, source_target_pairs={{0,2},{1,3},{2,0},{3,1},{4,6},{5,7},{6,4},{7,5},{8,9},{9,8},{10,11... | collective-permute-start | bytes 2457608 | tf_op jit(solution)/shard_map/ppermute | solution.py:70
  37.7 5.9 %vision_own.1 = (f32[256,1280]{1,0:T(8,128)S(1)}, bf16[5120,1280]{1,0:T(8,128)(2,1)S(1)}) custom-call(bf16[128,1280]{1,0:T(8,128)(2,1)} %get-tuple-element.25.first_ref, bf16[128,1280]{1,0:T(8,128)(2,1)} %get-tuple-element.26.second_ref, bf16[1280,1280]{1,0:T(8,128)(2,1)S(1)} %copy-done.1, f32[1280]{0:T(1024)S(1)} %copy-done.14, ...), custom_call_target="tpu_custom_call" | custom-call | flops 1000000 | bytes 1000 | tf_op jit(solution)/shard_map/vision_own/pallas_call | solution.py:32
  43.8 4.8 %merge_rows.1 = (bf16[640,1280]{1,0:T(8,128)(2,1)S(1)}, bf16[320,1280]{1,0:T(8,128)(2,1)}, bf16[256,1408]{1,0:T(8,128)(2,1)}) custom-call(s32[1]{0:T(128)} %bitcast.core_ref, bf16[256,1280]{1,0:T(8,128)(2,1)S(1)} %copy-done.9, f32[256,1280]{1,0:T(8,128)S(1)} %get-tuple-element.33.own_ref, ...), custom_call_target="tpu_custom_call", output_to_operand_aliasing={{0}: (8, {})} | custom-call | flops 1000000 | bytes 1000 | tf_op jit(solution)/shard_map/merge_rows/pallas_call | solution.py:32
  48.5 1.5 %collective-permute-start.12 = (bf16[320,1280]{1,0:T(8,128)(2,1)}, bf16[320,1280]{1,0:T(8,128)(2,1)}, u32[]{:S(2)}, u32[]{:S(2)}) collective-permute-start(bf16[320,1280]{1,0:T(8,128)(2,1)} %get-tuple-element.42), channel_id=1, source_target_pairs={{0,2},{1,3},{2,0},{3,1},{4,6},{5,7},{6,4},{7,5},{8,9},{9,8},{10,11... | collective-permute-start | bytes 2457608 | tf_op jit(solution)/shard_map/ppermute | solution.py:70
  50.1 2.8 %collective-permute-start.13 = (bf16[128,1280]{1,0:T(8,128)(2,1)S(1)}, bf16[128,1280]{1,0:T(8,128)(2,1)S(1)}, u32[]{:S(2)}, u32[]{:S(2)}) collective-permute-start(bf16[128,1280]{1,0:T(8,128)(2,1)S(1)} %copy-done.12), channel_id=1, source_target_pairs={{0,4},{1,5},{2,6},{3,7},{4,0},{5,1},{6,2},{7,3},{8,12},{9,13},{10,... | collective-permute-start | bytes 983048 | tf_op jit(solution)/shard_map/ppermute | solution.py:64
  53.4 4.2 %all-to-all-start = ((bf16[8,32,1408]{2,1,0:T(8,128)(2,1)}), bf16[8,32,1408]{2,1,0:T(8,128)(2,1)}, u32[]{:S(2)}, u32[]{:S(2)}) async-start(bf16[8,32,1408]{2,1,0:T(8,128)(2,1)} %bitcast.1), calls=%async_computation | async-start | bytes 1441792 | tf_op jit(solution)/shard_map/all_to_all | solution.py:376
  57.5 13.7 %collective-permute-done.13.embed_ref = bf16[128,1280]{1,0:T(8,128)(2,1)S(1)} collective-permute-done((bf16[128,1280]{1,0:T(8,128)(2,1)S(1)}, bf16[128,1280]{1,0:T(8,128)(2,1)S(1)}, u32[]{:S(2)}, u32[]{:S(2)}) %collective-permute-start.13) | collective-permute-done | bytes 327712 | tf_op jit(solution)/shard_map/ppermute | solution.py:64
  72.7 2.7 %join_across.1.refs_6_.refs_0_ = bf16[640,1280]{1,0:T(8,128)(2,1)} custom-call(bf16[320,1280]{1,0:T(8,128)(2,1)} %collective-permute-done.11.up_ref, bf16[320,1280]{1,0:T(8,128)(2,1)} %collective-permute-done.12.down_ref, bf16[256,1408]{1,0:T(8,128)(2,1)} %get-tuple-element.36.before_ref, bf16[128,1280]{1,0:T(8,128)(2,1)S(1)} %collective-permute-done.13.embed_ref), custom_call_target="tpu_custom_call" | custom-call | flops 20000000000 | bytes 1000 | tf_op jit(solution)/shard_map/join_across/pallas_call | solution.py:32
  76.2 3.9 %all-to-all-done = bf16[8,32,1408]{2,1,0:T(8,128)(2,1)} async-done(((bf16[8,32,1408]{2,1,0:T(8,128)(2,1)}), bf16[8,32,1408]{2,1,0:T(8,128)(2,1)}, u32[]{:S(2)}, u32[]{:S(2)}) %all-to-all-start) | async-done | bytes 720928 | tf_op jit(solution)/shard_map/all_to_all | solution.py:376
  82.5 6.0 %text_theirs.1 = (bf16[128,1280]{1,0:T(8,128)(2,1)S(1)}, f32[128,1280]{1,0:T(8,128)S(1)}) custom-call(bf16[128,1280]{1,0:T(8,128)(2,1)S(1)} %copy-done.11, bf16[256,1408]{1,0:T(8,128)(2,1)} %bitcast.2.got_ref, f32[1280]{0:T(1024)S(1)} %copy-done.15, bf16[640,1280]{1,0:T(8,128)(2,1)S(1)} %copy-done.4, bf16[640,1280]{1,0:T(8,128)(2,1)S(1)} %copy-done.5, ...), custom_call_target="tpu_custom_call" | custom-call | flops 1000000 | bytes 1000 | tf_op jit(solution)/shard_map/text_theirs/pallas_call | solution.py:32
  88.5 3.3 %text_theirs_last.1 = bf16[128,1280]{1,0:T(8,128)(2,1)S(1)} custom-call(bf16[128,1280]{1,0:T(8,128)(2,1)S(1)} %get-tuple-element.43.normed_ref, f32[128,1280]{1,0:T(8,128)S(1)} %get-tuple-element.44.total_ref, bf16[640,1280]{1,0:T(8,128)(2,1)} %join_across.1.refs_6_.refs_0_, bf16[640,1280]{1,0:T(8,128)(2,1)} %collective-permute-done.14.refs_7_.refs_1_), custom_call_target="tpu_custom_call" | custom-call | flops 1000000 | bytes 1000 | tf_op jit(solution)/shard_map/text_theirs_last/pallas_call | solution.py:32
  91.8 1.6 %collective-permute-start.15 = (bf16[128,1280]{1,0:T(8,128)(2,1)S(1)}, bf16[128,1280]{1,0:T(8,128)(2,1)S(1)}, u32[]{:S(2)}, u32[]{:S(2)}) collective-permute-start(bf16[128,1280]{1,0:T(8,128)(2,1)S(1)} %text_theirs_last.1), channel_id=1, source_target_pairs={{0,4},{1,5},{2,6},{3,7},{4,0},{5,1},{6,2},{7,3},{8,12},{9,13},{10,... | collective-permute-start | bytes 983048 | tf_op jit(solution)/shard_map/ppermute | solution.py:64
  93.5 8.4 %text_mine.1 = f32[128,1280]{1,0:T(8,128)S(1)} custom-call(bf16[128,1280]{1,0:T(8,128)(2,1)S(1)} %copy-done.13, bf16[256,1408]{1,0:T(8,128)(2,1)} %bitcast.2.got_ref, f32[1280]{0:T(1024)S(1)} %copy-done.15, bf16[640,1280]{1,0:T(8,128)(2,1)S(1)} %copy-done.4, bf16[640,1280]{1,0:T(8,128)(2,1)S(1)} %copy-done.6, bf16[640,1280]{1,0:T(8,128)(2,1)} %get-tuple-element.37.refs_2_, ...), custom_call_target="tpu_custom_call" | custom-call | flops 1000000 | bytes 1000 | tf_op jit(solution)/shard_map/text_mine/pallas_call | solution.py:32
  101.8 7.1 %collective-permute-done.15 = bf16[128,1280]{1,0:T(8,128)(2,1)S(1)} collective-permute-done((bf16[128,1280]{1,0:T(8,128)(2,1)S(1)}, bf16[128,1280]{1,0:T(8,128)(2,1)S(1)}, u32[]{:S(2)}, u32[]{:S(2)}) %collective-permute-start.15) | collective-permute-done | bytes 327712 | tf_op jit(solution)/shard_map/ppermute | solution.py:64
  (68 shorter events, 14.7 us)
Async XLA Ops:
  0.0 10.7 %collective-permute-start.1 = (bf16[1280,1280]{1,0:T(8,128)(2,1)}, bf16[1280,1280]{1,0:T(8,128)(2,1)S(1)}, u32[]{:S(2)}, u32[]{:S(2)}) collective-permute-start(bf16[1280,1280]{1,0:T(8,128)(2,1)} %ua.5), channel_id=1, source_target_pairs={{0,8},{8,0},{16,24},{24,16},{1,9},{9,1},{17,25},{25,17},{2,10},{10... | collective-permute-start | bytes 9830408 | tf_op jit(solution)/shard_map/ppermute | solution.py:64
  0.0 16.7 %collective-permute-start.3 = (bf16[1280,1280]{1,0:T(8,128)(2,1)}, bf16[1280,1280]{1,0:T(8,128)(2,1)}, u32[]{:S(2)}, u32[]{:S(2)}) collective-permute-start(bf16[1280,1280]{1,0:T(8,128)(2,1)} %da.1), channel_id=1, source_target_pairs={{0,8},{8,0},{16,24},{24,16},{1,9},{9,1},{17,25},{25,17},{2,10},{10... | collective-permute-start | bytes 9830408 | tf_op jit(solution)/shard_map/ppermute | solution.py:64
  0.5 28.4 %collective-permute-start.5 = (bf16[640,1280]{1,0:T(8,128)(2,1)}, bf16[640,1280]{1,0:T(8,128)(2,1)}, u32[]{:S(2)}, u32[]{:S(2)}) collective-permute-start(bf16[640,1280]{1,0:T(8,128)(2,1)} %refs_0_.4), channel_id=1, source_target_pairs={{0,1},{1,0},{2,3},{3,2},{4,5},{5,4},{6,7},{7,6},{8,10},{9,11},{10,... | collective-permute-start | bytes 4915208 | tf_op jit(solution)/shard_map/ppermute | solution.py:70
  4.3 10.9 %collective-permute-start = (bf16[128,1280]{1,0:T(8,128)(2,1)}, bf16[128,1280]{1,0:T(8,128)(2,1)}, u32[]{:S(2)}, u32[]{:S(2)}) collective-permute-start(bf16[128,1280]{1,0:T(8,128)(2,1)} %get-tuple-element.25.first_ref), channel_id=1, source_target_pairs={{0,16},{8,24},{16,0},{24,8},{1,17},{9,25},{17,1},{25,9},{2,18},{10... | collective-permute-start | bytes 983048 | tf_op jit(solution)/shard_map/ppermute | solution.py:64
  4.3 24.6 %collective-permute-start.4 = (bf16[128,1280]{1,0:T(8,128)(2,1)}, bf16[128,1280]{1,0:T(8,128)(2,1)}, u32[]{:S(2)}, u32[]{:S(2)}) collective-permute-start(bf16[128,1280]{1,0:T(8,128)(2,1)} %get-tuple-element.26.second_ref), channel_id=1, source_target_pairs={{0,16},{8,24},{16,0},{24,8},{1,17},{9,25},{17,1},{25,9},{2,18},{10... | collective-permute-start | bytes 983048 | tf_op jit(solution)/shard_map/ppermute | solution.py:64
  8.0 8.7 %copy-start.14 = (f32[1280]{0:T(1024)S(1)}, f32[1280]{0:T(1024)}, u32[]{:S(2)}) copy-start(f32[1280]{0:T(1024)} %ba.5) | copy-start | bytes 15364
  12.5 4.2 %collective-permute-start.2 = (f32[1280]{0:T(1024)S(1)}, f32[1280]{0:T(1024)S(1)}, u32[]{:S(2)}, u32[]{:S(2)}) collective-permute-start(f32[1280]{0:T(1024)S(1)} %after.1), channel_id=1, source_target_pairs={{0,8},{8,0},{16,24},{24,16},{1,9},{9,1},{17,25},{25,17},{2,10},{10... | collective-permute-start | bytes 15368 | tf_op jit(solution)/shard_map/ppermute | solution.py:64
  15.2 28.4 %collective-permute-start.8 = (bf16[640,1280]{1,0:T(8,128)(2,1)}, bf16[640,1280]{1,0:T(8,128)(2,1)S(1)}, u32[]{:S(2)}, u32[]{:S(2)}) collective-permute-start(bf16[640,1280]{1,0:T(8,128)(2,1)} %refs_1_.3), channel_id=1, source_target_pairs={{0,1},{1,0},{2,3},{3,2},{4,5},{5,4},{6,7},{7,6},{8,10},{9,11},{10,... | collective-permute-start | bytes 4915208 | tf_op jit(solution)/shard_map/ppermute | solution.py:70
  22.5 6.4 %copy-start.1 = (bf16[1280,1280]{1,0:T(8,128)(2,1)S(1)}, bf16[1280,1280]{1,0:T(8,128)(2,1)}, u32[]{:S(2)}) copy-start(bf16[1280,1280]{1,0:T(8,128)(2,1)} %ua.5) | copy-start | bytes 9830404
  28.3 9.4 %collective-permute-start.6 = (bf16[128,1280]{1,0:T(8,128)(2,1)S(1)}, bf16[128,1280]{1,0:T(8,128)(2,1)S(1)}, u32[]{:S(2)}, u32[]{:S(2)}) collective-permute-start(bf16[128,1280]{1,0:T(8,128)(2,1)S(1)} %get-tuple-element.32), channel_id=1, source_target_pairs={{0,16},{8,24},{16,0},{24,8},{1,17},{9,25},{17,1},{25,9},{2,18},{10... | collective-permute-start | bytes 983048 | tf_op jit(solution)/shard_map/ppermute | solution.py:64
  34.1 9.5 %collective-permute-start.7 = (bf16[128,1280]{1,0:T(8,128)(2,1)S(1)}, bf16[128,1280]{1,0:T(8,128)(2,1)S(1)}, u32[]{:S(2)}, u32[]{:S(2)}) collective-permute-start(bf16[128,1280]{1,0:T(8,128)(2,1)S(1)} %get-tuple-element.34), channel_id=1, source_target_pairs={{0,16},{8,24},{16,0},{24,8},{1,17},{9,25},{17,1},{25,9},{2,18},{10... | collective-permute-start | bytes 983048 | tf_op jit(solution)/shard_map/ppermute | solution.py:64
  36.0 35.2 %collective-permute-start.11 = (bf16[320,1280]{1,0:T(8,128)(2,1)S(1)}, bf16[320,1280]{1,0:T(8,128)(2,1)}, u32[]{:S(2)}, u32[]{:S(2)}) collective-permute-start(bf16[320,1280]{1,0:T(8,128)(2,1)S(1)} %get-tuple-element.41), channel_id=1, source_target_pairs={{0,2},{1,3},{2,0},{3,1},{4,6},{5,7},{6,4},{7,5},{8,9},{9,8},{10,11... | collective-permute-start | bytes 2457608 | tf_op jit(solution)/shard_map/ppermute | solution.py:70
  37.7 6.0 %copy-start.9 = (bf16[256,1280]{1,0:T(8,128)(2,1)S(1)}, bf16[256,1280]{1,0:T(8,128)(2,1)}, u32[]{:S(2)}) copy-start(bf16[256,1280]{1,0:T(8,128)(2,1)} %patches_ref.3) | copy-start | bytes 1966084
  37.7 6.0 %copy-start.16 = (f32[1280]{0:T(1024)S(1)}, f32[1280]{0:T(1024)}, u32[]{:S(2)}) copy-start(f32[1280]{0:T(1024)} %gain_ref.5) | copy-start | bytes 15364
  43.8 6.3 %copy-start.12 = (bf16[128,1280]{1,0:T(8,128)(2,1)S(1)}, bf16[128,1280]{1,0:T(8,128)(2,1)}, u32[]{:S(2)}) copy-start(bf16[128,1280]{1,0:T(8,128)(2,1)} %embed_ref.1) | copy-start | bytes 983044
  48.5 24.1 %collective-permute-start.12 = (bf16[320,1280]{1,0:T(8,128)(2,1)}, bf16[320,1280]{1,0:T(8,128)(2,1)}, u32[]{:S(2)}, u32[]{:S(2)}) collective-permute-start(bf16[320,1280]{1,0:T(8,128)(2,1)} %get-tuple-element.42), channel_id=1, source_target_pairs={{0,2},{1,3},{2,0},{3,1},{4,6},{5,7},{6,4},{7,5},{8,9},{9,8},{10,11... | collective-permute-start | bytes 2457608 | tf_op jit(solution)/shard_map/ppermute | solution.py:70
  50.1 21.1 %collective-permute-start.13 = (bf16[128,1280]{1,0:T(8,128)(2,1)S(1)}, bf16[128,1280]{1,0:T(8,128)(2,1)S(1)}, u32[]{:S(2)}, u32[]{:S(2)}) collective-permute-start(bf16[128,1280]{1,0:T(8,128)(2,1)S(1)} %copy-done.12), channel_id=1, source_target_pairs={{0,4},{1,5},{2,6},{3,7},{4,0},{5,1},{6,2},{7,3},{8,12},{9,13},{10,... | collective-permute-start | bytes 983048 | tf_op jit(solution)/shard_map/ppermute | solution.py:64
  52.9 23.3 %collective-permute-start.9 = (bf16[640,1280]{1,0:T(8,128)(2,1)}, bf16[640,1280]{1,0:T(8,128)(2,1)}, u32[]{:S(2)}, u32[]{:S(2)}) collective-permute-start(bf16[640,1280]{1,0:T(8,128)(2,1)} %get-tuple-element.37.refs_2_), channel_id=1, source_target_pairs={{0,8},{8,0},{16,24},{24,16},{1,9},{9,1},{17,25},{25,17},{2,10},{10... | collective-permute-start | bytes 4915208 | tf_op jit(solution)/shard_map/ppermute | solution.py:64
  52.9 23.3 %collective-permute-start.10 = (bf16[640,1280]{1,0:T(8,128)(2,1)S(1)}, bf16[640,1280]{1,0:T(8,128)(2,1)}, u32[]{:S(2)}, u32[]{:S(2)}) collective-permute-start(bf16[640,1280]{1,0:T(8,128)(2,1)S(1)} %get-tuple-element.38.refs_3_), channel_id=1, source_target_pairs={{0,8},{8,0},{16,24},{24,16},{1,9},{9,1},{17,25},{25,17},{2,10},{10... | collective-permute-start | bytes 4915208 | tf_op jit(solution)/shard_map/ppermute | solution.py:64
  53.4 26.7 %all-to-all-start = ((bf16[8,32,1408]{2,1,0:T(8,128)(2,1)}), bf16[8,32,1408]{2,1,0:T(8,128)(2,1)}, u32[]{:S(2)}, u32[]{:S(2)}) async-start(bf16[8,32,1408]{2,1,0:T(8,128)(2,1)} %bitcast.1), calls=%async_computation | async-start | bytes 1441792 | tf_op jit(solution)/shard_map/all_to_all | solution.py:376
  76.1 12.4 %collective-permute-start.14 = (bf16[640,1280]{1,0:T(8,128)(2,1)}, bf16[640,1280]{1,0:T(8,128)(2,1)}, u32[]{:S(2)}, u32[]{:S(2)}) collective-permute-start(bf16[640,1280]{1,0:T(8,128)(2,1)} %join_across.1.refs_6_.refs_0_), channel_id=1, source_target_pairs={{0,8},{8,0},{16,24},{24,16},{1,9},{9,1},{17,25},{25,17},{2,10},{10... | collective-permute-start | bytes 4915208 | tf_op jit(solution)/shard_map/ppermute | solution.py:64
  88.5 5.0 %copy-start.6 = (bf16[640,1280]{1,0:T(8,128)(2,1)S(1)}, bf16[640,1280]{1,0:T(8,128)(2,1)}, u32[]{:S(2)}) copy-start(bf16[640,1280]{1,0:T(8,128)(2,1)} %refs_1_.3) | copy-start | bytes 4915204
  88.5 5.0 %copy-start.13 = (bf16[128,1280]{1,0:T(8,128)(2,1)S(1)}, bf16[128,1280]{1,0:T(8,128)(2,1)}, u32[]{:S(2)}) copy-start(bf16[128,1280]{1,0:T(8,128)(2,1)} %embed_ref.1) | copy-start | bytes 983044
  91.8 17.2 %collective-permute-start.15 = (bf16[128,1280]{1,0:T(8,128)(2,1)S(1)}, bf16[128,1280]{1,0:T(8,128)(2,1)S(1)}, u32[]{:S(2)}, u32[]{:S(2)}) collective-permute-start(bf16[128,1280]{1,0:T(8,128)(2,1)S(1)} %text_theirs_last.1), channel_id=1, source_target_pairs={{0,4},{1,5},{2,6},{3,7},{4,0},{5,1},{6,2},{7,3},{8,12},{9,13},{10,... | collective-permute-start | bytes 983048 | tf_op jit(solution)/shard_map/ppermute | solution.py:64
  (11 other events, 20.4 us)

commit v3 on v2

--- a/solution.py
+++ b/solution.py
@@ -99,8 +99,8 @@
     pass
 
 
-def after(x, before):
-    return call(same_kernel, "after", like(x), (x, before), aliases={0: 0}, stored=(1,))
+def after(x, before, microseconds=0.001):
+    return call(same_kernel, "after", like(x), (x, before), microseconds=microseconds, aliases={0: 0}, stored=(1,))
 
 
 def feed_forward(rows, pieces):
@@ -133,39 +133,56 @@
     return pieces
 
 
-def first_kernel(rows_ref, ua, ba, da, ub, bb, db, *refs):
-    out_ref, token_ref, da_out, ub_out, db_out, sems = refs
-    copies = start_copies([(da, da_out), (ub, ub_out), (db, db_out)], sems)
-    rows = rows_ref[...]
-    copies[0].wait()
-    total = feed_forward(rows, vision_pieces(ua, ba, da_out))
-    for copy in copies[1:]:
+def bring_kernel(ua, da, before_ref, ua_out, da_out, sems):
+    for copy in start_copies([(ua, ua_out), (da, da_out)], sems):
         copy.wait()
-    total = total + feed_forward(rows, vision_pieces(ub_out, bb, db_out))
-    out_ref[...] = total.astype(BF16)
+
+
+def first_kernel(rows_ref, ua, ba, da, ub, bb, db, out_ref, token_ref, ub_out, db_out, sems):
+    copies = start_copies([(ub, ub_out), (db, db_out)], sems)
+
+    def far(at, ref, cut):
+        def there():
+            if cut.start == 0:
+                copies[at].wait()
+            return ref[cut, :]
+
+        return there
+
+    tile = ua.shape[0] // 2
+    pieces = vision_pieces(ua, ba, da)
+    for first in (0, tile):
+        cut = pl.ds(first, tile)
+        pieces.append((far(0, ub_out, cut), functools.partial(lambda cut: bb[cut], cut), far(1, db_out, cut)))
+    out_ref[...] = feed_forward(rows_ref[...], pieces).astype(BF16)
     token_ref[...] = jnp.zeros_like(token_ref)
 
 
 def pass_on(core_ref, ref, out_ref, sem):
     half = out_ref.shape[0]
-    for core in range(2):
-
-        @pl.when(core_ref[0] == core)
-        def _():
-            copy = pltpu.make_async_copy(ref.at[pl.ds(core * half, half)], out_ref, sem)
-            copy.start()
-            copy.wait()
+    first = pl.multiple_of(core_ref[0] * half, half)
+    return start_copies([(ref.at[pl.ds(first, half)], out_ref)], sem)
+
+
+def pass_kernel(core_ref, side_ref, *refs):
+    half_ref, sems = refs[-2:]
+    for copy in pass_on(core_ref, side_ref, half_ref, sems):
+        copy.wait()
 
 
 def second_kernel(core_ref, rows_ref, ua, ba, da, ub, bb, db, before_ref, *refs):
     if len(refs) > 2:
-        side_ref, _, half_ref, out_ref, token_ref, sems = refs
-        pass_on(core_ref, side_ref, half_ref, sems.at[0])
+        side_ref, embed_ref, _, half_ref, embed_out_ref, out_ref, token_ref, sems = refs
+        copies = pass_on(core_ref, side_ref, half_ref, sems)
+        embed_out_ref[...] = embed_ref[...]
     else:
         out_ref, token_ref = refs
+        copies = ()
     total = feed_forward(rows_ref[...], vision_pieces(ua, ba, da) + vision_pieces(ub, bb, db))
     out_ref[...] = total.astype(BF16)
     token_ref[...] = jnp.zeros_like(token_ref)
+    for copy in copies:
+        copy.wait()
 
 
 def own_kernel(first_ref, second_ref, ua, ba, da, ub, bb, db, before_ref, back_ref, proj, out_ref, proj_out, sems):
@@ -179,12 +196,7 @@
         copy.wait()
 
 
-def merge_kernel(core_ref, patches_ref, own_ref, back_ref, gain_ref, proj_ref, place_ref, where_ref, *refs):
-    if len(refs) > 1:
-        side_ref, _, half_ref, out_ref, sems = refs
-        pass_on(core_ref, side_ref, half_ref, sems.at[0])
-    else:
-        out_ref = refs[0]
+def merge_kernel(patches_ref, own_ref, back_ref, gain_ref, proj_ref, place_ref, where_ref, out_ref):
     rows, width = patches_ref.shape
     count = rows // 8
     wide = plane_rows(patches_ref[...])
@@ -205,78 +217,68 @@
     out_ref[:, width:] = where_ref[...]
 
 
-def place_text_rows(which, capacity, embed_ref, got_ref):
-    width = embed_ref.shape[1]
-    where = got_ref[:, width:].astype(F32)
+def place_text_rows(which, capacity, embed, got):
+    width = embed.shape[1]
+    where = got[:, width:].astype(F32)
     token = lax.broadcasted_iota(jnp.int32, where.shape, 1).astype(F32)
     side_of = lax.broadcasted_iota(jnp.int32, where.shape, 0) // capacity % 2
     pick = ((where == token) & (side_of == which)).astype(F32).astype(BF16)
     by_token = (((0,), (0,)), ((), ()))
-    picked = lax.dot_general(pick, got_ref[:, :width], by_token, preferred_element_type=F32)
+    picked = lax.dot_general(pick, got[:, :width], by_token, preferred_element_type=F32)
     taken = lax.dot_general(pick, jnp.ones((pick.shape[0], 128), BF16), by_token, preferred_element_type=F32)
-    return jnp.where(taken[:, :1] > 0.5, picked, embed_ref[...].astype(F32))
-
-
-def joined_kernel(up_ref, down_ref, before_ref, embed_ref, out_ref):
-    half = up_ref.shape[0]
-    out_ref[pl.ds(0, half), :] = up_ref[...]
-    out_ref[pl.ds(half, half), :] = down_ref[...]
-
-
-def text_pieces(slices):
-    return [
-        (functools.partial(lambda ref: ref[...], up), None, functools.partial(lambda ref: ref[...], down))
-        for up, down in slices
-    ]
-
-
-def across_pieces(halves):
-    half = halves[0].shape[0] // 2
-    up, down = pl.ds(0, half), pl.ds(half, half)
-    return [
-        (
-            functools.partial(lambda ref: ref[up, :], ref),
-            None,
-            functools.partial(lambda ref: ref[down, :], ref),
-        )
-        for ref in halves
-    ]
-
-
-def loaded_pieces(refs, up, down, sems):
-    copies = start_copies(
-        [(ref, (up, down)[at % 2].at[at // 2]) for at, ref in enumerate(refs)], sems
-    )
+    return jnp.where(taken[:, :1] > 0.5, picked, embed.astype(F32))
+
+
+def load_text(rows, slices, halves, rooms, up, down, sems):
+    half = up.shape[1] // 2
+    pairs = list(zip(rows, rooms))
+    waits = []
+    for at in range(3):
+        for ref, room in ((slices[2 * at], up), (slices[2 * at + 1], down)):
+            waits.append([len(pairs)])
+            pairs.append((ref, room.at[at]))
+    for at, room in enumerate((up, down)):
+        if halves:
+            waits.append([len(pairs), len(pairs) + 1])
+        for number, ref in enumerate(halves[2 * at : 2 * at + 2]):
+            pairs.append((ref, room.at[3, pl.ds(number * half, half)]))
+    copies = start_copies(pairs, sems)
 
     def read(at):
-        copies[at].wait()
+        for number in waits[at]:
+            copies[number].wait()
         return (up, down)[at % 2][at // 2]
 
-    return [
-        (functools.partial(read, at), None, functools.partial(read, at + 1)) for at in range(0, len(refs), 2)
-    ]
-
-
-def theirs_kernel(capacity, embed_ref, got_ref, gain_ref, *refs):
-    slices, (normed_ref, total_ref), scratch = refs[:6], refs[6:8], refs[8:]
-    pieces = loaded_pieces(slices, *scratch)
-    text_rows = place_text_rows(1, capacity, embed_ref, got_ref)
+    pieces = [(functools.partial(read, at), None, functools.partial(read, at + 1)) for at in range(0, len(waits), 2)]
+    for copy in copies[: len(rows)]:
+        copy.wait()
+    return pieces
+
+
+def theirs_kernel(capacity, embed_ref, got_ref, *refs):
+    slices, gain_ref, normed_ref, total_ref = refs[:6], refs[6], refs[7], refs[8]
+    embed, got, up, down, sems = refs[9:]
+    pieces = load_text((embed_ref, got_ref), slices, (), (embed, got), up, down, sems)
+    text_rows = place_text_rows(1, capacity, embed[...], got[...])
     normed = normalize(text_rows, gain_ref[...]).astype(BF16)
     normed_ref[...] = normed
     total_ref[...] = feed_forward(normed, pieces)
 
 
-def theirs_last_kernel(normed_ref, total_ref, *refs):
-    pieces = across_pieces(refs[:-1])
-    refs[-1][...] = (total_ref[...] + feed_forward(normed_ref[...], pieces)).astype(BF16)
-
-
-def mine_kernel(capacity, embed_ref, got_ref, gain_ref, *refs):
-    slices, halves, out_ref, scratch = refs[:6], refs[6:8], refs[8], refs[9:]
-    pieces = loaded_pieces(slices, *scratch)
-    text_rows = place_text_rows(0, capacity, embed_ref, got_ref)
-    normed = normalize(text_rows, gain_ref[...]).astype(BF16)
-    out_ref[...] = text_rows + feed_forward(normed, across_pieces(halves) + pieces)
+def theirs_last_kernel(normed_ref, total_ref, up_ref, other_up_ref, down_ref, other_down_ref, out_ref):
+    def both(mine_ref, other_ref):
+        return lambda: jnp.concatenate([mine_ref[...], other_ref[...]], axis=0)
+
+    total = feed_forward(normed_ref[...], [(both(up_ref, other_up_ref), None, both(down_ref, other_down_ref))])
+    out_ref[...] = (total_ref[...] + total).astype(BF16)
+
+
+def mine_kernel(capacity, embed_ref, got_ref, *refs):
+    slices, halves, gain_ref, out_ref = refs[:6], refs[6:10], refs[10], refs[11]
+    embed, got, up, down, sems = refs[12:]
+    pieces = load_text((embed_ref, got_ref), slices, halves, (embed, got), up, down, sems)
+    text_rows = place_text_rows(0, capacity, embed[...], got[...])
+    out_ref[...] = text_rows + feed_forward(normalize(text_rows, gain_ref[...]).astype(BF16), pieces)
 
 
 def per_device(
@@ -316,36 +318,44 @@
     half_rows = jax.ShapeDtypeStruct((patch_count // 2, width), BF16)
     far_up, far_down = swap(vis_up, "seq", 1), swap(vis_down, "seq", 1)
     other_bias = swap(after(vis_bias, far_up), "seq", 1)
-    first, second, _ = call(
-        norm_patches_kernel, "norm_patches", (half_rows, half_rows, TOKEN), (patches, vis_gain)
+    first, second, normed = call(
+        norm_patches_kernel, "norm_patches", (half_rows, half_rows, TOKEN), (patches, vis_gain), megabytes=40
     )
     far_first, far_second = swap(first, "seq", 2), swap(second, "seq", 2)
-    args = (far_first, vis_up, vis_bias, vis_down, far_up, other_bias, far_down)
-    outs = (half_rows, TOKEN, like(vis_down), like(vis_up), like(vis_down))
+    near_up, near_down = call(
+        bring_kernel,
+        "bring_vision",
+        (like(vis_up), like(vis_down)),
+        (vis_up, vis_down, normed),
+        stored=(0, 1),
+        copies=2,
+        megabytes=44,
+    )
+    args = (far_first, near_up, vis_bias, near_down, far_up, other_bias, far_down)
+    outs = (half_rows, TOKEN, like(vis_up), like(vis_down))
     if paired:
         side_up, side_down = swap_by_core(text_up, (1, 2)), swap_by_core(text_down, (1, 2))
-    part_first, first_done, near_down, far_up, far_down = call(
-        first_kernel, "vision_first", outs, args, stored=(3, 4, 6), copies=3
-    )
-    weights = (vis_up, vis_bias, near_down, far_up, other_bias, far_down)
+    part_first, first_done, far_up, far_down = call(
+        first_kernel, "vision_first", outs, args, stored=(4, 6), copies=2, megabytes=36
+    )
+    weights = (near_up, vis_bias, near_down, far_up, other_bias, far_down)
     back_first = swap(part_first, "seq", 2)
-    if paired:
-        other_embed = swap(text_embed, "blk", 4)
     args = (core, far_second, *weights, first_done)
     outs = (half_rows, TOKEN)
     half_slice = jax.ShapeDtypeStruct((text_up.shape[0] // 2, width), BF16)
     if paired:
-        side_up, across_up, part_second, second_done = call(
+        side_up, across_up, other_embed, part_second, second_done = call(
             second_kernel,
             "vision_second",
-            (like(side_up), half_slice, *outs),
-            args + (side_up,),
+            (like(side_up), half_slice, like(text_embed), *outs),
+            args + (side_up, text_embed),
             aliases={len(args): 0},
             copies=1,
             scalars=1,
             microseconds=30,
         )
         other_up, across_up = swap(side_up, "seq", 1), swap_by_core(across_up, (2, 1))
+        other_embed = swap(other_embed, "blk", 4)
     else:
         part_second, second_done = call(second_kernel, "vision_second", outs, args, scalars=1, microseconds=30)
     back_second = swap(part_second, "seq", 2)
@@ -356,59 +366,58 @@
         (own_rows, like(merge_proj)),
         (first, second, *weights, second_done, back_first, merge_proj),
         stored=(10,),
+        microseconds=5,
         copies=1,
     )
-    args = (core, patches, own, back_second, merge_gain, merge_proj, place, where)
     sent_rows = jax.ShapeDtypeStruct((place.shape[0], width + 128), BF16)
+    args = (patches, own, back_second, merge_gain, merge_proj, place, where)
+    send = call(merge_kernel, "merge_rows", sent_rows, args)
     if paired:
-        side_down, across_down, send = call(
-            merge_kernel,
-            "merge_rows",
-            (like(side_down), half_slice, sent_rows),
-            args + (side_down,),
-            aliases={len(args): 0},
+        side_down, across_up, across_down = call(
+            pass_kernel,
+            "pass_down",
+            (like(side_down), like(across_up), half_slice),
+            (core, side_down, send, across_up, other_embed),
+            aliases={1: 0, 3: 1},
+            scalars=1,
+            stored=(2, 3, 4),
             copies=1,
-            scalars=1,
+            microseconds=0.001,
         )
         other_down, across_down = swap(side_down, "seq", 1), swap_by_core(across_down, (2, 1))
-    else:
-        send = call(merge_kernel, "merge_rows", sent_rows, args, scalars=1)
     got = lax.all_to_all(send, "blk", split_axis=0, concat_axis=0, tiled=True)
     if paired:
-        across = call(joined_kernel, "join_across", like(text_up), (across_up, across_down, send, other_embed), stored=(2,), microseconds=20)
-        halves = (across, swap(across, "seq", 1))
-        other_up, other_down = call(
-            same_kernel,
-            "hold",
-            (like(other_up), like(other_down)),
-            (other_up, other_down),
-            aliases={0: 0, 1: 1},
-            stored=(0, 1),
-            microseconds=20,
-        )
+        got = after(got, send, microseconds=5)
         slices = (text_up, text_down, side_up, side_down, other_up, other_down)
-        room = tuple(pltpu.VMEM((3, *text_up.shape), BF16) for _ in range(2))
-        tokens = jax.ShapeDtypeStruct((token_count, width), F32)
+        room = (
+            pltpu.VMEM(text_embed.shape, BF16),
+            pltpu.VMEM(got.shape, BF16),
+            pltpu.VMEM((4, *text_up.shape), BF16),
+            pltpu.VMEM((4, *text_up.shape), BF16),
+        )
+        sums = jax.ShapeDtypeStruct((token_count, width), F32)
         text_normed, total = call(
             functools.partial(theirs_kernel, capacity),
             "text_theirs",
-            (like(text_embed), tokens),
-            (other_embed, got, text_gain, *slices),
-            stored=tuple(range(3, 9)),
-            copies=6,
+            (like(text_embed), sums),
+            (other_embed, got, *slices, text_gain),
+            stored=tuple(range(8)),
+            copies=8,
             scratch=room,
-            megabytes=20,
-        )
+            megabytes=24,
+        )
+        across_down = after(across_down, text_normed)
+        halves = (across_up, swap(across_up, "seq", 1), across_down, swap(across_down, "seq", 1))
         theirs = call(theirs_last_kernel, "text_theirs_last", like(text_embed), (text_normed, total, *halves))
         mine = call(
             functools.partial(mine_kernel, capacity),
             "text_mine",
-            tokens,
-            (text_embed, got, text_gain, *slices, *halves),
-            stored=tuple(range(3, 9)),
-            copies=6,
+            sums,
+            (text_embed, got, *slices, *halves, text_gain),
+            stored=tuple(range(12)),
+            copies=12,
             scratch=room,
-            megabytes=20,
+            megabytes=24,
         )
         return (mine + swap(theirs, "blk", 4).astype(F32)).astype(BF16)
     tokens = jnp.arange(token_count, dtype=jnp.int32).astype(BF16)

time: 111 us -> 103 us (0.928)
  the two profiles are of different devices: /device:TPU:6 before, /device:TPU:0 now
where the time goes in v3:
time: 103 us
  Pallas kernels  40.2 us (39%)
  waiting for transfers between devices  30.1 us (29%)
  starting transfers between devices  20.9 us (20%)
  local copies, waits for them, and re-layouts  8.93 us (9%)
  other arithmetic  2.17 us (2%)
    pallas_call x13, Pallas kernels, call(): pl.pallas_call(kernel, out_shape=out_shape, in_specs=specs, out_specs=tup...  40.2 us
    ppermute x13, waiting for transfers between devices, swap(): return lax.ppermute(x, axis, [(i, i ^ bit) for i in range(size)])  17.2 us
    all_to_all x1, waiting for transfers between devices, per_device(): got = lax.all_to_all(send, 'blk', split_axis=0, concat_axis=0, tiled=True)  12.8 us
    ppermute x4, starting transfers between devices, swap_by_core(): return lax.ppermute(x, ('seq', 'blk'), pairs)  8.85 us
    unnamed x29, local copies, waits for them, and re-layouts  8.83 us
    ppermute x13, starting transfers between devices, swap(): return lax.ppermute(x, axis, [(i, i ^ bit) for i in range(size)])  7.71 us
    all_to_all x1, starting transfers between devices, per_device(): got = lax.all_to_all(send, 'blk', split_axis=0, concat_axis=0, tiled=True)  4.38 us
  transfers between devices with their start and end apart: 18, of which 5 were waited for; matrix products, arithmetic and copies ran while one was open for 2% of the time, Pallas kernels for 37%

profile of v3, /device:TPU:0, one launch (start us, length us, event | category | flops | bytes accessed | tf_op | source)
XLA Modules:
  0.0 102.6 jit_solution(13993664033861853264)
XLA Ops:
  0.5 3.0 %collective-permute-start.5 = (bf16[640,1280]{1,0:T(8,128)(2,1)}, bf16[640,1280]{1,0:T(8,128)(2,1)}, u32[]{:S(2)}, u32[]{:S(2)}) collective-permute-start(bf16[640,1280]{1,0:T(8,128)(2,1)} %refs_0_.4), channel_id=1, source_target_pairs={{0,1},{1,0},{2,3},{3,2},{4,5},{5,4},{6,7},{7,6},{8,10},{9,11},{10,... | collective-permute-start | bytes 4915208 | tf_op jit(solution)/shard_map/ppermute | solution.py:70
  5.3 1.4 %norm_patches.1 = (bf16[128,1280]{1,0:T(8,128)(2,1)}, bf16[128,1280]{1,0:T(8,128)(2,1)}, f32[8,128]{1,0:T(8,128)S(1)}) custom-call(bf16[256,1280]{1,0:T(8,128)(2,1)S(1)} %copy-done.4, f32[1280]{0:T(1024)S(1)} %copy-done.13), custom_call_target="tpu_custom_call" | custom-call | flops 1000000 | bytes 1000 | tf_op jit(solution)/shard_map/norm_patches/pallas_call | solution.py:32
  6.7 1.5 %collective-permute-start = (bf16[128,1280]{1,0:T(8,128)(2,1)}, bf16[128,1280]{1,0:T(8,128)(2,1)}, u32[]{:S(2)}, u32[]{:S(2)}) collective-permute-start(bf16[128,1280]{1,0:T(8,128)(2,1)} %get-tuple-element.26.first_ref), channel_id=1, source_target_pairs={{0,16},{8,24},{16,0},{24,8},{1,17},{9,25},{17,1},{25,9},{2,18},{10... | collective-permute-start | bytes 983048 | tf_op jit(solution)/shard_map/ppermute | solution.py:64
  10.6 2.9 %copy-done.3 = bf16[1280,1280]{1,0:T(8,128)(2,1)S(1)} copy-done((bf16[1280,1280]{1,0:T(8,128)(2,1)S(1)}, bf16[1280,1280]{1,0:T(8,128)(2,1)}, u32[]{:S(2)}) %copy-start.3) | copy-done | bytes 3276824
  13.6 2.3 %bring_vision.1 = (bf16[1280,1280]{1,0:T(8,128)(2,1)S(1)}, bf16[1280,1280]{1,0:T(8,128)(2,1)S(1)}) custom-call(bf16[1280,1280]{1,0:T(8,128)(2,1)S(1)} %copy-done.3, bf16[1280,1280]{1,0:T(8,128)(2,1)} %da.1, f32[8,128]{1,0:T(8,128)S(1)} %get-tuple-element.28.before_ref), custom_call_target="tpu_custom_call" | custom-call | flops 1000000 | bytes 1000 | tf_op jit(solution)/shard_map/bring_vision/pallas_call | solution.py:32
  15.9 1.7 %collective-permute-done.rows_ref = bf16[128,1280]{1,0:T(8,128)(2,1)} collective-permute-done((bf16[128,1280]{1,0:T(8,128)(2,1)}, bf16[128,1280]{1,0:T(8,128)(2,1)}, u32[]{:S(2)}, u32[]{:S(2)}) %collective-permute-start) | collective-permute-done | bytes 327712 | tf_op jit(solution)/shard_map/ppermute | solution.py:64
  17.6 1.6 %collective-permute-start.8 = (bf16[640,1280]{1,0:T(8,128)(2,1)}, bf16[640,1280]{1,0:T(8,128)(2,1)S(1)}, u32[]{:S(2)}, u32[]{:S(2)}) collective-permute-start(bf16[640,1280]{1,0:T(8,128)(2,1)} %refs_1_.5), channel_id=1, source_target_pairs={{0,1},{1,0},{2,3},{3,2},{4,5},{5,4},{6,7},{7,6},{8,10},{9,11},{10,... | collective-permute-start | bytes 4915208 | tf_op jit(solution)/shard_map/ppermute | solution.py:70
  19.2 1.9 %copy-done.1 = bf16[1280,1280]{1,0:T(8,128)(2,1)S(1)} copy-done((bf16[1280,1280]{1,0:T(8,128)(2,1)S(1)}, bf16[1280,1280]{1,0:T(8,128)(2,1)}, u32[]{:S(2)}) %copy-start.1) | copy-done | bytes 3276824
  21.2 5.1 %vision_first.1 = (bf16[128,1280]{1,0:T(8,128)(2,1)S(1)}, f32[8,128]{1,0:T(8,128)S(1)}, bf16[1280,1280]{1,0:T(8,128)(2,1)S(1)}, bf16[1280,1280]{1,0:T(8,128)(2,1)S(1)}) custom-call(bf16[128,1280]{1,0:T(8,128)(2,1)} %collective-permute-done.rows_ref, bf16[1280,1280]{1,0:T(8,128)(2,1)S(1)} %get-tuple-element.29.ua, f32[1280]{0:T(1024)S(1)} %copy-done.10, ...), custom_call_target="tpu_custom_call" | custom-call | flops 1000000 | bytes 1000 | tf_op jit(solution)/shard_map/vision_first/pallas_call | solution.py:32
  26.2 1.6 %collective-permute-start.6 = (bf16[128,1280]{1,0:T(8,128)(2,1)S(1)}, bf16[128,1280]{1,0:T(8,128)(2,1)S(1)}, u32[]{:S(2)}, u32[]{:S(2)}) collective-permute-start(bf16[128,1280]{1,0:T(8,128)(2,1)S(1)} %get-tuple-element.35), channel_id=1, source_target_pairs={{0,16},{8,24},{16,0},{24,8},{1,17},{9,25},{17,1},{25,9},{2,18},{10... | collective-permute-start | bytes 983048 | tf_op jit(solution)/shard_map/ppermute | solution.py:64
  27.8 5.5 %vision_second.1 = (bf16[640,1280]{1,0:T(8,128)(2,1)}, bf16[320,1280]{1,0:T(8,128)(2,1)}, bf16[128,1280]{1,0:T(8,128)(2,1)S(1)}, bf16[128,1280]{1,0:T(8,128)(2,1)S(1)}, f32[8,128]{1,0:T(8,128)S(1)}) custom-call(s32[1]{0:T(128)} %bitcast.core_ref, bf16[128,1280]{1,0:T(8,128)(2,1)} %collective-permute-done.4.rows_ref, ...), custom_call_target="tpu_custom_call", output_to_operand_aliasing={{0}: (9, {})} | custom-call | flops 30000001024 | bytes 1000 | tf_op jit(solution)/shard_map/vision_second/pallas_call | solution.py:32
  33.3 1.6 %collective-permute-start.9 = (bf16[320,1280]{1,0:T(8,128)(2,1)}, bf16[320,1280]{1,0:T(8,128)(2,1)S(1)}, u32[]{:S(2)}, u32[]{:S(2)}) collective-permute-start(bf16[320,1280]{1,0:T(8,128)(2,1)} %get-tuple-element.40), channel_id=1, source_target_pairs={{0,2},{1,3},{2,0},{3,1},{4,6},{5,7},{6,4},{7,5},{8,9},{9,8},{10,11... | collective-permute-start | bytes 2457608 | tf_op jit(solution)/shard_map/ppermute | solution.py:70
  35.9 2.6 %collective-permute-start.10 = (bf16[128,1280]{1,0:T(8,128)(2,1)S(1)}, bf16[128,1280]{1,0:T(8,128)(2,1)S(1)}, u32[]{:S(2)}, u32[]{:S(2)}) collective-permute-start(bf16[128,1280]{1,0:T(8,128)(2,1)S(1)} %get-tuple-element.41), channel_id=1, source_target_pairs={{0,4},{1,5},{2,6},{3,7},{4,0},{5,1},{6,2},{7,3},{8,12},{9,13},{10,... | collective-permute-start | bytes 983048 | tf_op jit(solution)/shard_map/ppermute | solution.py:64
  38.5 5.9 %vision_own.1 = (f32[256,1280]{1,0:T(8,128)S(1)}, bf16[5120,1280]{1,0:T(8,128)(2,1)S(1)}) custom-call(bf16[128,1280]{1,0:T(8,128)(2,1)} %get-tuple-element.26.first_ref, bf16[128,1280]{1,0:T(8,128)(2,1)} %get-tuple-element.27.second_ref, bf16[1280,1280]{1,0:T(8,128)(2,1)S(1)} %get-tuple-element.29.ua, f32[1280]{0:T(1024)S(1)} %copy-done.10, ...), custom_call_target="tpu_custom_call" | custom-call | flops 5000000000 | bytes 1000 | tf_op jit(solution)/shard_map/vision_own/pallas_call | solution.py:32
  44.6 4.5 %merge_rows.1.refs_1_.refs_0_ = bf16[256,1408]{1,0:T(8,128)(2,1)} custom-call(bf16[256,1280]{1,0:T(8,128)(2,1)S(1)} %copy-done.5, f32[256,1280]{1,0:T(8,128)S(1)} %get-tuple-element.36.own_ref, bf16[128,1280]{1,0:T(8,128)(2,1)S(1)} %collective-permute-done.7.back_ref, f32[1280]{0:T(1024)S(1)} %copy-done.12, ...), custom_call_target="tpu_custom_call" | custom-call | flops 1000000 | bytes 1000 | tf_op jit(solution)/shard_map/merge_rows/pallas_call | solution.py:32
  49.1 4.4 %all-to-all-start = ((bf16[8,32,1408]{2,1,0:T(8,128)(2,1)}), bf16[8,32,1408]{2,1,0:T(8,128)(2,1)}, u32[]{:S(2)}, u32[]{:S(2)}) async-start(bf16[8,32,1408]{2,1,0:T(8,128)(2,1)} %bitcast.1), calls=%async_computation | async-start | bytes 1441792 | tf_op jit(solution)/shard_map/all_to_all | solution.py:388
  53.6 3.2 %collective-permute-done.10.refs_2_.embed_ref = bf16[128,1280]{1,0:T(8,128)(2,1)S(1)} collective-permute-done((bf16[128,1280]{1,0:T(8,128)(2,1)S(1)}, bf16[128,1280]{1,0:T(8,128)(2,1)S(1)}, u32[]{:S(2)}, u32[]{:S(2)}) %collective-permute-start.10) | collective-permute-done | bytes 327712 | tf_op jit(solution)/shard_map/ppermute | solution.py:64
  57.9 2.6 %collective-permute-start.14 = (bf16[320,1280]{1,0:T(8,128)(2,1)}, bf16[320,1280]{1,0:T(8,128)(2,1)S(1)}, u32[]{:S(2)}, u32[]{:S(2)}) collective-permute-start(bf16[320,1280]{1,0:T(8,128)(2,1)} %get-tuple-element.44), channel_id=1, source_target_pairs={{0,2},{1,3},{2,0},{3,1},{4,6},{5,7},{6,4},{7,5},{8,9},{9,8},{10,11... | collective-permute-start | bytes 2457608 | tf_op jit(solution)/shard_map/ppermute | solution.py:70
  60.5 12.8 %all-to-all-done = bf16[8,32,1408]{2,1,0:T(8,128)(2,1)} async-done(((bf16[8,32,1408]{2,1,0:T(8,128)(2,1)}), bf16[8,32,1408]{2,1,0:T(8,128)(2,1)}, u32[]{:S(2)}, u32[]{:S(2)}) %all-to-all-start) | async-done | bytes 720928 | tf_op jit(solution)/shard_map/all_to_all | solution.py:388
  74.8 5.5 %text_theirs.1 = (bf16[128,1280]{1,0:T(8,128)(2,1)S(1)}, f32[128,1280]{1,0:T(8,128)S(1)}) custom-call(bf16[128,1280]{1,0:T(8,128)(2,1)S(1)} %copy-done.7, bf16[256,1408]{1,0:T(8,128)(2,1)} %after.4.got_ref, bf16[640,1280]{1,0:T(8,128)(2,1)S(1)} %copy-done.2, bf16[640,1280]{1,0:T(8,128)(2,1)} %refs_1_.5, bf16[640,1280]{1,0:T(8,128)(2,1)} %get-tuple-element.39.refs_2_, ...), custom_call_target="tpu_custom_call" | custom-call | flops 1000000 | bytes 1000 | tf_op jit(solution)/shard_map/text_theirs/pallas_call | solution.py:32
  80.5 2.3 %collective-permute-done.15.refs_9_.other_down_ref = bf16[320,1280]{1,0:T(8,128)(2,1)S(1)} collective-permute-done((bf16[320,1280]{1,0:T(8,128)(2,1)S(1)}, bf16[320,1280]{1,0:T(8,128)(2,1)S(1)}, u32[]{:S(2)}, u32[]{:S(2)}) %collective-permute-start.15) | collective-permute-done | bytes 819232 | tf_op jit(solution)/shard_map/ppermute | solution.py:64
  82.8 2.2 %text_theirs_last.1 = bf16[128,1280]{1,0:T(8,128)(2,1)S(1)} custom-call(bf16[128,1280]{1,0:T(8,128)(2,1)S(1)} %get-tuple-element.45.refs_1_.normed_ref, f32[128,1280]{1,0:T(8,128)S(1)} %get-tuple-element.46.total_ref, bf16[320,1280]{1,0:T(8,128)(2,1)S(1)} %get-tuple-element.43.refs_6_.up_ref, bf16[320,1280]{1,0:T(8,128)(2,1)} %collective-permute-done.13.refs_7_.other_up_ref, ...), custom_call_target="tpu_custom_call" | custom-call | flops 1000000 | bytes 1000 | tf_op jit(solution)/shard_map/text_theirs_last/pallas_call | solution.py:32
  85.1 6.7 %text_mine.1 = f32[128,1280]{1,0:T(8,128)S(1)} custom-call(bf16[128,1280]{1,0:T(8,128)(2,1)S(1)} %copy-done.9, bf16[256,1408]{1,0:T(8,128)(2,1)} %after.4.got_ref, bf16[640,1280]{1,0:T(8,128)(2,1)S(1)} %copy-done.2, bf16[640,1280]{1,0:T(8,128)(2,1)} %refs_1_.5, bf16[640,1280]{1,0:T(8,128)(2,1)} %get-tuple-element.39.refs_2_, ...), custom_call_target="tpu_custom_call" | custom-call | flops 1000000 | bytes 1000 | tf_op jit(solution)/shard_map/text_mine/pallas_call | solution.py:32
  91.8 10.0 %collective-permute-done.16 = bf16[128,1280]{1,0:T(8,128)(2,1)S(1)} collective-permute-done((bf16[128,1280]{1,0:T(8,128)(2,1)S(1)}, bf16[128,1280]{1,0:T(8,128)(2,1)S(1)}, u32[]{:S(2)}, u32[]{:S(2)}) %collective-permute-start.16) | collective-permute-done | bytes 327712 | tf_op jit(solution)/shard_map/ppermute | solution.py:64
  (64 shorter events, 9.3 us)
Async XLA Ops:
  0.0 10.4 %collective-permute-start.1 = (bf16[1280,1280]{1,0:T(8,128)(2,1)}, bf16[1280,1280]{1,0:T(8,128)(2,1)S(1)}, u32[]{:S(2)}, u32[]{:S(2)}) collective-permute-start(bf16[1280,1280]{1,0:T(8,128)(2,1)} %ua.1), channel_id=1, source_target_pairs={{0,8},{8,0},{16,24},{24,16},{1,9},{9,1},{17,25},{25,17},{2,10},{10... | collective-permute-start | bytes 9830408 | tf_op jit(solution)/shard_map/ppermute | solution.py:64
  0.5 18.8 %collective-permute-start.3 = (bf16[1280,1280]{1,0:T(8,128)(2,1)}, bf16[1280,1280]{1,0:T(8,128)(2,1)}, u32[]{:S(2)}, u32[]{:S(2)}) collective-permute-start(bf16[1280,1280]{1,0:T(8,128)(2,1)} %da.1), channel_id=1, source_target_pairs={{0,8},{8,0},{16,24},{24,16},{1,9},{9,1},{17,25},{25,17},{2,10},{10... | collective-permute-start | bytes 9830408 | tf_op jit(solution)/shard_map/ppermute | solution.py:64
  0.5 27.3 %collective-permute-start.5 = (bf16[640,1280]{1,0:T(8,128)(2,1)}, bf16[640,1280]{1,0:T(8,128)(2,1)}, u32[]{:S(2)}, u32[]{:S(2)}) collective-permute-start(bf16[640,1280]{1,0:T(8,128)(2,1)} %refs_0_.4), channel_id=1, source_target_pairs={{0,1},{1,0},{2,3},{3,2},{4,5},{5,4},{6,7},{7,6},{8,10},{9,11},{10,... | collective-permute-start | bytes 4915208 | tf_op jit(solution)/shard_map/ppermute | solution.py:70
  6.7 10.9 %collective-permute-start = (bf16[128,1280]{1,0:T(8,128)(2,1)}, bf16[128,1280]{1,0:T(8,128)(2,1)}, u32[]{:S(2)}, u32[]{:S(2)}) collective-permute-start(bf16[128,1280]{1,0:T(8,128)(2,1)} %get-tuple-element.26.first_ref), channel_id=1, source_target_pairs={{0,16},{8,24},{16,0},{24,8},{1,17},{9,25},{17,1},{25,9},{2,18},{10... | collective-permute-start | bytes 983048 | tf_op jit(solution)/shard_map/ppermute | solution.py:64
  8.2 19.6 %collective-permute-start.4 = (bf16[128,1280]{1,0:T(8,128)(2,1)}, bf16[128,1280]{1,0:T(8,128)(2,1)}, u32[]{:S(2)}, u32[]{:S(2)}) collective-permute-start(bf16[128,1280]{1,0:T(8,128)(2,1)} %get-tuple-element.27.second_ref), channel_id=1, source_target_pairs={{0,16},{8,24},{16,0},{24,8},{1,17},{9,25},{17,1},{25,9},{2,18},{10... | collective-permute-start | bytes 983048 | tf_op jit(solution)/shard_map/ppermute | solution.py:64
  10.5 5.5 %copy-start = (bf16[1280,1280]{1,0:T(8,128)(2,1)}, bf16[1280,1280]{1,0:T(8,128)(2,1)S(1)}, u32[]{:S(2)}) copy-start(bf16[1280,1280]{1,0:T(8,128)(2,1)S(1)} %collective-permute-done.1.refs_1_.ub) | copy-start | bytes 9830404
  10.5 8.7 %collective-permute-start.2 = (f32[1280]{0:T(1024)S(1)}, f32[1280]{0:T(1024)S(1)}, u32[]{:S(2)}, u32[]{:S(2)}) collective-permute-start(f32[1280]{0:T(1024)S(1)} %after.3), channel_id=1, source_target_pairs={{0,8},{8,0},{16,24},{24,16},{1,9},{9,1},{17,25},{25,17},{2,10},{10... | collective-permute-start | bytes 15368 | tf_op jit(solution)/shard_map/ppermute | solution.py:64
  13.6 5.6 %copy-start.10 = (f32[1280]{0:T(1024)S(1)}, f32[1280]{0:T(1024)}, u32[]{:S(2)}) copy-start(f32[1280]{0:T(1024)} %ba.5) | copy-start | bytes 15364
  17.6 36.0 %collective-permute-start.8 = (bf16[640,1280]{1,0:T(8,128)(2,1)}, bf16[640,1280]{1,0:T(8,128)(2,1)S(1)}, u32[]{:S(2)}, u32[]{:S(2)}) collective-permute-start(bf16[640,1280]{1,0:T(8,128)(2,1)} %refs_1_.5), channel_id=1, source_target_pairs={{0,1},{1,0},{2,3},{3,2},{4,5},{5,4},{6,7},{7,6},{8,10},{9,11},{10,... | collective-permute-start | bytes 4915208 | tf_op jit(solution)/shard_map/ppermute | solution.py:70
  21.2 6.6 %copy-start.8 = (bf16[128,1280]{1,0:T(8,128)(2,1)S(1)}, bf16[128,1280]{1,0:T(8,128)(2,1)}, u32[]{:S(2)}) copy-start(bf16[128,1280]{1,0:T(8,128)(2,1)} %embed_ref.1) | copy-start | bytes 983044
  26.2 12.3 %collective-permute-start.6 = (bf16[128,1280]{1,0:T(8,128)(2,1)S(1)}, bf16[128,1280]{1,0:T(8,128)(2,1)S(1)}, u32[]{:S(2)}, u32[]{:S(2)}) collective-permute-start(bf16[128,1280]{1,0:T(8,128)(2,1)S(1)} %get-tuple-element.35), channel_id=1, source_target_pairs={{0,16},{8,24},{16,0},{24,8},{1,17},{9,25},{17,1},{25,9},{2,18},{10... | collective-permute-start | bytes 983048 | tf_op jit(solution)/shard_map/ppermute | solution.py:64
  33.3 23.5 %collective-permute-start.9 = (bf16[320,1280]{1,0:T(8,128)(2,1)}, bf16[320,1280]{1,0:T(8,128)(2,1)S(1)}, u32[]{:S(2)}, u32[]{:S(2)}) collective-permute-start(bf16[320,1280]{1,0:T(8,128)(2,1)} %get-tuple-element.40), channel_id=1, source_target_pairs={{0,2},{1,3},{2,0},{3,1},{4,6},{5,7},{6,4},{7,5},{8,9},{9,8},{10,11... | collective-permute-start | bytes 2457608 | tf_op jit(solution)/shard_map/ppermute | solution.py:70
  35.3 9.1 %collective-permute-start.7 = (bf16[128,1280]{1,0:T(8,128)(2,1)S(1)}, bf16[128,1280]{1,0:T(8,128)(2,1)S(1)}, u32[]{:S(2)}, u32[]{:S(2)}) collective-permute-start(bf16[128,1280]{1,0:T(8,128)(2,1)S(1)} %get-tuple-element.37), channel_id=1, source_target_pairs={{0,16},{8,24},{16,0},{24,8},{1,17},{9,25},{17,1},{25,9},{2,18},{10... | collective-permute-start | bytes 983048 | tf_op jit(solution)/shard_map/ppermute | solution.py:64
  35.9 20.8 %collective-permute-start.10 = (bf16[128,1280]{1,0:T(8,128)(2,1)S(1)}, bf16[128,1280]{1,0:T(8,128)(2,1)S(1)}, u32[]{:S(2)}, u32[]{:S(2)}) collective-permute-start(bf16[128,1280]{1,0:T(8,128)(2,1)S(1)} %get-tuple-element.41), channel_id=1, source_target_pairs={{0,4},{1,5},{2,6},{3,7},{4,0},{5,1},{6,2},{7,3},{8,12},{9,13},{10,... | collective-permute-start | bytes 983048 | tf_op jit(solution)/shard_map/ppermute | solution.py:64
  38.5 6.0 %copy-start.5 = (bf16[256,1280]{1,0:T(8,128)(2,1)S(1)}, bf16[256,1280]{1,0:T(8,128)(2,1)}, u32[]{:S(2)}) copy-start(bf16[256,1280]{1,0:T(8,128)(2,1)} %patches_ref.3) | copy-start | bytes 1966084
  38.5 6.0 %copy-start.12 = (f32[1280]{0:T(1024)S(1)}, f32[1280]{0:T(1024)}, u32[]{:S(2)}) copy-start(f32[1280]{0:T(1024)} %gain_ref.3) | copy-start | bytes 15364
  49.1 24.2 %all-to-all-start = ((bf16[8,32,1408]{2,1,0:T(8,128)(2,1)}), bf16[8,32,1408]{2,1,0:T(8,128)(2,1)}, u32[]{:S(2)}, u32[]{:S(2)}) async-start(bf16[8,32,1408]{2,1,0:T(8,128)(2,1)} %bitcast.1), calls=%async_computation | async-start | bytes 1441792 | tf_op jit(solution)/shard_map/all_to_all | solution.py:388
  53.5 19.9 %collective-permute-start.11 = (bf16[640,1280]{1,0:T(8,128)(2,1)}, bf16[640,1280]{1,0:T(8,128)(2,1)}, u32[]{:S(2)}, u32[]{:S(2)}) collective-permute-start(bf16[640,1280]{1,0:T(8,128)(2,1)} %get-tuple-element.39.refs_2_), channel_id=1, source_target_pairs={{0,8},{8,0},{16,24},{24,16},{1,9},{9,1},{17,25},{25,17},{2,10},{10... | collective-permute-start | bytes 4915208 | tf_op jit(solution)/shard_map/ppermute | solution.py:64
  57.8 15.6 %collective-permute-start.12 = (bf16[640,1280]{1,0:T(8,128)(2,1)S(1)}, bf16[640,1280]{1,0:T(8,128)(2,1)}, u32[]{:S(2)}, u32[]{:S(2)}) collective-permute-start(bf16[640,1280]{1,0:T(8,128)(2,1)S(1)} %get-tuple-element.42.refs_3_), channel_id=1, source_target_pairs={{0,8},{8,0},{16,24},{24,16},{1,9},{9,1},{17,25},{25,17},{2,10},{10... | collective-permute-start | bytes 4915208 | tf_op jit(solution)/shard_map/ppermute | solution.py:64
  57.9 22.5 %collective-permute-start.14 = (bf16[320,1280]{1,0:T(8,128)(2,1)}, bf16[320,1280]{1,0:T(8,128)(2,1)S(1)}, u32[]{:S(2)}, u32[]{:S(2)}) collective-permute-start(bf16[320,1280]{1,0:T(8,128)(2,1)} %get-tuple-element.44), channel_id=1, source_target_pairs={{0,2},{1,3},{2,0},{3,1},{4,6},{5,7},{6,4},{7,5},{8,9},{9,8},{10,11... | collective-permute-start | bytes 2457608 | tf_op jit(solution)/shard_map/ppermute | solution.py:70
  60.5 19.9 %collective-permute-start.13 = (bf16[320,1280]{1,0:T(8,128)(2,1)S(1)}, bf16[320,1280]{1,0:T(8,128)(2,1)}, u32[]{:S(2)}, u32[]{:S(2)}) collective-permute-start(bf16[320,1280]{1,0:T(8,128)(2,1)S(1)} %get-tuple-element.43.refs_6_.up_ref), channel_id=1, source_target_pairs={{0,8},{8,0},{16,24},{24,16},{1,9},{9,1},{17,25},{25,17},{2,10},{10... | collective-permute-start | bytes 2457608 | tf_op jit(solution)/shard_map/ppermute | solution.py:64
  80.4 4.7 %copy-start.9 = (bf16[128,1280]{1,0:T(8,128)(2,1)S(1)}, bf16[128,1280]{1,0:T(8,128)(2,1)}, u32[]{:S(2)}) copy-start(bf16[128,1280]{1,0:T(8,128)(2,1)} %embed_ref.1) | copy-start | bytes 983044
  80.4 2.4 %collective-permute-start.15 = (bf16[320,1280]{1,0:T(8,128)(2,1)S(1)}, bf16[320,1280]{1,0:T(8,128)(2,1)S(1)}, u32[]{:S(2)}, u32[]{:S(2)}) collective-permute-start(bf16[320,1280]{1,0:T(8,128)(2,1)S(1)} %after.5.refs_8_.down_ref), channel_id=1, source_target_pairs={{0,8},{8,0},{16,24},{24,16},{1,9},{9,1},{17,25},{25,17},{2,10},{10... | collective-permute-start | bytes 2457608 | tf_op jit(solution)/shard_map/ppermute | solution.py:64
  85.0 16.8 %collective-permute-start.16 = (bf16[128,1280]{1,0:T(8,128)(2,1)S(1)}, bf16[128,1280]{1,0:T(8,128)(2,1)S(1)}, u32[]{:S(2)}, u32[]{:S(2)}) collective-permute-start(bf16[128,1280]{1,0:T(8,128)(2,1)S(1)} %text_theirs_last.1), channel_id=1, source_target_pairs={{0,4},{1,5},{2,6},{3,7},{4,0},{5,1},{6,2},{7,3},{8,12},{9,13},{10,... | collective-permute-start | bytes 983048 | tf_op jit(solution)/shard_map/ppermute | solution.py:64
  (8 other events, 12.1 us)

commit v4 on v3

--- a/solution.py
+++ b/solution.py
@@ -158,6 +158,18 @@
     token_ref[...] = jnp.zeros_like(token_ref)
 
 
+def pass_quarter(place_ref, ref, out_ref, sems):
+    quarter = out_ref.shape[0]
+    first = pl.multiple_of((2 * place_ref[0] + place_ref[1]) * quarter, quarter)
+    return start_copies([(ref.at[pl.ds(first, quarter)], out_ref)], sems)
+
+
+def order_kernel(place_ref, mine_ref, other_ref, out_ref):
+    quarter = mine_ref.shape[0]
+    for chip in range(2):
+        out_ref[pl.ds(chip * quarter, quarter), :] = jnp.where(place_ref[1] == chip, mine_ref[...], other_ref[...])
+
+
 def pass_on(core_ref, ref, out_ref, sem):
     half = out_ref.shape[0]
     first = pl.multiple_of(core_ref[0] * half, half)
@@ -173,7 +185,7 @@
 def second_kernel(core_ref, rows_ref, ua, ba, da, ub, bb, db, before_ref, *refs):
     if len(refs) > 2:
         side_ref, embed_ref, _, half_ref, embed_out_ref, out_ref, token_ref, sems = refs
-        copies = pass_on(core_ref, side_ref, half_ref, sems)
+        copies = pass_quarter(core_ref, side_ref, half_ref, sems)
         embed_out_ref[...] = embed_ref[...]
     else:
         out_ref, token_ref = refs
@@ -315,6 +327,7 @@
     where = jnp.broadcast_to(where.astype(BF16), (where.shape[0], 128))
 
     core = (lax.axis_index("seq") % 2).reshape(1)
+    core_and_x = jnp.stack([lax.axis_index("seq") % 2, lax.axis_index("seq") // 2 % 2])
     half_rows = jax.ShapeDtypeStruct((patch_count // 2, width), BF16)
     far_up, far_down = swap(vis_up, "seq", 1), swap(vis_down, "seq", 1)
     other_bias = swap(after(vis_bias, far_up), "seq", 1)
@@ -336,18 +349,19 @@
     if paired:
         side_up, side_down = swap_by_core(text_up, (1, 2)), swap_by_core(text_down, (1, 2))
     part_first, first_done, far_up, far_down = call(
-        first_kernel, "vision_first", outs, args, stored=(4, 6), copies=2, megabytes=36
+        first_kernel, "vision_first", outs, args, stored=(4, 6), copies=2, megabytes=38
     )
     weights = (near_up, vis_bias, near_down, far_up, other_bias, far_down)
     back_first = swap(part_first, "seq", 2)
-    args = (core, far_second, *weights, first_done)
+    args = (core_and_x, far_second, *weights, first_done)
     outs = (half_rows, TOKEN)
     half_slice = jax.ShapeDtypeStruct((text_up.shape[0] // 2, width), BF16)
+    quarter_slice = jax.ShapeDtypeStruct((text_up.shape[0] // 4, width), BF16)
     if paired:
         side_up, across_up, other_embed, part_second, second_done = call(
             second_kernel,
             "vision_second",
-            (like(side_up), half_slice, like(text_embed), *outs),
+            (like(side_up), quarter_slice, like(text_embed), *outs),
             args + (side_up, text_embed),
             aliases={len(args): 0},
             copies=1,
@@ -366,28 +380,45 @@
         (own_rows, like(merge_proj)),
         (first, second, *weights, second_done, back_first, merge_proj),
         stored=(10,),
-        microseconds=5,
+        microseconds=10,
         copies=1,
     )
     sent_rows = jax.ShapeDtypeStruct((place.shape[0], width + 128), BF16)
     args = (patches, own, back_second, merge_gain, merge_proj, place, where)
     send = call(merge_kernel, "merge_rows", sent_rows, args)
     if paired:
-        side_down, across_up, across_down = call(
+        side_down, across_down = call(
             pass_kernel,
             "pass_down",
-            (like(side_down), like(across_up), half_slice),
-            (core, side_down, send, across_up, other_embed),
-            aliases={1: 0, 3: 1},
+            (like(side_down), half_slice),
+            (core, side_down, send),
+            aliases={1: 0},
             scalars=1,
-            stored=(2, 3, 4),
+            stored=(2,),
             copies=1,
+            microseconds=0.001,
+        )
+        other_embed, across_up = call(
+            same_kernel,
+            "gate",
+            (like(other_embed), like(across_up)),
+            (other_embed, across_up, send),
+            aliases={0: 0, 1: 1},
+            stored=(2,),
+            microseconds=9,
+        )
+        across_up = call(
+            order_kernel,
+            "order_across",
+            half_slice,
+            (core_and_x, across_up, swap(across_up, "seq", 2)),
+            scalars=1,
             microseconds=0.001,
         )
         other_down, across_down = swap(side_down, "seq", 1), swap_by_core(across_down, (2, 1))
     got = lax.all_to_all(send, "blk", split_axis=0, concat_axis=0, tiled=True)
     if paired:
-        got = after(got, send, microseconds=5)
+        got = after(got, send, microseconds=6)
         slices = (text_up, text_down, side_up, side_down, other_up, other_down)
         room = (
             pltpu.VMEM(text_embed.shape, BF16),

time: 103 us -> 99.6 us (0.967)
  waiting for transfers between devices: 30.1 us -> 25.5 us
  starting transfers between devices: 20.9 us -> 22.5 us
    all_to_all x1, waiting for transfers between devices: 12.8 us -> 3.13 us  [per_device(): got = lax.all_to_all(send, 'blk', split_axis=0, concat_axis=0, tiled=True)]
    ppermute x13 -> x14, waiting for transfers between devices: 17.2 us -> 22.3 us  [swap(): return lax.ppermute(x, axis, [(i, i ^ bit) for i in range(size)])]
    ppermute x13 -> x14, starting transfers between devices: 7.71 us -> 10.5 us  [swap(): return lax.ppermute(x, axis, [(i, i ^ bit) for i in range(size)])]
    ppermute x4, starting transfers between devices: 8.85 us -> 6.92 us  [swap_by_core(): return lax.ppermute(x, ('seq', 'blk'), pairs)]
    pallas_call x13 -> x15, Pallas kernels: 40.2 us -> 39.8 us  [call(): pl.pallas_call(kernel, out_shape=out_shape, in_specs=specs, out_specs=tup...]
    unnamed x29 -> x31, local copies, waits for them, and re-layouts: 8.83 us -> 8.59 us
  transfers between devices with their start and end apart: 18 -> 19, of which waited for: 5 -> 5; matrix products, arithmetic and copies ran while one was open for 2% -> 2% of each run, Pallas kernels for 37% -> 38%
where the time goes in v4:
time: 99.6 us; the launch traced here: 99 us
  Pallas kernels  39.8 us (40%)
  waiting for transfers between devices  25.5 us (26%)
  starting transfers between devices  22.5 us (23%)
  local copies, waits for them, and re-layouts  8.69 us (9%)
  other arithmetic  2.26 us (2%)
    pallas_call x15, Pallas kernels, call(): pl.pallas_call(kernel, out_shape=out_shape, in_specs=specs, out_specs=tup...  39.8 us
    ppermute x14, waiting for transfers between devices, swap(): return lax.ppermute(x, axis, [(i, i ^ bit) for i in range(size)])  22.3 us
    ppermute x14, starting transfers between devices, swap(): return lax.ppermute(x, axis, [(i, i ^ bit) for i in range(size)])  10.5 us
    unnamed x31, local copies, waits for them, and re-layouts  8.59 us
    ppermute x4, starting transfers between devices, swap_by_core(): return lax.ppermute(x, ('seq', 'blk'), pairs)  6.92 us
    all_to_all x1, starting transfers between devices, per_device(): got = lax.all_to_all(send, 'blk', split_axis=0, concat_axis=0, tiled=True)  5.04 us
    all_to_all x1, waiting for transfers between devices, per_device(): got = lax.all_to_all(send, 'blk', split_axis=0, concat_axis=0, tiled=True)  3.13 us
  transfers between devices with their start and end apart: 19, of which 5 were waited for; matrix products, arithmetic and copies ran while one was open for 2% of the time, Pallas kernels for 38%

profile of v4, /device:TPU:0, one launch (start us, length us, event | category | flops | bytes accessed | tf_op | source)
XLA Modules:
  0.0 99.0 jit_solution(15258496131057243044)
XLA Ops:
  0.5 3.0 %collective-permute-start.5 = (bf16[640,1280]{1,0:T(8,128)(2,1)}, bf16[640,1280]{1,0:T(8,128)(2,1)}, u32[]{:S(2)}, u32[]{:S(2)}) collective-permute-start(bf16[640,1280]{1,0:T(8,128)(2,1)} %refs_0_.4), channel_id=1, source_target_pairs={{0,1},{1,0},{2,3},{3,2},{4,5},{5,4},{6,7},{7,6},{8,10},{9,11},{10,... | collective-permute-start | bytes 4915208 | tf_op jit(solution)/shard_map/ppermute | solution.py:70
  5.3 1.4 %norm_patches.1 = (bf16[128,1280]{1,0:T(8,128)(2,1)}, bf16[128,1280]{1,0:T(8,128)(2,1)}, f32[8,128]{1,0:T(8,128)S(1)}) custom-call(bf16[256,1280]{1,0:T(8,128)(2,1)S(1)} %copy-done.3, f32[1280]{0:T(1024)S(1)} %copy-done.14), custom_call_target="tpu_custom_call" | custom-call | flops 1000000 | bytes 1000 | tf_op jit(solution)/shard_map/norm_patches/pallas_call | solution.py:32
  6.7 1.5 %collective-permute-start = (bf16[128,1280]{1,0:T(8,128)(2,1)}, bf16[128,1280]{1,0:T(8,128)(2,1)}, u32[]{:S(2)}, u32[]{:S(2)}) collective-permute-start(bf16[128,1280]{1,0:T(8,128)(2,1)} %get-tuple-element.27.first_ref), channel_id=1, source_target_pairs={{0,16},{8,24},{16,0},{24,8},{1,17},{9,25},{17,1},{25,9},{2,18},{10... | collective-permute-start | bytes 983048 | tf_op jit(solution)/shard_map/ppermute | solution.py:64
  11.1 2.1 %copy-done.2 = bf16[1280,1280]{1,0:T(8,128)(2,1)S(1)} copy-done((bf16[1280,1280]{1,0:T(8,128)(2,1)S(1)}, bf16[1280,1280]{1,0:T(8,128)(2,1)}, u32[]{:S(2)}) %copy-start.2) | copy-done | bytes 3276824
  13.2 2.3 %bring_vision.1 = (bf16[1280,1280]{1,0:T(8,128)(2,1)S(1)}, bf16[1280,1280]{1,0:T(8,128)(2,1)S(1)}) custom-call(bf16[1280,1280]{1,0:T(8,128)(2,1)S(1)} %copy-done.2, bf16[1280,1280]{1,0:T(8,128)(2,1)} %da.1, f32[8,128]{1,0:T(8,128)S(1)} %get-tuple-element.29.before_ref), custom_call_target="tpu_custom_call" | custom-call | flops 1000000 | bytes 1000 | tf_op jit(solution)/shard_map/bring_vision/pallas_call | solution.py:32
  15.5 2.1 %collective-permute-done.rows_ref = bf16[128,1280]{1,0:T(8,128)(2,1)} collective-permute-done((bf16[128,1280]{1,0:T(8,128)(2,1)}, bf16[128,1280]{1,0:T(8,128)(2,1)}, u32[]{:S(2)}, u32[]{:S(2)}) %collective-permute-start) | collective-permute-done | bytes 327712 | tf_op jit(solution)/shard_map/ppermute | solution.py:64
  17.7 5.5 %vision_first.1 = (bf16[128,1280]{1,0:T(8,128)(2,1)S(1)}, f32[8,128]{1,0:T(8,128)S(1)}, bf16[1280,1280]{1,0:T(8,128)(2,1)S(1)}, bf16[1280,1280]{1,0:T(8,128)(2,1)S(1)}) custom-call(bf16[128,1280]{1,0:T(8,128)(2,1)} %collective-permute-done.rows_ref, bf16[1280,1280]{1,0:T(8,128)(2,1)S(1)} %get-tuple-element.30.ua, f32[1280]{0:T(1024)S(1)} %copy-done.12, ...), custom_call_target="tpu_custom_call" | custom-call | flops 1000000 | bytes 1000 | tf_op jit(solution)/shard_map/vision_first/pallas_call | solution.py:32
  23.1 2.0 %collective-permute-start.6 = (bf16[128,1280]{1,0:T(8,128)(2,1)S(1)}, bf16[128,1280]{1,0:T(8,128)(2,1)S(1)}, u32[]{:S(2)}, u32[]{:S(2)}) collective-permute-start(bf16[128,1280]{1,0:T(8,128)(2,1)S(1)} %get-tuple-element.36), channel_id=1, source_target_pairs={{0,16},{8,24},{16,0},{24,8},{1,17},{9,25},{17,1},{25,9},{2,18},{10... | collective-permute-start | bytes 983048 | tf_op jit(solution)/shard_map/ppermute | solution.py:64
  25.2 4.1 %vision_second.1 = (bf16[640,1280]{1,0:T(8,128)(2,1)}, bf16[160,1280]{1,0:T(8,128)(2,1)S(1)}, bf16[128,1280]{1,0:T(8,128)(2,1)S(1)}, bf16[128,1280]{1,0:T(8,128)(2,1)S(1)}, f32[8,128]{1,0:T(8,128)S(1)}) custom-call(s32[2]{0:T(128)S(1)} %pad_add_fusion.core_ref.place_ref, ...), custom_call_target="tpu_custom_call", output_to_operand_aliasing={{0}: (9, {})} | custom-call | flops 30000001024 | bytes 1000 | tf_op jit(solution)/shard_map/vision_second/pallas_call | solution.py:32
  29.4 2.1 %collective-permute-start.12 = (bf16[160,1280]{1,0:T(8,128)(2,1)S(1)}, bf16[160,1280]{1,0:T(8,128)(2,1)S(1)}, u32[]{:S(2)}, u32[]{:S(2)}) collective-permute-start(bf16[160,1280]{1,0:T(8,128)(2,1)S(1)} %get-tuple-element.43), channel_id=1, source_target_pairs={{0,2},{1,3},{2,0},{3,1},{4,6},{5,7},{6,4},{7,5},{8,9},{9,8},{10,11... | collective-permute-start | bytes 1228808 | tf_op jit(solution)/shard_map/ppermute | solution.py:70
  31.5 2.6 %collective-permute-start.11 = (bf16[128,1280]{1,0:T(8,128)(2,1)S(1)}, bf16[128,1280]{1,0:T(8,128)(2,1)S(1)}, u32[]{:S(2)}, u32[]{:S(2)}) collective-permute-start(bf16[128,1280]{1,0:T(8,128)(2,1)S(1)} %get-tuple-element.42), channel_id=1, source_target_pairs={{0,4},{1,5},{2,6},{3,7},{4,0},{5,1},{6,2},{7,3},{8,12},{9,13},{10,... | collective-permute-start | bytes 983048 | tf_op jit(solution)/shard_map/ppermute | solution.py:64
  34.1 5.9 %vision_own.1 = (f32[256,1280]{1,0:T(8,128)S(1)}, bf16[5120,1280]{1,0:T(8,128)(2,1)S(1)}) custom-call(bf16[128,1280]{1,0:T(8,128)(2,1)} %get-tuple-element.27.first_ref, bf16[128,1280]{1,0:T(8,128)(2,1)} %get-tuple-element.28.second_ref, bf16[1280,1280]{1,0:T(8,128)(2,1)S(1)} %get-tuple-element.30.ua, f32[1280]{0:T(1024)S(1)} %copy-done.12, ...), custom_call_target="tpu_custom_call" | custom-call | flops 10000000000 | bytes 1000 | tf_op jit(solution)/shard_map/vision_own/pallas_call | solution.py:32
  40.1 4.6 %merge_rows.1.refs_1_.refs_0_.refs_2_ = bf16[256,1408]{1,0:T(8,128)(2,1)} custom-call(bf16[256,1280]{1,0:T(8,128)(2,1)S(1)} %copy-done.4, f32[256,1280]{1,0:T(8,128)S(1)} %get-tuple-element.37.own_ref, bf16[128,1280]{1,0:T(8,128)(2,1)S(1)} %collective-permute-done.7.back_ref, f32[1280]{0:T(1024)S(1)} %copy-done.13, ...), custom_call_target="tpu_custom_call" | custom-call | flops 1000000 | bytes 1000 | tf_op jit(solution)/shard_map/merge_rows/pallas_call | solution.py:32
  44.7 5.0 %all-to-all-start = ((bf16[8,32,1408]{2,1,0:T(8,128)(2,1)}), bf16[8,32,1408]{2,1,0:T(8,128)(2,1)}, u32[]{:S(2)}, u32[]{:S(2)}) async-start(bf16[8,32,1408]{2,1,0:T(8,128)(2,1)} %bitcast.2), calls=%async_computation | async-start | bytes 1441792 | tf_op jit(solution)/shard_map/all_to_all | solution.py:419
  52.7 1.7 %collective-permute-start.13 = (bf16[160,1280]{1,0:T(8,128)(2,1)S(1)}, bf16[160,1280]{1,0:T(8,128)(2,1)S(1)}, u32[]{:S(2)}, u32[]{:S(2)}) collective-permute-start(bf16[160,1280]{1,0:T(8,128)(2,1)S(1)} %get-tuple-element.44.mine_ref), channel_id=1, source_target_pairs={{0,16},{8,24},{16,0},{24,8},{1,17},{9,25},{17,1},{25,9},{2,18},{10... | collective-permute-start | bytes 1228808 | tf_op jit(solution)/shard_map/ppermute | solution.py:64
  55.2 1.9 %collective-permute-start.15 = (bf16[320,1280]{1,0:T(8,128)(2,1)}, bf16[320,1280]{1,0:T(8,128)(2,1)S(1)}, u32[]{:S(2)}, u32[]{:S(2)}) collective-permute-start(bf16[320,1280]{1,0:T(8,128)(2,1)} %get-tuple-element.45), channel_id=1, source_target_pairs={{0,2},{1,3},{2,0},{3,1},{4,6},{5,7},{6,4},{7,5},{8,9},{9,8},{10,11... | collective-permute-start | bytes 2457608 | tf_op jit(solution)/shard_map/ppermute | solution.py:70
  57.0 7.1 %collective-permute-done.13.other_ref = bf16[160,1280]{1,0:T(8,128)(2,1)S(1)} collective-permute-done((bf16[160,1280]{1,0:T(8,128)(2,1)S(1)}, bf16[160,1280]{1,0:T(8,128)(2,1)S(1)}, u32[]{:S(2)}, u32[]{:S(2)}) %collective-permute-start.13) | collective-permute-done | bytes 409632 | tf_op jit(solution)/shard_map/ppermute | solution.py:64
  65.8 3.1 %all-to-all-done = bf16[8,32,1408]{2,1,0:T(8,128)(2,1)} async-done(((bf16[8,32,1408]{2,1,0:T(8,128)(2,1)}), bf16[8,32,1408]{2,1,0:T(8,128)(2,1)}, u32[]{:S(2)}, u32[]{:S(2)}) %all-to-all-start) | async-done | bytes 720928 | tf_op jit(solution)/shard_map/all_to_all | solution.py:419
  69.0 1.4 %copy-done.1 = bf16[640,1280]{1,0:T(8,128)(2,1)S(1)} copy-done((bf16[640,1280]{1,0:T(8,128)(2,1)S(1)}, bf16[640,1280]{1,0:T(8,128)(2,1)}, u32[]{:S(2)}) %copy-start.1) | copy-done | bytes 1638424
  70.4 5.5 %text_theirs.1 = (bf16[128,1280]{1,0:T(8,128)(2,1)S(1)}, f32[128,1280]{1,0:T(8,128)S(1)}) custom-call(bf16[128,1280]{1,0:T(8,128)(2,1)S(1)} %copy-done.8, bf16[256,1408]{1,0:T(8,128)(2,1)} %after.4.got_ref, bf16[640,1280]{1,0:T(8,128)(2,1)S(1)} %copy-done.1, bf16[640,1280]{1,0:T(8,128)(2,1)} %refs_1_.5, bf16[640,1280]{1,0:T(8,128)(2,1)} %get-tuple-element.40.refs_2_, ...), custom_call_target="tpu_custom_call" | custom-call | flops 1000000 | bytes 1000 | tf_op jit(solution)/shard_map/text_theirs/pallas_call | solution.py:32
  76.1 2.3 %collective-permute-done.16.refs_9_.other_down_ref = bf16[320,1280]{1,0:T(8,128)(2,1)S(1)} collective-permute-done((bf16[320,1280]{1,0:T(8,128)(2,1)S(1)}, bf16[320,1280]{1,0:T(8,128)(2,1)S(1)}, u32[]{:S(2)}, u32[]{:S(2)}) %collective-permute-start.16) | collective-permute-done | bytes 819232 | tf_op jit(solution)/shard_map/ppermute | solution.py:64
  78.4 2.2 %text_theirs_last.1 = bf16[128,1280]{1,0:T(8,128)(2,1)S(1)} custom-call(bf16[128,1280]{1,0:T(8,128)(2,1)S(1)} %get-tuple-element.47.refs_1_.normed_ref, f32[128,1280]{1,0:T(8,128)S(1)} %get-tuple-element.48.total_ref, bf16[320,1280]{1,0:T(8,128)(2,1)S(1)} %order_across.1.refs_6_.up_ref, bf16[320,1280]{1,0:T(8,128)(2,1)} %collective-permute-done.14.refs_7_.other_up_ref, ...), custom_call_target="tpu_custom_call" | custom-call | flops 1000000 | bytes 1000 | tf_op jit(solution)/shard_map/text_theirs_last/pallas_call | solution.py:32
  80.7 6.7 %text_mine.1 = f32[128,1280]{1,0:T(8,128)S(1)} custom-call(bf16[128,1280]{1,0:T(8,128)(2,1)S(1)} %copy-done.10, bf16[256,1408]{1,0:T(8,128)(2,1)} %after.4.got_ref, bf16[640,1280]{1,0:T(8,128)(2,1)S(1)} %copy-done.1, bf16[640,1280]{1,0:T(8,128)(2,1)} %refs_1_.5, bf16[640,1280]{1,0:T(8,128)(2,1)} %get-tuple-element.40.refs_2_, ...), custom_call_target="tpu_custom_call" | custom-call | flops 1000000 | bytes 1000 | tf_op jit(solution)/shard_map/text_mine/pallas_call | solution.py:32
  87.4 10.8 %collective-permute-done.17 = bf16[128,1280]{1,0:T(8,128)(2,1)S(1)} collective-permute-done((bf16[128,1280]{1,0:T(8,128)(2,1)S(1)}, bf16[128,1280]{1,0:T(8,128)(2,1)S(1)}, u32[]{:S(2)}, u32[]{:S(2)}) %collective-permute-start.17) | collective-permute-done | bytes 327712 | tf_op jit(solution)/shard_map/ppermute | solution.py:64
  (71 shorter events, 11.8 us)
Async XLA Ops:
  0.0 10.9 %collective-permute-start.1 = (bf16[1280,1280]{1,0:T(8,128)(2,1)}, bf16[1280,1280]{1,0:T(8,128)(2,1)S(1)}, u32[]{:S(2)}, u32[]{:S(2)}) collective-permute-start(bf16[1280,1280]{1,0:T(8,128)(2,1)} %ua.1), channel_id=1, source_target_pairs={{0,8},{8,0},{16,24},{24,16},{1,9},{9,1},{17,25},{25,17},{2,10},{10... | collective-permute-start | bytes 9830408 | tf_op jit(solution)/shard_map/ppermute | solution.py:64
  0.5 17.2 %collective-permute-start.3 = (bf16[1280,1280]{1,0:T(8,128)(2,1)}, bf16[1280,1280]{1,0:T(8,128)(2,1)}, u32[]{:S(2)}, u32[]{:S(2)}) collective-permute-start(bf16[1280,1280]{1,0:T(8,128)(2,1)} %da.1), channel_id=1, source_target_pairs={{0,8},{8,0},{16,24},{24,16},{1,9},{9,1},{17,25},{25,17},{2,10},{10... | collective-permute-start | bytes 9830408 | tf_op jit(solution)/shard_map/ppermute | solution.py:64
  0.5 24.7 %collective-permute-start.5 = (bf16[640,1280]{1,0:T(8,128)(2,1)}, bf16[640,1280]{1,0:T(8,128)(2,1)}, u32[]{:S(2)}, u32[]{:S(2)}) collective-permute-start(bf16[640,1280]{1,0:T(8,128)(2,1)} %refs_0_.4), channel_id=1, source_target_pairs={{0,1},{1,0},{2,3},{3,2},{4,5},{5,4},{6,7},{7,6},{8,10},{9,11},{10,... | collective-permute-start | bytes 4915208 | tf_op jit(solution)/shard_map/ppermute | solution.py:70
  6.7 10.9 %collective-permute-start = (bf16[128,1280]{1,0:T(8,128)(2,1)}, bf16[128,1280]{1,0:T(8,128)(2,1)}, u32[]{:S(2)}, u32[]{:S(2)}) collective-permute-start(bf16[128,1280]{1,0:T(8,128)(2,1)} %get-tuple-element.27.first_ref), channel_id=1, source_target_pairs={{0,16},{8,24},{16,0},{24,8},{1,17},{9,25},{17,1},{25,9},{2,18},{10... | collective-permute-start | bytes 983048 | tf_op jit(solution)/shard_map/ppermute | solution.py:64
  8.2 17.0 %collective-permute-start.4 = (bf16[128,1280]{1,0:T(8,128)(2,1)}, bf16[128,1280]{1,0:T(8,128)(2,1)}, u32[]{:S(2)}, u32[]{:S(2)}) collective-permute-start(bf16[128,1280]{1,0:T(8,128)(2,1)} %get-tuple-element.28.second_ref), channel_id=1, source_target_pairs={{0,16},{8,24},{16,0},{24,8},{1,17},{9,25},{17,1},{25,9},{2,18},{10... | collective-permute-start | bytes 983048 | tf_op jit(solution)/shard_map/ppermute | solution.py:64
  10.9 4.7 %copy-start = (bf16[1280,1280]{1,0:T(8,128)(2,1)}, bf16[1280,1280]{1,0:T(8,128)(2,1)S(1)}, u32[]{:S(2)}) copy-start(bf16[1280,1280]{1,0:T(8,128)(2,1)S(1)} %collective-permute-done.1.refs_1_.ub) | copy-start | bytes 9830404
  10.9 6.8 %collective-permute-start.2 = (f32[1280]{0:T(1024)S(1)}, f32[1280]{0:T(1024)S(1)}, u32[]{:S(2)}, u32[]{:S(2)}) collective-permute-start(f32[1280]{0:T(1024)S(1)} %after.3), channel_id=1, source_target_pairs={{0,8},{8,0},{16,24},{24,16},{1,9},{9,1},{17,25},{25,17},{2,10},{10... | collective-permute-start | bytes 15368 | tf_op jit(solution)/shard_map/ppermute | solution.py:64
  17.6 32.1 %collective-permute-start.8 = (bf16[640,1280]{1,0:T(8,128)(2,1)}, bf16[640,1280]{1,0:T(8,128)(2,1)S(1)}, u32[]{:S(2)}, u32[]{:S(2)}) collective-permute-start(bf16[640,1280]{1,0:T(8,128)(2,1)} %refs_1_.5), channel_id=1, source_target_pairs={{0,1},{1,0},{2,3},{3,2},{4,5},{5,4},{6,7},{7,6},{8,10},{9,11},{10,... | collective-permute-start | bytes 4915208 | tf_op jit(solution)/shard_map/ppermute | solution.py:70
  17.7 7.5 %copy-start.9 = (bf16[128,1280]{1,0:T(8,128)(2,1)S(1)}, bf16[128,1280]{1,0:T(8,128)(2,1)}, u32[]{:S(2)}) copy-start(bf16[128,1280]{1,0:T(8,128)(2,1)} %embed_ref.1) | copy-start | bytes 983044
  23.1 10.9 %collective-permute-start.6 = (bf16[128,1280]{1,0:T(8,128)(2,1)S(1)}, bf16[128,1280]{1,0:T(8,128)(2,1)S(1)}, u32[]{:S(2)}, u32[]{:S(2)}) collective-permute-start(bf16[128,1280]{1,0:T(8,128)(2,1)S(1)} %get-tuple-element.36), channel_id=1, source_target_pairs={{0,16},{8,24},{16,0},{24,8},{1,17},{9,25},{17,1},{25,9},{2,18},{10... | collective-permute-start | bytes 983048 | tf_op jit(solution)/shard_map/ppermute | solution.py:64
  29.3 10.7 %collective-permute-start.7 = (bf16[128,1280]{1,0:T(8,128)(2,1)S(1)}, bf16[128,1280]{1,0:T(8,128)(2,1)S(1)}, u32[]{:S(2)}, u32[]{:S(2)}) collective-permute-start(bf16[128,1280]{1,0:T(8,128)(2,1)S(1)} %get-tuple-element.38), channel_id=1, source_target_pairs={{0,16},{8,24},{16,0},{24,8},{1,17},{9,25},{17,1},{25,9},{2,18},{10... | collective-permute-start | bytes 983048 | tf_op jit(solution)/shard_map/ppermute | solution.py:64
  29.4 22.6 %collective-permute-start.12 = (bf16[160,1280]{1,0:T(8,128)(2,1)S(1)}, bf16[160,1280]{1,0:T(8,128)(2,1)S(1)}, u32[]{:S(2)}, u32[]{:S(2)}) collective-permute-start(bf16[160,1280]{1,0:T(8,128)(2,1)S(1)} %get-tuple-element.43), channel_id=1, source_target_pairs={{0,2},{1,3},{2,0},{3,1},{4,6},{5,7},{6,4},{7,5},{8,9},{9,8},{10,11... | collective-permute-start | bytes 1228808 | tf_op jit(solution)/shard_map/ppermute | solution.py:70
  31.5 20.5 %collective-permute-start.11 = (bf16[128,1280]{1,0:T(8,128)(2,1)S(1)}, bf16[128,1280]{1,0:T(8,128)(2,1)S(1)}, u32[]{:S(2)}, u32[]{:S(2)}) collective-permute-start(bf16[128,1280]{1,0:T(8,128)(2,1)S(1)} %get-tuple-element.42), channel_id=1, source_target_pairs={{0,4},{1,5},{2,6},{3,7},{4,0},{5,1},{6,2},{7,3},{8,12},{9,13},{10,... | collective-permute-start | bytes 983048 | tf_op jit(solution)/shard_map/ppermute | solution.py:64
  34.1 6.0 %copy-start.4 = (bf16[256,1280]{1,0:T(8,128)(2,1)S(1)}, bf16[256,1280]{1,0:T(8,128)(2,1)}, u32[]{:S(2)}) copy-start(bf16[256,1280]{1,0:T(8,128)(2,1)} %patches_ref.3) | copy-start | bytes 1966084
  34.1 6.0 %copy-start.13 = (f32[1280]{0:T(1024)S(1)}, f32[1280]{0:T(1024)}, u32[]{:S(2)}) copy-start(f32[1280]{0:T(1024)} %gain_ref.3) | copy-start | bytes 15364
  44.7 24.3 %all-to-all-start = ((bf16[8,32,1408]{2,1,0:T(8,128)(2,1)}), bf16[8,32,1408]{2,1,0:T(8,128)(2,1)}, u32[]{:S(2)}, u32[]{:S(2)}) async-start(bf16[8,32,1408]{2,1,0:T(8,128)(2,1)} %bitcast.2), calls=%async_computation | async-start | bytes 1441792 | tf_op jit(solution)/shard_map/all_to_all | solution.py:419
  49.7 19.3 %collective-permute-start.9 = (bf16[640,1280]{1,0:T(8,128)(2,1)}, bf16[640,1280]{1,0:T(8,128)(2,1)}, u32[]{:S(2)}, u32[]{:S(2)}) collective-permute-start(bf16[640,1280]{1,0:T(8,128)(2,1)} %get-tuple-element.40.refs_2_), channel_id=1, source_target_pairs={{0,8},{8,0},{16,24},{24,16},{1,9},{9,1},{17,25},{25,17},{2,10},{10... | collective-permute-start | bytes 4915208 | tf_op jit(solution)/shard_map/ppermute | solution.py:64
  50.7 18.3 %collective-permute-start.10 = (bf16[640,1280]{1,0:T(8,128)(2,1)S(1)}, bf16[640,1280]{1,0:T(8,128)(2,1)}, u32[]{:S(2)}, u32[]{:S(2)}) collective-permute-start(bf16[640,1280]{1,0:T(8,128)(2,1)S(1)} %get-tuple-element.41.refs_3_), channel_id=1, source_target_pairs={{0,8},{8,0},{16,24},{24,16},{1,9},{9,1},{17,25},{25,17},{2,10},{10... | collective-permute-start | bytes 4915208 | tf_op jit(solution)/shard_map/ppermute | solution.py:64
  52.7 11.4 %collective-permute-start.13 = (bf16[160,1280]{1,0:T(8,128)(2,1)S(1)}, bf16[160,1280]{1,0:T(8,128)(2,1)S(1)}, u32[]{:S(2)}, u32[]{:S(2)}) collective-permute-start(bf16[160,1280]{1,0:T(8,128)(2,1)S(1)} %get-tuple-element.44.mine_ref), channel_id=1, source_target_pairs={{0,16},{8,24},{16,0},{24,8},{1,17},{9,25},{17,1},{25,9},{2,18},{10... | collective-permute-start | bytes 1228808 | tf_op jit(solution)/shard_map/ppermute | solution.py:64
  55.2 20.8 %collective-permute-start.15 = (bf16[320,1280]{1,0:T(8,128)(2,1)}, bf16[320,1280]{1,0:T(8,128)(2,1)S(1)}, u32[]{:S(2)}, u32[]{:S(2)}) collective-permute-start(bf16[320,1280]{1,0:T(8,128)(2,1)} %get-tuple-element.45), channel_id=1, source_target_pairs={{0,2},{1,3},{2,0},{3,1},{4,6},{5,7},{6,4},{7,5},{8,9},{9,8},{10,11... | collective-permute-start | bytes 2457608 | tf_op jit(solution)/shard_map/ppermute | solution.py:70
  65.8 10.3 %collective-permute-start.14 = (bf16[320,1280]{1,0:T(8,128)(2,1)S(1)}, bf16[320,1280]{1,0:T(8,128)(2,1)}, u32[]{:S(2)}, u32[]{:S(2)}) collective-permute-start(bf16[320,1280]{1,0:T(8,128)(2,1)S(1)} %order_across.1.refs_6_.up_ref), channel_id=1, source_target_pairs={{0,8},{8,0},{16,24},{24,16},{1,9},{9,1},{17,25},{25,17},{2,10},{10... | collective-permute-start | bytes 2457608 | tf_op jit(solution)/shard_map/ppermute | solution.py:64
  76.0 4.7 %copy-start.10 = (bf16[128,1280]{1,0:T(8,128)(2,1)S(1)}, bf16[128,1280]{1,0:T(8,128)(2,1)}, u32[]{:S(2)}) copy-start(bf16[128,1280]{1,0:T(8,128)(2,1)} %embed_ref.1) | copy-start | bytes 983044
  76.0 2.4 %collective-permute-start.16 = (bf16[320,1280]{1,0:T(8,128)(2,1)S(1)}, bf16[320,1280]{1,0:T(8,128)(2,1)S(1)}, u32[]{:S(2)}, u32[]{:S(2)}) collective-permute-start(bf16[320,1280]{1,0:T(8,128)(2,1)S(1)} %after.5.refs_8_.down_ref), channel_id=1, source_target_pairs={{0,8},{8,0},{16,24},{24,16},{1,9},{9,1},{17,25},{25,17},{2,10},{10... | collective-permute-start | bytes 2457608 | tf_op jit(solution)/shard_map/ppermute | solution.py:64
  80.6 17.6 %collective-permute-start.17 = (bf16[128,1280]{1,0:T(8,128)(2,1)S(1)}, bf16[128,1280]{1,0:T(8,128)(2,1)S(1)}, u32[]{:S(2)}, u32[]{:S(2)}) collective-permute-start(bf16[128,1280]{1,0:T(8,128)(2,1)S(1)} %text_theirs_last.1), channel_id=1, source_target_pairs={{0,4},{1,5},{2,6},{3,7},{4,0},{5,1},{6,2},{7,3},{8,12},{9,13},{10,... | collective-permute-start | bytes 983048 | tf_op jit(solution)/shard_map/ppermute | solution.py:64
  (10 other events, 16.0 us)

commit v5 on v4

--- a/solution.py
+++ b/solution.py
@@ -245,7 +245,7 @@
     half = up.shape[1] // 2
     pairs = list(zip(rows, rooms))
     waits = []
-    for at in range(3):
+    for at in range(len(slices) // 2):
         for ref, room in ((slices[2 * at], up), (slices[2 * at + 1], down)):
             waits.append([len(pairs)])
             pairs.append((ref, room.at[at]))
@@ -268,13 +268,18 @@
 
 
 def theirs_kernel(capacity, embed_ref, got_ref, *refs):
-    slices, gain_ref, normed_ref, total_ref = refs[:6], refs[6], refs[7], refs[8]
-    embed, got, up, down, sems = refs[9:]
+    slices, gain_ref, normed_ref, total_ref = refs[:4], refs[4], refs[5], refs[6]
+    embed, got, up, down, sems = refs[7:]
     pieces = load_text((embed_ref, got_ref), slices, (), (embed, got), up, down, sems)
     text_rows = place_text_rows(1, capacity, embed[...], got[...])
     normed = normalize(text_rows, gain_ref[...]).astype(BF16)
     normed_ref[...] = normed
     total_ref[...] = feed_forward(normed, pieces)
+
+
+def theirs_more_kernel(normed_ref, total_ref, up_ref, down_ref, out_ref, up, down, sems):
+    pieces = load_text((), (up_ref, down_ref), (), (), up, down, sems)
+    out_ref[...] = total_ref[...] + feed_forward(normed_ref[...], pieces)
 
 
 def theirs_last_kernel(normed_ref, total_ref, up_ref, other_up_ref, down_ref, other_down_ref, out_ref):
@@ -431,11 +436,20 @@
             functools.partial(theirs_kernel, capacity),
             "text_theirs",
             (like(text_embed), sums),
-            (other_embed, got, *slices, text_gain),
-            stored=tuple(range(8)),
-            copies=8,
-            scratch=room,
-            megabytes=24,
+            (other_embed, got, *slices[:4], text_gain),
+            stored=tuple(range(6)),
+            copies=6,
+            scratch=(*room[:2], *(pltpu.VMEM((2, *text_up.shape), BF16) for _ in range(2))),
+            megabytes=52,
+        )
+        total = call(
+            theirs_more_kernel,
+            "text_theirs_more",
+            sums,
+            (text_normed, total, *slices[4:]),
+            stored=(2, 3),
+            copies=2,
+            scratch=tuple(pltpu.VMEM((1, *text_up.shape), BF16) for _ in range(2)),
         )
         across_down = after(across_down, text_normed)
         halves = (across_up, swap(across_up, "seq", 1), across_down, swap(across_down, "seq", 1))

time: 99.6 us -> 98.3 us (0.987)
  waiting for transfers between devices: 25.5 us -> 23.5 us
  local copies, waits for them, and re-layouts: 8.69 us -> 6.74 us
  Pallas kernels: 39.8 us -> 41.7 us
    ppermute x14, waiting for transfers between devices: 22.3 us -> 18.1 us  [swap(): return lax.ppermute(x, axis, [(i, i ^ bit) for i in range(size)])]
    all_to_all x1, waiting for transfers between devices: 3.13 us -> 5.3 us  [per_device(): got = lax.all_to_all(send, 'blk', split_axis=0, concat_axis=0, tiled=True)]
    unnamed x31 -> x35, local copies, waits for them, and re-layouts: 8.59 us -> 6.65 us
    pallas_call x15 -> x16, Pallas kernels: 39.8 us -> 41.7 us  [call(): pl.pallas_call(kernel, out_shape=out_shape, in_specs=specs, out_specs=tup...]
  transfers between devices with their start and end apart: 19 -> 19, of which waited for: 5 -> 4; matrix products, arithmetic and copies ran while one was open for 2% -> 2% of each run, Pallas kernels for 38% -> 40%
where the time goes in v5:
time: 98.3 us; the launch traced here: 97.7 us
  Pallas kernels  41.7 us (42%)
  waiting for transfers between devices  23.5 us (24%)
  starting transfers between devices  23.2 us (24%)
  local copies, waits for them, and re-layouts  6.74 us (7%)
  other arithmetic  2.24 us (2%)
    pallas_call x16, Pallas kernels, call(): pl.pallas_call(kernel, out_shape=out_shape, in_specs=specs, out_specs=tup...  41.7 us
    ppermute x14, waiting for transfers between devices, swap(): return lax.ppermute(x, axis, [(i, i ^ bit) for i in range(size)])  18.1 us
    ppermute x14, starting transfers between devices, swap(): return lax.ppermute(x, axis, [(i, i ^ bit) for i in range(size)])  10.4 us
    ppermute x4, starting transfers between devices, swap_by_core(): return lax.ppermute(x, ('seq', 'blk'), pairs)  7.67 us
    unnamed x35, local copies, waits for them, and re-layouts  6.65 us
    all_to_all x1, waiting for transfers between devices, per_device(): got = lax.all_to_all(send, 'blk', split_axis=0, concat_axis=0, tiled=True)  5.3 us
    all_to_all x1, starting transfers between devices, per_device(): got = lax.all_to_all(send, 'blk', split_axis=0, concat_axis=0, tiled=True)  5.05 us
  transfers between devices with their start and end apart: 19, of which 4 were waited for; matrix products, arithmetic and copies ran while one was open for 2% of the time, Pallas kernels for 40%

profile of v5, /device:TPU:0, one launch (start us, length us, event | category | flops | bytes accessed | tf_op | source)
XLA Modules:
  0.0 97.7 jit_solution(3246131803499928662)
XLA Ops:
  0.5 3.0 %collective-permute-start.5 = (bf16[640,1280]{1,0:T(8,128)(2,1)}, bf16[640,1280]{1,0:T(8,128)(2,1)}, u32[]{:S(2)}, u32[]{:S(2)}) collective-permute-start(bf16[640,1280]{1,0:T(8,128)(2,1)} %refs_0_.4), channel_id=1, source_target_pairs={{0,1},{1,0},{2,3},{3,2},{4,5},{5,4},{6,7},{7,6},{8,10},{9,11},{10,... | collective-permute-start | bytes 4915208 | tf_op jit(solution)/shard_map/ppermute | solution.py:70
  3.5 1.1 %copy-done.5 = bf16[256,1280]{1,0:T(8,128)(2,1)S(1)} copy-done((bf16[256,1280]{1,0:T(8,128)(2,1)S(1)}, bf16[256,1280]{1,0:T(8,128)(2,1)}, u32[]{:S(2)}) %copy-start.5) | copy-done | bytes 655384
  5.3 1.4 %norm_patches.1 = (bf16[128,1280]{1,0:T(8,128)(2,1)}, bf16[128,1280]{1,0:T(8,128)(2,1)}, f32[8,128]{1,0:T(8,128)S(1)}) custom-call(bf16[256,1280]{1,0:T(8,128)(2,1)S(1)} %copy-done.5, f32[1280]{0:T(1024)S(1)} %copy-done.16), custom_call_target="tpu_custom_call" | custom-call | flops 1000000 | bytes 1000 | tf_op jit(solution)/shard_map/norm_patches/pallas_call | solution.py:32
  6.7 1.5 %collective-permute-start = (bf16[128,1280]{1,0:T(8,128)(2,1)}, bf16[128,1280]{1,0:T(8,128)(2,1)}, u32[]{:S(2)}, u32[]{:S(2)}) collective-permute-start(bf16[128,1280]{1,0:T(8,128)(2,1)} %get-tuple-element.27.first_ref), channel_id=1, source_target_pairs={{0,16},{8,24},{16,0},{24,8},{1,17},{9,25},{17,1},{25,9},{2,18},{10... | collective-permute-start | bytes 983048 | tf_op jit(solution)/shard_map/ppermute | solution.py:64
  11.0 2.1 %copy-done.4 = bf16[1280,1280]{1,0:T(8,128)(2,1)S(1)} copy-done((bf16[1280,1280]{1,0:T(8,128)(2,1)S(1)}, bf16[1280,1280]{1,0:T(8,128)(2,1)}, u32[]{:S(2)}) %copy-start.4) | copy-done | bytes 3276824
  13.2 2.3 %bring_vision.1 = (bf16[1280,1280]{1,0:T(8,128)(2,1)S(1)}, bf16[1280,1280]{1,0:T(8,128)(2,1)S(1)}) custom-call(bf16[1280,1280]{1,0:T(8,128)(2,1)S(1)} %copy-done.4, bf16[1280,1280]{1,0:T(8,128)(2,1)} %da.1, f32[8,128]{1,0:T(8,128)S(1)} %get-tuple-element.29.before_ref), custom_call_target="tpu_custom_call" | custom-call | flops 1000000 | bytes 1000 | tf_op jit(solution)/shard_map/bring_vision/pallas_call | solution.py:32
  15.5 2.1 %collective-permute-done.rows_ref = bf16[128,1280]{1,0:T(8,128)(2,1)} collective-permute-done((bf16[128,1280]{1,0:T(8,128)(2,1)}, bf16[128,1280]{1,0:T(8,128)(2,1)}, u32[]{:S(2)}, u32[]{:S(2)}) %collective-permute-start) | collective-permute-done | bytes 327712 | tf_op jit(solution)/shard_map/ppermute | solution.py:64
  17.7 5.4 %vision_first.1 = (bf16[128,1280]{1,0:T(8,128)(2,1)S(1)}, f32[8,128]{1,0:T(8,128)S(1)}, bf16[1280,1280]{1,0:T(8,128)(2,1)S(1)}, bf16[1280,1280]{1,0:T(8,128)(2,1)S(1)}) custom-call(bf16[128,1280]{1,0:T(8,128)(2,1)} %collective-permute-done.rows_ref, bf16[1280,1280]{1,0:T(8,128)(2,1)S(1)} %get-tuple-element.30.ua, f32[1280]{0:T(1024)S(1)} %copy-done.14, ...), custom_call_target="tpu_custom_call" | custom-call | flops 1000000 | bytes 1000 | tf_op jit(solution)/shard_map/vision_first/pallas_call | solution.py:32
  23.1 2.0 %collective-permute-start.6 = (bf16[128,1280]{1,0:T(8,128)(2,1)S(1)}, bf16[128,1280]{1,0:T(8,128)(2,1)S(1)}, u32[]{:S(2)}, u32[]{:S(2)}) collective-permute-start(bf16[128,1280]{1,0:T(8,128)(2,1)S(1)} %get-tuple-element.36), channel_id=1, source_target_pairs={{0,16},{8,24},{16,0},{24,8},{1,17},{9,25},{17,1},{25,9},{2,18},{10... | collective-permute-start | bytes 983048 | tf_op jit(solution)/shard_map/ppermute | solution.py:64
  25.2 4.1 %vision_second.1 = (bf16[640,1280]{1,0:T(8,128)(2,1)}, bf16[160,1280]{1,0:T(8,128)(2,1)S(1)}, bf16[128,1280]{1,0:T(8,128)(2,1)S(1)}, bf16[128,1280]{1,0:T(8,128)(2,1)S(1)}, f32[8,128]{1,0:T(8,128)S(1)}) custom-call(s32[2]{0:T(128)S(1)} %pad_add_fusion.core_ref.place_ref, ...), custom_call_target="tpu_custom_call", output_to_operand_aliasing={{0}: (9, {})} | custom-call | flops 30000001024 | bytes 1000 | tf_op jit(solution)/shard_map/vision_second/pallas_call | solution.py:32
  29.4 2.1 %collective-permute-start.12 = (bf16[160,1280]{1,0:T(8,128)(2,1)S(1)}, bf16[160,1280]{1,0:T(8,128)(2,1)S(1)}, u32[]{:S(2)}, u32[]{:S(2)}) collective-permute-start(bf16[160,1280]{1,0:T(8,128)(2,1)S(1)} %get-tuple-element.43), channel_id=1, source_target_pairs={{0,2},{1,3},{2,0},{3,1},{4,6},{5,7},{6,4},{7,5},{8,9},{9,8},{10,11... | collective-permute-start | bytes 1228808 | tf_op jit(solution)/shard_map/ppermute | solution.py:70
  31.5 2.6 %collective-permute-start.11 = (bf16[128,1280]{1,0:T(8,128)(2,1)S(1)}, bf16[128,1280]{1,0:T(8,128)(2,1)S(1)}, u32[]{:S(2)}, u32[]{:S(2)}) collective-permute-start(bf16[128,1280]{1,0:T(8,128)(2,1)S(1)} %get-tuple-element.42), channel_id=1, source_target_pairs={{0,4},{1,5},{2,6},{3,7},{4,0},{5,1},{6,2},{7,3},{8,12},{9,13},{10,... | collective-permute-start | bytes 983048 | tf_op jit(solution)/shard_map/ppermute | solution.py:64
  34.0 5.9 %vision_own.1 = (f32[256,1280]{1,0:T(8,128)S(1)}, bf16[5120,1280]{1,0:T(8,128)(2,1)S(1)}) custom-call(bf16[128,1280]{1,0:T(8,128)(2,1)} %get-tuple-element.27.first_ref, bf16[128,1280]{1,0:T(8,128)(2,1)} %get-tuple-element.28.second_ref, bf16[1280,1280]{1,0:T(8,128)(2,1)S(1)} %get-tuple-element.30.ua, f32[1280]{0:T(1024)S(1)} %copy-done.14, ...), custom_call_target="tpu_custom_call" | custom-call | flops 10000000000 | bytes 1000 | tf_op jit(solution)/shard_map/vision_own/pallas_call | solution.py:32
  40.1 4.6 %merge_rows.1.refs_1_.refs_0_.refs_2_ = bf16[256,1408]{1,0:T(8,128)(2,1)} custom-call(bf16[256,1280]{1,0:T(8,128)(2,1)S(1)} %copy-done.6, f32[256,1280]{1,0:T(8,128)S(1)} %get-tuple-element.37.own_ref, bf16[128,1280]{1,0:T(8,128)(2,1)S(1)} %collective-permute-done.7.back_ref, f32[1280]{0:T(1024)S(1)} %copy-done.15, ...), custom_call_target="tpu_custom_call" | custom-call | flops 1000000 | bytes 1000 | tf_op jit(solution)/shard_map/merge_rows/pallas_call | solution.py:32
  44.6 5.1 %all-to-all-start = ((bf16[8,32,1408]{2,1,0:T(8,128)(2,1)}), bf16[8,32,1408]{2,1,0:T(8,128)(2,1)}, u32[]{:S(2)}, u32[]{:S(2)}) async-start(bf16[8,32,1408]{2,1,0:T(8,128)(2,1)} %bitcast.2), calls=%async_computation | async-start | bytes 1441792 | tf_op jit(solution)/shard_map/all_to_all | solution.py:424
  49.7 2.3 %collective-permute-start.13 = (bf16[160,1280]{1,0:T(8,128)(2,1)S(1)}, bf16[160,1280]{1,0:T(8,128)(2,1)S(1)}, u32[]{:S(2)}, u32[]{:S(2)}) collective-permute-start(bf16[160,1280]{1,0:T(8,128)(2,1)S(1)} %get-tuple-element.44.mine_ref), channel_id=1, source_target_pairs={{0,16},{8,24},{16,0},{24,8},{1,17},{9,25},{17,1},{25,9},{2,18},{10... | collective-permute-start | bytes 1228808 | tf_op jit(solution)/shard_map/ppermute | solution.py:64
  53.7 2.6 %collective-permute-start.15 = (bf16[320,1280]{1,0:T(8,128)(2,1)}, bf16[320,1280]{1,0:T(8,128)(2,1)S(1)}, u32[]{:S(2)}, u32[]{:S(2)}) collective-permute-start(bf16[320,1280]{1,0:T(8,128)(2,1)} %get-tuple-element.45), channel_id=1, source_target_pairs={{0,2},{1,3},{2,0},{3,1},{4,6},{5,7},{6,4},{7,5},{8,9},{9,8},{10,11... | collective-permute-start | bytes 2457608 | tf_op jit(solution)/shard_map/ppermute | solution.py:70
  56.3 5.7 %collective-permute-done.13.other_ref = bf16[160,1280]{1,0:T(8,128)(2,1)S(1)} collective-permute-done((bf16[160,1280]{1,0:T(8,128)(2,1)S(1)}, bf16[160,1280]{1,0:T(8,128)(2,1)S(1)}, u32[]{:S(2)}, u32[]{:S(2)}) %collective-permute-start.13) | collective-permute-done | bytes 409632 | tf_op jit(solution)/shard_map/ppermute | solution.py:64
  63.7 5.3 %all-to-all-done = bf16[8,32,1408]{2,1,0:T(8,128)(2,1)} async-done(((bf16[8,32,1408]{2,1,0:T(8,128)(2,1)}), bf16[8,32,1408]{2,1,0:T(8,128)(2,1)}, u32[]{:S(2)}, u32[]{:S(2)}) %all-to-all-start) | async-done | bytes 720928 | tf_op jit(solution)/shard_map/all_to_all | solution.py:424
  69.9 4.6 %text_theirs.1 = (bf16[128,1280]{1,0:T(8,128)(2,1)S(1)}, f32[128,1280]{1,0:T(8,128)S(1)}) custom-call(bf16[128,1280]{1,0:T(8,128)(2,1)S(1)} %copy-done.10, bf16[256,1408]{1,0:T(8,128)(2,1)} %after.4.got_ref, bf16[640,1280]{1,0:T(8,128)(2,1)} %refs_0_.4, bf16[640,1280]{1,0:T(8,128)(2,1)} %refs_1_.5, bf16[640,1280]{1,0:T(8,128)(2,1)} %get-tuple-element.40.refs_2_, ...), custom_call_target="tpu_custom_call" | custom-call | flops 1000000 | bytes 1000 | tf_op jit(solution)/shard_map/text_theirs/pallas_call | solution.py:32
  74.7 2.6 %text_theirs_more.1.total_ref = f32[128,1280]{1,0:T(8,128)S(1)} custom-call(bf16[128,1280]{1,0:T(8,128)(2,1)S(1)} %get-tuple-element.47.refs_1_.normed_ref, f32[128,1280]{1,0:T(8,128)S(1)} %get-tuple-element.48.total_ref, bf16[640,1280]{1,0:T(8,128)(2,1)} %collective-permute-done.9.refs_4_.up_ref, bf16[640,1280]{1,0:T(8,128)(2,1)} %collective-permute-done.10.refs_5_.down_ref), custom_call_target="tpu_custom_call" | custom-call | flops 1000000 | bytes 1000 | tf_op jit(solution)/shard_map/text_theirs_more/pallas_call | solution.py:32
  77.4 2.4 %text_theirs_last.1 = bf16[128,1280]{1,0:T(8,128)(2,1)S(1)} custom-call(bf16[128,1280]{1,0:T(8,128)(2,1)S(1)} %get-tuple-element.47.refs_1_.normed_ref, f32[128,1280]{1,0:T(8,128)S(1)} %text_theirs_more.1.total_ref, bf16[320,1280]{1,0:T(8,128)(2,1)S(1)} %order_across.1.refs_6_.up_ref, bf16[320,1280]{1,0:T(8,128)(2,1)} %collective-permute-done.14.refs_7_.other_up_ref, ...), custom_call_target="tpu_custom_call" | custom-call | flops 1000000 | bytes 1000 | tf_op jit(solution)/shard_map/text_theirs_last/pallas_call | solution.py:32
  79.9 6.7 %text_mine.1 = f32[128,1280]{1,0:T(8,128)S(1)} custom-call(bf16[128,1280]{1,0:T(8,128)(2,1)S(1)} %copy-done.12, bf16[256,1408]{1,0:T(8,128)(2,1)} %after.4.got_ref, bf16[640,1280]{1,0:T(8,128)(2,1)S(1)} %copy-done.3, bf16[640,1280]{1,0:T(8,128)(2,1)} %refs_1_.5, bf16[640,1280]{1,0:T(8,128)(2,1)} %get-tuple-element.40.refs_2_, ...), custom_call_target="tpu_custom_call" | custom-call | flops 1000000 | bytes 1000 | tf_op jit(solution)/shard_map/text_mine/pallas_call | solution.py:32
  86.6 10.3 %collective-permute-done.17 = bf16[128,1280]{1,0:T(8,128)(2,1)S(1)} collective-permute-done((bf16[128,1280]{1,0:T(8,128)(2,1)S(1)}, bf16[128,1280]{1,0:T(8,128)(2,1)S(1)}, u32[]{:S(2)}, u32[]{:S(2)}) %collective-permute-start.17) | collective-permute-done | bytes 327712 | tf_op jit(solution)/shard_map/ppermute | solution.py:64
  (76 shorter events, 9.5 us)
Async XLA Ops:
  0.0 10.9 %collective-permute-start.1 = (bf16[1280,1280]{1,0:T(8,128)(2,1)}, bf16[1280,1280]{1,0:T(8,128)(2,1)S(1)}, u32[]{:S(2)}, u32[]{:S(2)}) collective-permute-start(bf16[1280,1280]{1,0:T(8,128)(2,1)} %ua.1), channel_id=1, source_target_pairs={{0,8},{8,0},{16,24},{24,16},{1,9},{9,1},{17,25},{25,17},{2,10},{10... | collective-permute-start | bytes 9830408 | tf_op jit(solution)/shard_map/ppermute | solution.py:64
  0.5 17.2 %collective-permute-start.3 = (bf16[1280,1280]{1,0:T(8,128)(2,1)}, bf16[1280,1280]{1,0:T(8,128)(2,1)}, u32[]{:S(2)}, u32[]{:S(2)}) collective-permute-start(bf16[1280,1280]{1,0:T(8,128)(2,1)} %da.1), channel_id=1, source_target_pairs={{0,8},{8,0},{16,24},{24,16},{1,9},{9,1},{17,25},{25,17},{2,10},{10... | collective-permute-start | bytes 9830408 | tf_op jit(solution)/shard_map/ppermute | solution.py:64
  0.5 24.6 %collective-permute-start.5 = (bf16[640,1280]{1,0:T(8,128)(2,1)}, bf16[640,1280]{1,0:T(8,128)(2,1)}, u32[]{:S(2)}, u32[]{:S(2)}) collective-permute-start(bf16[640,1280]{1,0:T(8,128)(2,1)} %refs_0_.4), channel_id=1, source_target_pairs={{0,1},{1,0},{2,3},{3,2},{4,5},{5,4},{6,7},{7,6},{8,10},{9,11},{10,... | collective-permute-start | bytes 4915208 | tf_op jit(solution)/shard_map/ppermute | solution.py:70
  6.7 10.9 %collective-permute-start = (bf16[128,1280]{1,0:T(8,128)(2,1)}, bf16[128,1280]{1,0:T(8,128)(2,1)}, u32[]{:S(2)}, u32[]{:S(2)}) collective-permute-start(bf16[128,1280]{1,0:T(8,128)(2,1)} %get-tuple-element.27.first_ref), channel_id=1, source_target_pairs={{0,16},{8,24},{16,0},{24,8},{1,17},{9,25},{17,1},{25,9},{2,18},{10... | collective-permute-start | bytes 983048 | tf_op jit(solution)/shard_map/ppermute | solution.py:64
  8.2 17.0 %collective-permute-start.4 = (bf16[128,1280]{1,0:T(8,128)(2,1)}, bf16[128,1280]{1,0:T(8,128)(2,1)}, u32[]{:S(2)}, u32[]{:S(2)}) collective-permute-start(bf16[128,1280]{1,0:T(8,128)(2,1)} %get-tuple-element.28.second_ref), channel_id=1, source_target_pairs={{0,16},{8,24},{16,0},{24,8},{1,17},{9,25},{17,1},{25,9},{2,18},{10... | collective-permute-start | bytes 983048 | tf_op jit(solution)/shard_map/ppermute | solution.py:64
  10.9 6.8 %collective-permute-start.2 = (f32[1280]{0:T(1024)S(1)}, f32[1280]{0:T(1024)S(1)}, u32[]{:S(2)}, u32[]{:S(2)}) collective-permute-start(f32[1280]{0:T(1024)S(1)} %after.3), channel_id=1, source_target_pairs={{0,8},{8,0},{16,24},{24,16},{1,9},{9,1},{17,25},{25,17},{2,10},{10... | collective-permute-start | bytes 15368 | tf_op jit(solution)/shard_map/ppermute | solution.py:64
  17.6 34.4 %collective-permute-start.8 = (bf16[640,1280]{1,0:T(8,128)(2,1)}, bf16[640,1280]{1,0:T(8,128)(2,1)S(1)}, u32[]{:S(2)}, u32[]{:S(2)}) collective-permute-start(bf16[640,1280]{1,0:T(8,128)(2,1)} %refs_1_.5), channel_id=1, source_target_pairs={{0,1},{1,0},{2,3},{3,2},{4,5},{5,4},{6,7},{7,6},{8,10},{9,11},{10,... | collective-permute-start | bytes 4915208 | tf_op jit(solution)/shard_map/ppermute | solution.py:70
  17.7 7.5 %copy-start.11 = (bf16[128,1280]{1,0:T(8,128)(2,1)S(1)}, bf16[128,1280]{1,0:T(8,128)(2,1)}, u32[]{:S(2)}) copy-start(bf16[128,1280]{1,0:T(8,128)(2,1)} %embed_ref.1) | copy-start | bytes 983044
  23.1 10.9 %collective-permute-start.6 = (bf16[128,1280]{1,0:T(8,128)(2,1)S(1)}, bf16[128,1280]{1,0:T(8,128)(2,1)S(1)}, u32[]{:S(2)}, u32[]{:S(2)}) collective-permute-start(bf16[128,1280]{1,0:T(8,128)(2,1)S(1)} %get-tuple-element.36), channel_id=1, source_target_pairs={{0,16},{8,24},{16,0},{24,8},{1,17},{9,25},{17,1},{25,9},{2,18},{10... | collective-permute-start | bytes 983048 | tf_op jit(solution)/shard_map/ppermute | solution.py:64
  29.2 10.7 %collective-permute-start.7 = (bf16[128,1280]{1,0:T(8,128)(2,1)S(1)}, bf16[128,1280]{1,0:T(8,128)(2,1)S(1)}, u32[]{:S(2)}, u32[]{:S(2)}) collective-permute-start(bf16[128,1280]{1,0:T(8,128)(2,1)S(1)} %get-tuple-element.38), channel_id=1, source_target_pairs={{0,16},{8,24},{16,0},{24,8},{1,17},{9,25},{17,1},{25,9},{2,18},{10... | collective-permute-start | bytes 983048 | tf_op jit(solution)/shard_map/ppermute | solution.py:64
  29.4 20.3 %collective-permute-start.12 = (bf16[160,1280]{1,0:T(8,128)(2,1)S(1)}, bf16[160,1280]{1,0:T(8,128)(2,1)S(1)}, u32[]{:S(2)}, u32[]{:S(2)}) collective-permute-start(bf16[160,1280]{1,0:T(8,128)(2,1)S(1)} %get-tuple-element.43), channel_id=1, source_target_pairs={{0,2},{1,3},{2,0},{3,1},{4,6},{5,7},{6,4},{7,5},{8,9},{9,8},{10,11... | collective-permute-start | bytes 1228808 | tf_op jit(solution)/shard_map/ppermute | solution.py:70
  31.5 18.2 %collective-permute-start.11 = (bf16[128,1280]{1,0:T(8,128)(2,1)S(1)}, bf16[128,1280]{1,0:T(8,128)(2,1)S(1)}, u32[]{:S(2)}, u32[]{:S(2)}) collective-permute-start(bf16[128,1280]{1,0:T(8,128)(2,1)S(1)} %get-tuple-element.42), channel_id=1, source_target_pairs={{0,4},{1,5},{2,6},{3,7},{4,0},{5,1},{6,2},{7,3},{8,12},{9,13},{10,... | collective-permute-start | bytes 983048 | tf_op jit(solution)/shard_map/ppermute | solution.py:64
  34.0 6.0 %copy-start.15 = (f32[1280]{0:T(1024)S(1)}, f32[1280]{0:T(1024)}, u32[]{:S(2)}) copy-start(f32[1280]{0:T(1024)} %gain_ref.3) | copy-start | bytes 15364
  44.6 24.3 %all-to-all-start = ((bf16[8,32,1408]{2,1,0:T(8,128)(2,1)}), bf16[8,32,1408]{2,1,0:T(8,128)(2,1)}, u32[]{:S(2)}, u32[]{:S(2)}) async-start(bf16[8,32,1408]{2,1,0:T(8,128)(2,1)} %bitcast.2), calls=%async_computation | async-start | bytes 1441792 | tf_op jit(solution)/shard_map/all_to_all | solution.py:424
  49.7 6.6 %copy-start.7 = (bf16[160,1280]{1,0:T(8,128)(2,1)}, bf16[160,1280]{1,0:T(8,128)(2,1)S(1)}, u32[]{:S(2)}) copy-start(bf16[160,1280]{1,0:T(8,128)(2,1)S(1)} %get-tuple-element.44.mine_ref) | copy-start | bytes 1228804
  49.7 6.6 %copy-start.9 = (bf16[128,1280]{1,0:T(8,128)(2,1)}, bf16[128,1280]{1,0:T(8,128)(2,1)S(1)}, u32[]{:S(2)}) copy-start(bf16[128,1280]{1,0:T(8,128)(2,1)S(1)} %get-tuple-element.46.embed_ref) | copy-start | bytes 983044
  49.7 12.2 %collective-permute-start.13 = (bf16[160,1280]{1,0:T(8,128)(2,1)S(1)}, bf16[160,1280]{1,0:T(8,128)(2,1)S(1)}, u32[]{:S(2)}, u32[]{:S(2)}) collective-permute-start(bf16[160,1280]{1,0:T(8,128)(2,1)S(1)} %get-tuple-element.44.mine_ref), channel_id=1, source_target_pairs={{0,16},{8,24},{16,0},{24,8},{1,17},{9,25},{17,1},{25,9},{2,18},{10... | collective-permute-start | bytes 1228808 | tf_op jit(solution)/shard_map/ppermute | solution.py:64
  52.0 22.6 %collective-permute-start.9 = (bf16[640,1280]{1,0:T(8,128)(2,1)}, bf16[640,1280]{1,0:T(8,128)(2,1)}, u32[]{:S(2)}, u32[]{:S(2)}) collective-permute-start(bf16[640,1280]{1,0:T(8,128)(2,1)} %get-tuple-element.40.refs_2_), channel_id=1, source_target_pairs={{0,8},{8,0},{16,24},{24,16},{1,9},{9,1},{17,25},{25,17},{2,10},{10... | collective-permute-start | bytes 4915208 | tf_op jit(solution)/shard_map/ppermute | solution.py:64
  53.1 15.9 %copy-start = (bf16[640,1280]{1,0:T(8,128)(2,1)}, bf16[640,1280]{1,0:T(8,128)(2,1)S(1)}, u32[]{:S(2)}) copy-start(bf16[640,1280]{1,0:T(8,128)(2,1)S(1)} %get-tuple-element.41.refs_3_) | copy-start | bytes 4915204
  53.1 21.6 %collective-permute-start.10 = (bf16[640,1280]{1,0:T(8,128)(2,1)S(1)}, bf16[640,1280]{1,0:T(8,128)(2,1)}, u32[]{:S(2)}, u32[]{:S(2)}) collective-permute-start(bf16[640,1280]{1,0:T(8,128)(2,1)S(1)} %get-tuple-element.41.refs_3_), channel_id=1, source_target_pairs={{0,8},{8,0},{16,24},{24,16},{1,9},{9,1},{17,25},{25,17},{2,10},{10... | collective-permute-start | bytes 4915208 | tf_op jit(solution)/shard_map/ppermute | solution.py:64
  53.7 20.9 %collective-permute-start.15 = (bf16[320,1280]{1,0:T(8,128)(2,1)}, bf16[320,1280]{1,0:T(8,128)(2,1)S(1)}, u32[]{:S(2)}, u32[]{:S(2)}) collective-permute-start(bf16[320,1280]{1,0:T(8,128)(2,1)} %get-tuple-element.45), channel_id=1, source_target_pairs={{0,2},{1,3},{2,0},{3,1},{4,6},{5,7},{6,4},{7,5},{8,9},{9,8},{10,11... | collective-permute-start | bytes 2457608 | tf_op jit(solution)/shard_map/ppermute | solution.py:70
  63.6 13.8 %collective-permute-start.14 = (bf16[320,1280]{1,0:T(8,128)(2,1)S(1)}, bf16[320,1280]{1,0:T(8,128)(2,1)}, u32[]{:S(2)}, u32[]{:S(2)}) collective-permute-start(bf16[320,1280]{1,0:T(8,128)(2,1)S(1)} %order_across.1.refs_6_.up_ref), channel_id=1, source_target_pairs={{0,8},{8,0},{16,24},{24,16},{1,9},{9,1},{17,25},{25,17},{2,10},{10... | collective-permute-start | bytes 2457608 | tf_op jit(solution)/shard_map/ppermute | solution.py:64
  74.6 2.8 %collective-permute-start.16 = (bf16[320,1280]{1,0:T(8,128)(2,1)S(1)}, bf16[320,1280]{1,0:T(8,128)(2,1)S(1)}, u32[]{:S(2)}, u32[]{:S(2)}) collective-permute-start(bf16[320,1280]{1,0:T(8,128)(2,1)S(1)} %after.5.refs_8_.down_ref), channel_id=1, source_target_pairs={{0,8},{8,0},{16,24},{24,16},{1,9},{9,1},{17,25},{25,17},{2,10},{10... | collective-permute-start | bytes 2457608 | tf_op jit(solution)/shard_map/ppermute | solution.py:64
  79.7 17.2 %collective-permute-start.17 = (bf16[128,1280]{1,0:T(8,128)(2,1)S(1)}, bf16[128,1280]{1,0:T(8,128)(2,1)S(1)}, u32[]{:S(2)}, u32[]{:S(2)}) collective-permute-start(bf16[128,1280]{1,0:T(8,128)(2,1)S(1)} %text_theirs_last.1), channel_id=1, source_target_pairs={{0,4},{1,5},{2,6},{3,7},{4,0},{5,1},{6,2},{7,3},{8,12},{9,13},{10,... | collective-permute-start | bytes 983048 | tf_op jit(solution)/shard_map/ppermute | solution.py:64
  (12 other events, 30.3 us)

commit v6 on v5

--- a/solution.py
+++ b/solution.py
@@ -337,7 +337,7 @@
     far_up, far_down = swap(vis_up, "seq", 1), swap(vis_down, "seq", 1)
     other_bias = swap(after(vis_bias, far_up), "seq", 1)
     first, second, normed = call(
-        norm_patches_kernel, "norm_patches", (half_rows, half_rows, TOKEN), (patches, vis_gain), megabytes=40
+        norm_patches_kernel, "norm_patches", (half_rows, half_rows, TOKEN), (patches, vis_gain), megabytes=60
     )
     far_first, far_second = swap(first, "seq", 2), swap(second, "seq", 2)
     near_up, near_down = call(

time: 98.3 us -> 98.1 us (level)
  starting transfers between devices: 23.2 us -> 26.2 us
  local copies, waits for them, and re-layouts: 6.74 us -> 4.56 us
  waiting for transfers between devices: 23.5 us -> 22.5 us
    ppermute x14, starting transfers between devices: 10.4 us -> 13.7 us  [swap(): return lax.ppermute(x, axis, [(i, i ^ bit) for i in range(size)])]
    unnamed x35 -> x37, local copies, waits for them, and re-layouts: 6.65 us -> 4.47 us
    ppermute x14, waiting for transfers between devices: 18.1 us -> 16.4 us  [swap(): return lax.ppermute(x, axis, [(i, i ^ bit) for i in range(size)])]
  transfers between devices with their start and end apart: 19 -> 19, of which waited for: 4 -> 6; matrix products, arithmetic and copies ran while one was open for 2% -> 2% of each run, Pallas kernels for 40% -> 40%
where the time goes in v6:
time: 98.1 us; the launch traced here: 97.7 us
  Pallas kernels  41.8 us (43%)
  starting transfers between devices  26.2 us (27%)
  waiting for transfers between devices  22.5 us (23%)
  local copies, waits for them, and re-layouts  4.56 us (5%)
  other arithmetic  2.24 us (2%)
    pallas_call x16, Pallas kernels, call(): pl.pallas_call(kernel, out_shape=out_shape, in_specs=specs, out_specs=tup...  41.8 us
    ppermute x14, waiting for transfers between devices, swap(): return lax.ppermute(x, axis, [(i, i ^ bit) for i in range(size)])  16.4 us
    ppermute x14, starting transfers between devices, swap(): return lax.ppermute(x, axis, [(i, i ^ bit) for i in range(size)])  13.7 us
    ppermute x4, starting transfers between devices, swap_by_core(): return lax.ppermute(x, ('seq', 'blk'), pairs)  7.58 us
    all_to_all x1, waiting for transfers between devices, per_device(): got = lax.all_to_all(send, 'blk', split_axis=0, concat_axis=0, tiled=True)  6.06 us
    all_to_all x1, starting transfers between devices, per_device(): got = lax.all_to_all(send, 'blk', split_axis=0, concat_axis=0, tiled=True)  4.93 us
    unnamed x37, local copies, waits for them, and re-layouts  4.47 us
  transfers between devices with their start and end apart: 19, of which 6 were waited for; matrix products, arithmetic and copies ran while one was open for 2% of the time, Pallas kernels for 40%

profile of v6, /device:TPU:0, one launch (start us, length us, event | category | flops | bytes accessed | tf_op | source)
XLA Modules:
  0.0 97.7 jit_solution(13794801858641032424)
XLA Ops:
  0.5 3.0 %collective-permute-start.5 = (bf16[640,1280]{1,0:T(8,128)(2,1)}, bf16[640,1280]{1,0:T(8,128)(2,1)}, u32[]{:S(2)}, u32[]{:S(2)}) collective-permute-start(bf16[640,1280]{1,0:T(8,128)(2,1)} %refs_0_.4), channel_id=1, source_target_pairs={{0,1},{1,0},{2,3},{3,2},{4,5},{5,4},{6,7},{7,6},{8,10},{9,11},{10,... | collective-permute-start | bytes 4915208 | tf_op jit(solution)/shard_map/ppermute | solution.py:70
  3.5 2.6 %norm_patches.1 = (bf16[128,1280]{1,0:T(8,128)(2,1)}, bf16[128,1280]{1,0:T(8,128)(2,1)}, f32[8,128]{1,0:T(8,128)}) custom-call(bf16[256,1280]{1,0:T(8,128)(2,1)} %patches_ref.3, f32[1280]{0:T(1024)} %gain_ref.2), custom_call_target="tpu_custom_call" | custom-call | flops 1000000 | bytes 1000 | tf_op jit(solution)/shard_map/norm_patches/pallas_call | solution.py:32
  10.7 1.7 %copy-done.4 = bf16[1280,1280]{1,0:T(8,128)(2,1)S(1)} copy-done((bf16[1280,1280]{1,0:T(8,128)(2,1)S(1)}, bf16[1280,1280]{1,0:T(8,128)(2,1)}, u32[]{:S(2)}) %copy-start.4) | copy-done | bytes 3276824
  12.4 2.3 %bring_vision.1 = (bf16[1280,1280]{1,0:T(8,128)(2,1)S(1)}, bf16[1280,1280]{1,0:T(8,128)(2,1)S(1)}) custom-call(bf16[1280,1280]{1,0:T(8,128)(2,1)S(1)} %copy-done.4, bf16[1280,1280]{1,0:T(8,128)(2,1)} %da.1, f32[8,128]{1,0:T(8,128)S(1)} %copy-done.15), custom_call_target="tpu_custom_call" | custom-call | flops 1000000 | bytes 1000 | tf_op jit(solution)/shard_map/bring_vision/pallas_call | solution.py:32
  14.8 2.2 %collective-permute-done.rows_ref = bf16[128,1280]{1,0:T(8,128)(2,1)} collective-permute-done((bf16[128,1280]{1,0:T(8,128)(2,1)}, bf16[128,1280]{1,0:T(8,128)(2,1)}, u32[]{:S(2)}, u32[]{:S(2)}) %collective-permute-start) | collective-permute-done | bytes 327712 | tf_op jit(solution)/shard_map/ppermute | solution.py:64
  17.0 5.5 %vision_first.1 = (bf16[128,1280]{1,0:T(8,128)(2,1)S(1)}, f32[8,128]{1,0:T(8,128)S(1)}, bf16[1280,1280]{1,0:T(8,128)(2,1)S(1)}, bf16[1280,1280]{1,0:T(8,128)(2,1)S(1)}) custom-call(bf16[128,1280]{1,0:T(8,128)(2,1)} %collective-permute-done.rows_ref, bf16[1280,1280]{1,0:T(8,128)(2,1)S(1)} %get-tuple-element.30.ua, f32[1280]{0:T(1024)S(1)} %copy-done.13, ...), custom_call_target="tpu_custom_call" | custom-call | flops 1000000 | bytes 1000 | tf_op jit(solution)/shard_map/vision_first/pallas_call | solution.py:32
  22.5 2.0 %collective-permute-start.6 = (bf16[128,1280]{1,0:T(8,128)(2,1)S(1)}, bf16[128,1280]{1,0:T(8,128)(2,1)S(1)}, u32[]{:S(2)}, u32[]{:S(2)}) collective-permute-start(bf16[128,1280]{1,0:T(8,128)(2,1)S(1)} %get-tuple-element.36), channel_id=1, source_target_pairs={{0,16},{8,24},{16,0},{24,8},{1,17},{9,25},{17,1},{25,9},{2,18},{10... | collective-permute-start | bytes 983048 | tf_op jit(solution)/shard_map/ppermute | solution.py:64
  24.5 4.1 %vision_second.1 = (bf16[640,1280]{1,0:T(8,128)(2,1)}, bf16[160,1280]{1,0:T(8,128)(2,1)S(1)}, bf16[128,1280]{1,0:T(8,128)(2,1)S(1)}, bf16[128,1280]{1,0:T(8,128)(2,1)S(1)}, f32[8,128]{1,0:T(8,128)S(1)}) custom-call(s32[2]{0:T(128)S(1)} %pad_add_fusion.core_ref.place_ref, ...), custom_call_target="tpu_custom_call", output_to_operand_aliasing={{0}: (9, {})} | custom-call | flops 30000001024 | bytes 1000 | tf_op jit(solution)/shard_map/vision_second/pallas_call | solution.py:32
  29.1 1.8 %collective-permute-start.12 = (bf16[160,1280]{1,0:T(8,128)(2,1)S(1)}, bf16[160,1280]{1,0:T(8,128)(2,1)S(1)}, u32[]{:S(2)}, u32[]{:S(2)}) collective-permute-start(bf16[160,1280]{1,0:T(8,128)(2,1)S(1)} %get-tuple-element.43), channel_id=1, source_target_pairs={{0,2},{1,3},{2,0},{3,1},{4,6},{5,7},{6,4},{7,5},{8,9},{9,8},{10,11... | collective-permute-start | bytes 1228808 | tf_op jit(solution)/shard_map/ppermute | solution.py:70
  30.9 2.6 %collective-permute-start.11 = (bf16[128,1280]{1,0:T(8,128)(2,1)S(1)}, bf16[128,1280]{1,0:T(8,128)(2,1)S(1)}, u32[]{:S(2)}, u32[]{:S(2)}) collective-permute-start(bf16[128,1280]{1,0:T(8,128)(2,1)S(1)} %get-tuple-element.42), channel_id=1, source_target_pairs={{0,4},{1,5},{2,6},{3,7},{4,0},{5,1},{6,2},{7,3},{8,12},{9,13},{10,... | collective-permute-start | bytes 983048 | tf_op jit(solution)/shard_map/ppermute | solution.py:64
  33.5 4.8 %vision_own.1 = (f32[256,1280]{1,0:T(8,128)S(1)}, bf16[5120,1280]{1,0:T(8,128)(2,1)S(1)}) custom-call(bf16[128,1280]{1,0:T(8,128)(2,1)S(1)} %copy-done.16, bf16[128,1280]{1,0:T(8,128)(2,1)S(1)} %copy-done.17, bf16[1280,1280]{1,0:T(8,128)(2,1)S(1)} %get-tuple-element.30.ua, f32[1280]{0:T(1024)S(1)} %copy-done.13, ...), custom_call_target="tpu_custom_call" | custom-call | flops 10000000000 | bytes 1000 | tf_op jit(solution)/shard_map/vision_own/pallas_call | solution.py:32
  39.1 4.6 %merge_rows.1.refs_1_.refs_0_.refs_2_ = bf16[256,1408]{1,0:T(8,128)(2,1)} custom-call(bf16[256,1280]{1,0:T(8,128)(2,1)S(1)} %copy-done.5, f32[256,1280]{1,0:T(8,128)S(1)} %get-tuple-element.37.own_ref, bf16[128,1280]{1,0:T(8,128)(2,1)S(1)} %collective-permute-done.7.back_ref, f32[1280]{0:T(1024)S(1)} %copy-done.14, ...), custom_call_target="tpu_custom_call" | custom-call | flops 1000000 | bytes 1000 | tf_op jit(solution)/shard_map/merge_rows/pallas_call | solution.py:32
  43.6 4.9 %all-to-all-start = ((bf16[8,32,1408]{2,1,0:T(8,128)(2,1)}), bf16[8,32,1408]{2,1,0:T(8,128)(2,1)}, u32[]{:S(2)}, u32[]{:S(2)}) async-start(bf16[8,32,1408]{2,1,0:T(8,128)(2,1)} %bitcast.2), calls=%async_computation | async-start | bytes 1441792 | tf_op jit(solution)/shard_map/all_to_all | solution.py:424
  48.6 1.6 %collective-permute-start.13 = (bf16[160,1280]{1,0:T(8,128)(2,1)S(1)}, bf16[160,1280]{1,0:T(8,128)(2,1)S(1)}, u32[]{:S(2)}, u32[]{:S(2)}) collective-permute-start(bf16[160,1280]{1,0:T(8,128)(2,1)S(1)} %get-tuple-element.44.mine_ref), channel_id=1, source_target_pairs={{0,16},{8,24},{16,0},{24,8},{1,17},{9,25},{17,1},{25,9},{2,18},{10... | collective-permute-start | bytes 1228808 | tf_op jit(solution)/shard_map/ppermute | solution.py:64
  50.2 2.1 %collective-permute-start.9 = (bf16[640,1280]{1,0:T(8,128)(2,1)}, bf16[640,1280]{1,0:T(8,128)(2,1)}, u32[]{:S(2)}, u32[]{:S(2)}) collective-permute-start(bf16[640,1280]{1,0:T(8,128)(2,1)} %get-tuple-element.40.refs_2_), channel_id=1, source_target_pairs={{0,8},{8,0},{16,24},{24,16},{1,9},{9,1},{17,25},{25,17},{2,10},{10... | collective-permute-start | bytes 4915208 | tf_op jit(solution)/shard_map/ppermute | solution.py:64
  53.4 2.8 %collective-permute-start.15 = (bf16[320,1280]{1,0:T(8,128)(2,1)}, bf16[320,1280]{1,0:T(8,128)(2,1)S(1)}, u32[]{:S(2)}, u32[]{:S(2)}) collective-permute-start(bf16[320,1280]{1,0:T(8,128)(2,1)} %get-tuple-element.45), channel_id=1, source_target_pairs={{0,2},{1,3},{2,0},{3,1},{4,6},{5,7},{6,4},{7,5},{8,9},{9,8},{10,11... | collective-permute-start | bytes 2457608 | tf_op jit(solution)/shard_map/ppermute | solution.py:70
  56.3 3.2 %collective-permute-done.13.other_ref = bf16[160,1280]{1,0:T(8,128)(2,1)S(1)} collective-permute-done((bf16[160,1280]{1,0:T(8,128)(2,1)S(1)}, bf16[160,1280]{1,0:T(8,128)(2,1)S(1)}, u32[]{:S(2)}, u32[]{:S(2)}) %collective-permute-start.13) | collective-permute-done | bytes 409632 | tf_op jit(solution)/shard_map/ppermute | solution.py:64
  61.1 1.8 %collective-permute-start.14 = (bf16[320,1280]{1,0:T(8,128)(2,1)S(1)}, bf16[320,1280]{1,0:T(8,128)(2,1)}, u32[]{:S(2)}, u32[]{:S(2)}) collective-permute-start(bf16[320,1280]{1,0:T(8,128)(2,1)S(1)} %order_across.1.refs_6_.up_ref), channel_id=1, source_target_pairs={{0,8},{8,0},{16,24},{24,16},{1,9},{9,1},{17,25},{25,17},{2,10},{10... | collective-permute-start | bytes 2457608 | tf_op jit(solution)/shard_map/ppermute | solution.py:64
  62.9 6.1 %all-to-all-done = bf16[8,32,1408]{2,1,0:T(8,128)(2,1)} async-done(((bf16[8,32,1408]{2,1,0:T(8,128)(2,1)}), bf16[8,32,1408]{2,1,0:T(8,128)(2,1)}, u32[]{:S(2)}, u32[]{:S(2)}) %all-to-all-start) | async-done | bytes 720928 | tf_op jit(solution)/shard_map/all_to_all | solution.py:424
  69.9 4.6 %text_theirs.1 = (bf16[128,1280]{1,0:T(8,128)(2,1)S(1)}, f32[128,1280]{1,0:T(8,128)S(1)}) custom-call(bf16[128,1280]{1,0:T(8,128)(2,1)S(1)} %copy-done.9, bf16[256,1408]{1,0:T(8,128)(2,1)} %after.4.got_ref, bf16[640,1280]{1,0:T(8,128)(2,1)} %refs_0_.4, bf16[640,1280]{1,0:T(8,128)(2,1)} %refs_1_.5, bf16[640,1280]{1,0:T(8,128)(2,1)} %get-tuple-element.40.refs_2_, ...), custom_call_target="tpu_custom_call" | custom-call | flops 1000000 | bytes 1000 | tf_op jit(solution)/shard_map/text_theirs/pallas_call | solution.py:32
  74.7 2.6 %text_theirs_more.1.total_ref = f32[128,1280]{1,0:T(8,128)S(1)} custom-call(bf16[128,1280]{1,0:T(8,128)(2,1)S(1)} %get-tuple-element.47.refs_1_.normed_ref, f32[128,1280]{1,0:T(8,128)S(1)} %get-tuple-element.48.total_ref, bf16[640,1280]{1,0:T(8,128)(2,1)} %collective-permute-done.9.refs_4_.up_ref, bf16[640,1280]{1,0:T(8,128)(2,1)} %collective-permute-done.10.refs_5_.down_ref), custom_call_target="tpu_custom_call" | custom-call | flops 1000000 | bytes 1000 | tf_op jit(solution)/shard_map/text_theirs_more/pallas_call | solution.py:32
  77.4 2.4 %text_theirs_last.1 = bf16[128,1280]{1,0:T(8,128)(2,1)S(1)} custom-call(bf16[128,1280]{1,0:T(8,128)(2,1)S(1)} %get-tuple-element.47.refs_1_.normed_ref, f32[128,1280]{1,0:T(8,128)S(1)} %text_theirs_more.1.total_ref, bf16[320,1280]{1,0:T(8,128)(2,1)S(1)} %order_across.1.refs_6_.up_ref, bf16[320,1280]{1,0:T(8,128)(2,1)} %collective-permute-done.14.refs_7_.other_up_ref, ...), custom_call_target="tpu_custom_call" | custom-call | flops 1000000 | bytes 1000 | tf_op jit(solution)/shard_map/text_theirs_last/pallas_call | solution.py:32
  79.9 6.7 %text_mine.1 = f32[128,1280]{1,0:T(8,128)S(1)} custom-call(bf16[128,1280]{1,0:T(8,128)(2,1)S(1)} %copy-done.11, bf16[256,1408]{1,0:T(8,128)(2,1)} %after.4.got_ref, bf16[640,1280]{1,0:T(8,128)(2,1)S(1)} %copy-done.3, bf16[640,1280]{1,0:T(8,128)(2,1)} %refs_1_.5, bf16[640,1280]{1,0:T(8,128)(2,1)} %get-tuple-element.40.refs_2_, ...), custom_call_target="tpu_custom_call" | custom-call | flops 1000000 | bytes 1000 | tf_op jit(solution)/shard_map/text_mine/pallas_call | solution.py:32
  86.6 10.3 %collective-permute-done.17 = bf16[128,1280]{1,0:T(8,128)(2,1)S(1)} collective-permute-done((bf16[128,1280]{1,0:T(8,128)(2,1)S(1)}, bf16[128,1280]{1,0:T(8,128)(2,1)S(1)}, u32[]{:S(2)}, u32[]{:S(2)}) %collective-permute-start.17) | collective-permute-done | bytes 327712 | tf_op jit(solution)/shard_map/ppermute | solution.py:64
  (78 shorter events, 11.0 us)
Async XLA Ops:
  0.0 10.2 %collective-permute-start.1 = (bf16[1280,1280]{1,0:T(8,128)(2,1)}, bf16[1280,1280]{1,0:T(8,128)(2,1)S(1)}, u32[]{:S(2)}, u32[]{:S(2)}) collective-permute-start(bf16[1280,1280]{1,0:T(8,128)(2,1)} %ua.1), channel_id=1, source_target_pairs={{0,8},{8,0},{16,24},{24,16},{1,9},{9,1},{17,25},{25,17},{2,10},{10... | collective-permute-start | bytes 9830408 | tf_op jit(solution)/shard_map/ppermute | solution.py:64
  0.5 16.5 %collective-permute-start.3 = (bf16[1280,1280]{1,0:T(8,128)(2,1)}, bf16[1280,1280]{1,0:T(8,128)(2,1)}, u32[]{:S(2)}, u32[]{:S(2)}) collective-permute-start(bf16[1280,1280]{1,0:T(8,128)(2,1)} %da.1), channel_id=1, source_target_pairs={{0,8},{8,0},{16,24},{24,16},{1,9},{9,1},{17,25},{25,17},{2,10},{10... | collective-permute-start | bytes 9830408 | tf_op jit(solution)/shard_map/ppermute | solution.py:64
  0.5 24.0 %collective-permute-start.5 = (bf16[640,1280]{1,0:T(8,128)(2,1)}, bf16[640,1280]{1,0:T(8,128)(2,1)}, u32[]{:S(2)}, u32[]{:S(2)}) collective-permute-start(bf16[640,1280]{1,0:T(8,128)(2,1)} %refs_0_.4), channel_id=1, source_target_pairs={{0,1},{1,0},{2,3},{3,2},{4,5},{5,4},{6,7},{7,6},{8,10},{9,11},{10,... | collective-permute-start | bytes 4915208 | tf_op jit(solution)/shard_map/ppermute | solution.py:70
  6.0 10.9 %collective-permute-start = (bf16[128,1280]{1,0:T(8,128)(2,1)}, bf16[128,1280]{1,0:T(8,128)(2,1)}, u32[]{:S(2)}, u32[]{:S(2)}) collective-permute-start(bf16[128,1280]{1,0:T(8,128)(2,1)} %get-tuple-element.27.first_ref), channel_id=1, source_target_pairs={{0,16},{8,24},{16,0},{24,8},{1,17},{9,25},{17,1},{25,9},{2,18},{10... | collective-permute-start | bytes 983048 | tf_op jit(solution)/shard_map/ppermute | solution.py:64
  7.5 17.0 %collective-permute-start.4 = (bf16[128,1280]{1,0:T(8,128)(2,1)}, bf16[128,1280]{1,0:T(8,128)(2,1)}, u32[]{:S(2)}, u32[]{:S(2)}) collective-permute-start(bf16[128,1280]{1,0:T(8,128)(2,1)} %get-tuple-element.28.second_ref), channel_id=1, source_target_pairs={{0,16},{8,24},{16,0},{24,8},{1,17},{9,25},{17,1},{25,9},{2,18},{10... | collective-permute-start | bytes 983048 | tf_op jit(solution)/shard_map/ppermute | solution.py:64
  10.2 6.7 %collective-permute-start.2 = (f32[1280]{0:T(1024)S(1)}, f32[1280]{0:T(1024)S(1)}, u32[]{:S(2)}, u32[]{:S(2)}) collective-permute-start(f32[1280]{0:T(1024)S(1)} %after.3), channel_id=1, source_target_pairs={{0,8},{8,0},{16,24},{24,16},{1,9},{9,1},{17,25},{25,17},{2,10},{10... | collective-permute-start | bytes 15368 | tf_op jit(solution)/shard_map/ppermute | solution.py:64
  17.0 35.4 %collective-permute-start.8 = (bf16[640,1280]{1,0:T(8,128)(2,1)}, bf16[640,1280]{1,0:T(8,128)(2,1)S(1)}, u32[]{:S(2)}, u32[]{:S(2)}) collective-permute-start(bf16[640,1280]{1,0:T(8,128)(2,1)} %refs_1_.5), channel_id=1, source_target_pairs={{0,1},{1,0},{2,3},{3,2},{4,5},{5,4},{6,7},{7,6},{8,10},{9,11},{10,... | collective-permute-start | bytes 4915208 | tf_op jit(solution)/shard_map/ppermute | solution.py:70
  22.5 11.0 %collective-permute-start.6 = (bf16[128,1280]{1,0:T(8,128)(2,1)S(1)}, bf16[128,1280]{1,0:T(8,128)(2,1)S(1)}, u32[]{:S(2)}, u32[]{:S(2)}) collective-permute-start(bf16[128,1280]{1,0:T(8,128)(2,1)S(1)} %get-tuple-element.36), channel_id=1, source_target_pairs={{0,16},{8,24},{16,0},{24,8},{1,17},{9,25},{17,1},{25,9},{2,18},{10... | collective-permute-start | bytes 983048 | tf_op jit(solution)/shard_map/ppermute | solution.py:64
  24.5 9.0 %copy-start.16 = (bf16[128,1280]{1,0:T(8,128)(2,1)S(1)}, bf16[128,1280]{1,0:T(8,128)(2,1)}, u32[]{:S(2)}) copy-start(bf16[128,1280]{1,0:T(8,128)(2,1)} %get-tuple-element.27.first_ref) | copy-start | bytes 983044
  24.5 9.0 %copy-start.17 = (bf16[128,1280]{1,0:T(8,128)(2,1)S(1)}, bf16[128,1280]{1,0:T(8,128)(2,1)}, u32[]{:S(2)}) copy-start(bf16[128,1280]{1,0:T(8,128)(2,1)} %get-tuple-element.28.second_ref) | copy-start | bytes 983044
  28.7 10.3 %collective-permute-start.7 = (bf16[128,1280]{1,0:T(8,128)(2,1)S(1)}, bf16[128,1280]{1,0:T(8,128)(2,1)S(1)}, u32[]{:S(2)}, u32[]{:S(2)}) collective-permute-start(bf16[128,1280]{1,0:T(8,128)(2,1)S(1)} %get-tuple-element.38), channel_id=1, source_target_pairs={{0,16},{8,24},{16,0},{24,8},{1,17},{9,25},{17,1},{25,9},{2,18},{10... | collective-permute-start | bytes 983048 | tf_op jit(solution)/shard_map/ppermute | solution.py:64
  29.1 19.5 %collective-permute-start.12 = (bf16[160,1280]{1,0:T(8,128)(2,1)S(1)}, bf16[160,1280]{1,0:T(8,128)(2,1)S(1)}, u32[]{:S(2)}, u32[]{:S(2)}) collective-permute-start(bf16[160,1280]{1,0:T(8,128)(2,1)S(1)} %get-tuple-element.43), channel_id=1, source_target_pairs={{0,2},{1,3},{2,0},{3,1},{4,6},{5,7},{6,4},{7,5},{8,9},{9,8},{10,11... | collective-permute-start | bytes 1228808 | tf_op jit(solution)/shard_map/ppermute | solution.py:70
  30.9 17.7 %collective-permute-start.11 = (bf16[128,1280]{1,0:T(8,128)(2,1)S(1)}, bf16[128,1280]{1,0:T(8,128)(2,1)S(1)}, u32[]{:S(2)}, u32[]{:S(2)}) collective-permute-start(bf16[128,1280]{1,0:T(8,128)(2,1)S(1)} %get-tuple-element.42), channel_id=1, source_target_pairs={{0,4},{1,5},{2,6},{3,7},{4,0},{5,1},{6,2},{7,3},{8,12},{9,13},{10,... | collective-permute-start | bytes 983048 | tf_op jit(solution)/shard_map/ppermute | solution.py:64
  43.6 25.3 %all-to-all-start = ((bf16[8,32,1408]{2,1,0:T(8,128)(2,1)}), bf16[8,32,1408]{2,1,0:T(8,128)(2,1)}, u32[]{:S(2)}, u32[]{:S(2)}) async-start(bf16[8,32,1408]{2,1,0:T(8,128)(2,1)} %bitcast.2), calls=%async_computation | async-start | bytes 1441792 | tf_op jit(solution)/shard_map/all_to_all | solution.py:424
  48.6 7.7 %copy-start.6 = (bf16[160,1280]{1,0:T(8,128)(2,1)}, bf16[160,1280]{1,0:T(8,128)(2,1)S(1)}, u32[]{:S(2)}) copy-start(bf16[160,1280]{1,0:T(8,128)(2,1)S(1)} %get-tuple-element.44.mine_ref) | copy-start | bytes 1228804
  48.6 7.7 %copy-start.8 = (bf16[128,1280]{1,0:T(8,128)(2,1)}, bf16[128,1280]{1,0:T(8,128)(2,1)S(1)}, u32[]{:S(2)}) copy-start(bf16[128,1280]{1,0:T(8,128)(2,1)S(1)} %get-tuple-element.46.embed_ref) | copy-start | bytes 983044
  48.6 10.9 %collective-permute-start.13 = (bf16[160,1280]{1,0:T(8,128)(2,1)S(1)}, bf16[160,1280]{1,0:T(8,128)(2,1)S(1)}, u32[]{:S(2)}, u32[]{:S(2)}) collective-permute-start(bf16[160,1280]{1,0:T(8,128)(2,1)S(1)} %get-tuple-element.44.mine_ref), channel_id=1, source_target_pairs={{0,16},{8,24},{16,0},{24,8},{1,17},{9,25},{17,1},{25,9},{2,18},{10... | collective-permute-start | bytes 1228808 | tf_op jit(solution)/shard_map/ppermute | solution.py:64
  50.2 24.5 %collective-permute-start.9 = (bf16[640,1280]{1,0:T(8,128)(2,1)}, bf16[640,1280]{1,0:T(8,128)(2,1)}, u32[]{:S(2)}, u32[]{:S(2)}) collective-permute-start(bf16[640,1280]{1,0:T(8,128)(2,1)} %get-tuple-element.40.refs_2_), channel_id=1, source_target_pairs={{0,8},{8,0},{16,24},{24,16},{1,9},{9,1},{17,25},{25,17},{2,10},{10... | collective-permute-start | bytes 4915208 | tf_op jit(solution)/shard_map/ppermute | solution.py:64
  53.4 15.6 %copy-start = (bf16[640,1280]{1,0:T(8,128)(2,1)}, bf16[640,1280]{1,0:T(8,128)(2,1)S(1)}, u32[]{:S(2)}) copy-start(bf16[640,1280]{1,0:T(8,128)(2,1)S(1)} %get-tuple-element.41.refs_3_) | copy-start | bytes 4915204
  53.4 21.3 %collective-permute-start.10 = (bf16[640,1280]{1,0:T(8,128)(2,1)S(1)}, bf16[640,1280]{1,0:T(8,128)(2,1)}, u32[]{:S(2)}, u32[]{:S(2)}) collective-permute-start(bf16[640,1280]{1,0:T(8,128)(2,1)S(1)} %get-tuple-element.41.refs_3_), channel_id=1, source_target_pairs={{0,8},{8,0},{16,24},{24,16},{1,9},{9,1},{17,25},{25,17},{2,10},{10... | collective-permute-start | bytes 4915208 | tf_op jit(solution)/shard_map/ppermute | solution.py:64
  53.4 21.1 %collective-permute-start.15 = (bf16[320,1280]{1,0:T(8,128)(2,1)}, bf16[320,1280]{1,0:T(8,128)(2,1)S(1)}, u32[]{:S(2)}, u32[]{:S(2)}) collective-permute-start(bf16[320,1280]{1,0:T(8,128)(2,1)} %get-tuple-element.45), channel_id=1, source_target_pairs={{0,2},{1,3},{2,0},{3,1},{4,6},{5,7},{6,4},{7,5},{8,9},{9,8},{10,11... | collective-permute-start | bytes 2457608 | tf_op jit(solution)/shard_map/ppermute | solution.py:70
  61.1 16.3 %collective-permute-start.14 = (bf16[320,1280]{1,0:T(8,128)(2,1)S(1)}, bf16[320,1280]{1,0:T(8,128)(2,1)}, u32[]{:S(2)}, u32[]{:S(2)}) collective-permute-start(bf16[320,1280]{1,0:T(8,128)(2,1)S(1)} %order_across.1.refs_6_.up_ref), channel_id=1, source_target_pairs={{0,8},{8,0},{16,24},{24,16},{1,9},{9,1},{17,25},{25,17},{2,10},{10... | collective-permute-start | bytes 2457608 | tf_op jit(solution)/shard_map/ppermute | solution.py:64
  74.6 2.8 %collective-permute-start.16 = (bf16[320,1280]{1,0:T(8,128)(2,1)S(1)}, bf16[320,1280]{1,0:T(8,128)(2,1)S(1)}, u32[]{:S(2)}, u32[]{:S(2)}) collective-permute-start(bf16[320,1280]{1,0:T(8,128)(2,1)S(1)} %after.5.refs_8_.down_ref), channel_id=1, source_target_pairs={{0,8},{8,0},{16,24},{24,16},{1,9},{9,1},{17,25},{25,17},{2,10},{10... | collective-permute-start | bytes 2457608 | tf_op jit(solution)/shard_map/ppermute | solution.py:64
  79.8 17.1 %collective-permute-start.17 = (bf16[128,1280]{1,0:T(8,128)(2,1)S(1)}, bf16[128,1280]{1,0:T(8,128)(2,1)S(1)}, u32[]{:S(2)}, u32[]{:S(2)}) collective-permute-start(bf16[128,1280]{1,0:T(8,128)(2,1)S(1)} %text_theirs_last.1), channel_id=1, source_target_pairs={{0,4},{1,5},{2,6},{3,7},{4,0},{5,1},{6,2},{7,3},{8,12},{9,13},{10,... | collective-permute-start | bytes 983048 | tf_op jit(solution)/shard_map/ppermute | solution.py:64
  (13 other events, 45.6 us)

commit v7 on v6

--- a/solution.py
+++ b/solution.py
@@ -282,11 +282,23 @@
     out_ref[...] = total_ref[...] + feed_forward(normed_ref[...], pieces)
 
 
-def theirs_last_kernel(normed_ref, total_ref, up_ref, other_up_ref, down_ref, other_down_ref, out_ref):
-    def both(mine_ref, other_ref):
-        return lambda: jnp.concatenate([mine_ref[...], other_ref[...]], axis=0)
-
-    total = feed_forward(normed_ref[...], [(both(up_ref, other_up_ref), None, both(down_ref, other_down_ref))])
+def theirs_last_kernel(normed_ref, total_ref, *refs):
+    halves, out_ref, (up, down, sems) = refs[:4], refs[4], refs[5:]
+    half = up.shape[1] // 2
+    pairs = [
+        (ref, (up, down)[at // 2].at[0, pl.ds(at % 2 * half, half)]) for at, ref in enumerate(halves)
+    ]
+    copies = start_copies(pairs, sems)
+
+    def both(at):
+        def read():
+            for copy in copies[at : at + 2]:
+                copy.wait()
+            return (up, down)[at // 2][0]
+
+        return read
+
+    total = feed_forward(normed_ref[...], [(both(0), None, both(2))])
     out_ref[...] = (total_ref[...] + total).astype(BF16)
 
 
@@ -453,7 +465,15 @@
         )
         across_down = after(across_down, text_normed)
         halves = (across_up, swap(across_up, "seq", 1), across_down, swap(across_down, "seq", 1))
-        theirs = call(theirs_last_kernel, "text_theirs_last", like(text_embed), (text_normed, total, *halves))
+        theirs = call(
+            theirs_last_kernel,
+            "text_theirs_last",
+            like(text_embed),
+            (text_normed, total, *halves),
+            stored=(2, 3, 4, 5),
+            copies=4,
+            scratch=tuple(pltpu.VMEM((1, *text_up.shape), BF16) for _ in range(2)),
+        )
         mine = call(
             functools.partial(mine_kernel, capacity),
             "text_mine",

time: 98.1 us -> 98.4 us (level)
  no operation moved by 1% of the time
where the time goes in v7:
time: 98.4 us; the launch traced here: 97.9 us
  Pallas kernels  42 us (43%)
  starting transfers between devices  26.2 us (27%)
  waiting for transfers between devices  22.5 us (23%)
  local copies, waits for them, and re-layouts  4.56 us (5%)
  other arithmetic  2.24 us (2%)
    pallas_call x16, Pallas kernels, call(): pl.pallas_call(kernel, out_shape=out_shape, in_specs=specs, out_specs=tup...  42 us
    ppermute x14, waiting for transfers between devices, swap(): return lax.ppermute(x, axis, [(i, i ^ bit) for i in range(size)])  16.4 us
    ppermute x14, starting transfers between devices, swap(): return lax.ppermute(x, axis, [(i, i ^ bit) for i in range(size)])  13.7 us
    ppermute x4, starting transfers between devices, swap_by_core(): return lax.ppermute(x, ('seq', 'blk'), pairs)  7.58 us
    all_to_all x1, waiting for transfers between devices, per_device(): got = lax.all_to_all(send, 'blk', split_axis=0, concat_axis=0, tiled=True)  6.06 us
    all_to_all x1, starting transfers between devices, per_device(): got = lax.all_to_all(send, 'blk', split_axis=0, concat_axis=0, tiled=True)  4.93 us
    unnamed x37, local copies, waits for them, and re-layouts  4.47 us
  transfers between devices with their start and end apart: 19, of which 6 were waited for; matrix products, arithmetic and copies ran while one was open for 2% of the time, Pallas kernels for 40%

profile of v7, /device:TPU:0, one launch (start us, length us, event | category | flops | bytes accessed | tf_op | source)
XLA Modules:
  0.0 97.9 jit_solution(15855470794961018991)
XLA Ops:
  0.5 3.0 %collective-permute-start.5 = (bf16[640,1280]{1,0:T(8,128)(2,1)}, bf16[640,1280]{1,0:T(8,128)(2,1)}, u32[]{:S(2)}, u32[]{:S(2)}) collective-permute-start(bf16[640,1280]{1,0:T(8,128)(2,1)} %refs_0_.4), channel_id=1, source_target_pairs={{0,1},{1,0},{2,3},{3,2},{4,5},{5,4},{6,7},{7,6},{8,10},{9,11},{10,... | collective-permute-start | bytes 4915208 | tf_op jit(solution)/shard_map/ppermute | solution.py:70
  3.5 2.6 %norm_patches.1 = (bf16[128,1280]{1,0:T(8,128)(2,1)}, bf16[128,1280]{1,0:T(8,128)(2,1)}, f32[8,128]{1,0:T(8,128)}) custom-call(bf16[256,1280]{1,0:T(8,128)(2,1)} %patches_ref.3, f32[1280]{0:T(1024)} %gain_ref.2), custom_call_target="tpu_custom_call" | custom-call | flops 1000000 | bytes 1000 | tf_op jit(solution)/shard_map/norm_patches/pallas_call | solution.py:32
  10.7 1.7 %copy-done.4 = bf16[1280,1280]{1,0:T(8,128)(2,1)S(1)} copy-done((bf16[1280,1280]{1,0:T(8,128)(2,1)S(1)}, bf16[1280,1280]{1,0:T(8,128)(2,1)}, u32[]{:S(2)}) %copy-start.4) | copy-done | bytes 3276824
  12.4 2.3 %bring_vision.1 = (bf16[1280,1280]{1,0:T(8,128)(2,1)S(1)}, bf16[1280,1280]{1,0:T(8,128)(2,1)S(1)}) custom-call(bf16[1280,1280]{1,0:T(8,128)(2,1)S(1)} %copy-done.4, bf16[1280,1280]{1,0:T(8,128)(2,1)} %da.1, f32[8,128]{1,0:T(8,128)S(1)} %copy-done.15), custom_call_target="tpu_custom_call" | custom-call | flops 1000000 | bytes 1000 | tf_op jit(solution)/shard_map/bring_vision/pallas_call | solution.py:32
  14.8 2.2 %collective-permute-done.rows_ref = bf16[128,1280]{1,0:T(8,128)(2,1)} collective-permute-done((bf16[128,1280]{1,0:T(8,128)(2,1)}, bf16[128,1280]{1,0:T(8,128)(2,1)}, u32[]{:S(2)}, u32[]{:S(2)}) %collective-permute-start) | collective-permute-done | bytes 327712 | tf_op jit(solution)/shard_map/ppermute | solution.py:64
  17.0 5.5 %vision_first.1 = (bf16[128,1280]{1,0:T(8,128)(2,1)S(1)}, f32[8,128]{1,0:T(8,128)S(1)}, bf16[1280,1280]{1,0:T(8,128)(2,1)S(1)}, bf16[1280,1280]{1,0:T(8,128)(2,1)S(1)}) custom-call(bf16[128,1280]{1,0:T(8,128)(2,1)} %collective-permute-done.rows_ref, bf16[1280,1280]{1,0:T(8,128)(2,1)S(1)} %get-tuple-element.30.ua, f32[1280]{0:T(1024)S(1)} %copy-done.13, ...), custom_call_target="tpu_custom_call" | custom-call | flops 1000000 | bytes 1000 | tf_op jit(solution)/shard_map/vision_first/pallas_call | solution.py:32
  22.5 2.0 %collective-permute-start.6 = (bf16[128,1280]{1,0:T(8,128)(2,1)S(1)}, bf16[128,1280]{1,0:T(8,128)(2,1)S(1)}, u32[]{:S(2)}, u32[]{:S(2)}) collective-permute-start(bf16[128,1280]{1,0:T(8,128)(2,1)S(1)} %get-tuple-element.36), channel_id=1, source_target_pairs={{0,16},{8,24},{16,0},{24,8},{1,17},{9,25},{17,1},{25,9},{2,18},{10... | collective-permute-start | bytes 983048 | tf_op jit(solution)/shard_map/ppermute | solution.py:64
  24.5 4.1 %vision_second.1 = (bf16[640,1280]{1,0:T(8,128)(2,1)}, bf16[160,1280]{1,0:T(8,128)(2,1)S(1)}, bf16[128,1280]{1,0:T(8,128)(2,1)S(1)}, bf16[128,1280]{1,0:T(8,128)(2,1)S(1)}, f32[8,128]{1,0:T(8,128)S(1)}) custom-call(s32[2]{0:T(128)S(1)} %pad_add_fusion.core_ref.place_ref, ...), custom_call_target="tpu_custom_call", output_to_operand_aliasing={{0}: (9, {})} | custom-call | flops 30000001024 | bytes 1000 | tf_op jit(solution)/shard_map/vision_second/pallas_call | solution.py:32
  29.1 1.8 %collective-permute-start.12 = (bf16[160,1280]{1,0:T(8,128)(2,1)S(1)}, bf16[160,1280]{1,0:T(8,128)(2,1)S(1)}, u32[]{:S(2)}, u32[]{:S(2)}) collective-permute-start(bf16[160,1280]{1,0:T(8,128)(2,1)S(1)} %get-tuple-element.43), channel_id=1, source_target_pairs={{0,2},{1,3},{2,0},{3,1},{4,6},{5,7},{6,4},{7,5},{8,9},{9,8},{10,11... | collective-permute-start | bytes 1228808 | tf_op jit(solution)/shard_map/ppermute | solution.py:70
  30.9 2.6 %collective-permute-start.11 = (bf16[128,1280]{1,0:T(8,128)(2,1)S(1)}, bf16[128,1280]{1,0:T(8,128)(2,1)S(1)}, u32[]{:S(2)}, u32[]{:S(2)}) collective-permute-start(bf16[128,1280]{1,0:T(8,128)(2,1)S(1)} %get-tuple-element.42), channel_id=1, source_target_pairs={{0,4},{1,5},{2,6},{3,7},{4,0},{5,1},{6,2},{7,3},{8,12},{9,13},{10,... | collective-permute-start | bytes 983048 | tf_op jit(solution)/shard_map/ppermute | solution.py:64
  33.5 4.8 %vision_own.1 = (f32[256,1280]{1,0:T(8,128)S(1)}, bf16[5120,1280]{1,0:T(8,128)(2,1)S(1)}) custom-call(bf16[128,1280]{1,0:T(8,128)(2,1)S(1)} %copy-done.16, bf16[128,1280]{1,0:T(8,128)(2,1)S(1)} %copy-done.17, bf16[1280,1280]{1,0:T(8,128)(2,1)S(1)} %get-tuple-element.30.ua, f32[1280]{0:T(1024)S(1)} %copy-done.13, ...), custom_call_target="tpu_custom_call" | custom-call | flops 10000000000 | bytes 1000 | tf_op jit(solution)/shard_map/vision_own/pallas_call | solution.py:32
  39.1 4.6 %merge_rows.1.refs_1_.refs_0_.refs_2_ = bf16[256,1408]{1,0:T(8,128)(2,1)} custom-call(bf16[256,1280]{1,0:T(8,128)(2,1)S(1)} %copy-done.5, f32[256,1280]{1,0:T(8,128)S(1)} %get-tuple-element.37.own_ref, bf16[128,1280]{1,0:T(8,128)(2,1)S(1)} %collective-permute-done.7.back_ref, f32[1280]{0:T(1024)S(1)} %copy-done.14, ...), custom_call_target="tpu_custom_call" | custom-call | flops 1000000 | bytes 1000 | tf_op jit(solution)/shard_map/merge_rows/pallas_call | solution.py:32
  43.6 4.9 %all-to-all-start = ((bf16[8,32,1408]{2,1,0:T(8,128)(2,1)}), bf16[8,32,1408]{2,1,0:T(8,128)(2,1)}, u32[]{:S(2)}, u32[]{:S(2)}) async-start(bf16[8,32,1408]{2,1,0:T(8,128)(2,1)} %bitcast.2), calls=%async_computation | async-start | bytes 1441792 | tf_op jit(solution)/shard_map/all_to_all | solution.py:436
  48.6 1.6 %collective-permute-start.13 = (bf16[160,1280]{1,0:T(8,128)(2,1)S(1)}, bf16[160,1280]{1,0:T(8,128)(2,1)S(1)}, u32[]{:S(2)}, u32[]{:S(2)}) collective-permute-start(bf16[160,1280]{1,0:T(8,128)(2,1)S(1)} %get-tuple-element.44.mine_ref), channel_id=1, source_target_pairs={{0,16},{8,24},{16,0},{24,8},{1,17},{9,25},{17,1},{25,9},{2,18},{10... | collective-permute-start | bytes 1228808 | tf_op jit(solution)/shard_map/ppermute | solution.py:64
  50.2 2.1 %collective-permute-start.9 = (bf16[640,1280]{1,0:T(8,128)(2,1)}, bf16[640,1280]{1,0:T(8,128)(2,1)}, u32[]{:S(2)}, u32[]{:S(2)}) collective-permute-start(bf16[640,1280]{1,0:T(8,128)(2,1)} %get-tuple-element.40.refs_2_), channel_id=1, source_target_pairs={{0,8},{8,0},{16,24},{24,16},{1,9},{9,1},{17,25},{25,17},{2,10},{10... | collective-permute-start | bytes 4915208 | tf_op jit(solution)/shard_map/ppermute | solution.py:64
  53.4 2.8 %collective-permute-start.15 = (bf16[320,1280]{1,0:T(8,128)(2,1)}, bf16[320,1280]{1,0:T(8,128)(2,1)S(1)}, u32[]{:S(2)}, u32[]{:S(2)}) collective-permute-start(bf16[320,1280]{1,0:T(8,128)(2,1)} %get-tuple-element.45), channel_id=1, source_target_pairs={{0,2},{1,3},{2,0},{3,1},{4,6},{5,7},{6,4},{7,5},{8,9},{9,8},{10,11... | collective-permute-start | bytes 2457608 | tf_op jit(solution)/shard_map/ppermute | solution.py:70
  56.3 3.2 %collective-permute-done.13.other_ref = bf16[160,1280]{1,0:T(8,128)(2,1)S(1)} collective-permute-done((bf16[160,1280]{1,0:T(8,128)(2,1)S(1)}, bf16[160,1280]{1,0:T(8,128)(2,1)S(1)}, u32[]{:S(2)}, u32[]{:S(2)}) %collective-permute-start.13) | collective-permute-done | bytes 409632 | tf_op jit(solution)/shard_map/ppermute | solution.py:64
  61.1 1.8 %collective-permute-start.14 = (bf16[320,1280]{1,0:T(8,128)(2,1)S(1)}, bf16[320,1280]{1,0:T(8,128)(2,1)}, u32[]{:S(2)}, u32[]{:S(2)}) collective-permute-start(bf16[320,1280]{1,0:T(8,128)(2,1)S(1)} %order_across.1.refs_6_.refs_0_), channel_id=1, source_target_pairs={{0,8},{8,0},{16,24},{24,16},{1,9},{9,1},{17,25},{25,17},{2,10},{10... | collective-permute-start | bytes 2457608 | tf_op jit(solution)/shard_map/ppermute | solution.py:64
  62.9 6.1 %all-to-all-done = bf16[8,32,1408]{2,1,0:T(8,128)(2,1)} async-done(((bf16[8,32,1408]{2,1,0:T(8,128)(2,1)}), bf16[8,32,1408]{2,1,0:T(8,128)(2,1)}, u32[]{:S(2)}, u32[]{:S(2)}) %all-to-all-start) | async-done | bytes 720928 | tf_op jit(solution)/shard_map/all_to_all | solution.py:436
  69.9 4.6 %text_theirs.1 = (bf16[128,1280]{1,0:T(8,128)(2,1)S(1)}, f32[128,1280]{1,0:T(8,128)S(1)}) custom-call(bf16[128,1280]{1,0:T(8,128)(2,1)S(1)} %copy-done.9, bf16[256,1408]{1,0:T(8,128)(2,1)} %after.4.got_ref, bf16[640,1280]{1,0:T(8,128)(2,1)} %refs_0_.4, bf16[640,1280]{1,0:T(8,128)(2,1)} %refs_1_.5, bf16[640,1280]{1,0:T(8,128)(2,1)} %get-tuple-element.40.refs_2_, ...), custom_call_target="tpu_custom_call" | custom-call | flops 1000000 | bytes 1000 | tf_op jit(solution)/shard_map/text_theirs/pallas_call | solution.py:32
  74.7 2.6 %text_theirs_more.1.total_ref = f32[128,1280]{1,0:T(8,128)S(1)} custom-call(bf16[128,1280]{1,0:T(8,128)(2,1)S(1)} %get-tuple-element.47.refs_1_.normed_ref, f32[128,1280]{1,0:T(8,128)S(1)} %get-tuple-element.48.total_ref, bf16[640,1280]{1,0:T(8,128)(2,1)} %collective-permute-done.9.refs_4_.up_ref, bf16[640,1280]{1,0:T(8,128)(2,1)} %collective-permute-done.10.refs_5_.down_ref), custom_call_target="tpu_custom_call" | custom-call | flops 1000000 | bytes 1000 | tf_op jit(solution)/shard_map/text_theirs_more/pallas_call | solution.py:32
  77.4 2.6 %text_theirs_last.1 = bf16[128,1280]{1,0:T(8,128)(2,1)S(1)} custom-call(bf16[128,1280]{1,0:T(8,128)(2,1)S(1)} %get-tuple-element.47.refs_1_.normed_ref, f32[128,1280]{1,0:T(8,128)S(1)} %text_theirs_more.1.total_ref, bf16[320,1280]{1,0:T(8,128)(2,1)S(1)} %order_across.1.refs_6_.refs_0_, bf16[320,1280]{1,0:T(8,128)(2,1)} %collective-permute-done.14.refs_7_.refs_1_, ...), custom_call_target="tpu_custom_call" | custom-call | flops 1000000 | bytes 1000 | tf_op jit(solution)/shard_map/text_theirs_last/pallas_call | solution.py:32
  80.1 6.7 %text_mine.1 = f32[128,1280]{1,0:T(8,128)S(1)} custom-call(bf16[128,1280]{1,0:T(8,128)(2,1)S(1)} %copy-done.11, bf16[256,1408]{1,0:T(8,128)(2,1)} %after.4.got_ref, bf16[640,1280]{1,0:T(8,128)(2,1)S(1)} %copy-done.3, bf16[640,1280]{1,0:T(8,128)(2,1)} %refs_1_.5, bf16[640,1280]{1,0:T(8,128)(2,1)} %get-tuple-element.40.refs_2_, ...), custom_call_target="tpu_custom_call" | custom-call | flops 1000000 | bytes 1000 | tf_op jit(solution)/shard_map/text_mine/pallas_call | solution.py:32
  86.8 10.3 %collective-permute-done.17 = bf16[128,1280]{1,0:T(8,128)(2,1)S(1)} collective-permute-done((bf16[128,1280]{1,0:T(8,128)(2,1)S(1)}, bf16[128,1280]{1,0:T(8,128)(2,1)S(1)}, u32[]{:S(2)}, u32[]{:S(2)}) %collective-permute-start.17) | collective-permute-done | bytes 327712 | tf_op jit(solution)/shard_map/ppermute | solution.py:64
  (78 shorter events, 11.0 us)
Async XLA Ops:
  0.0 10.2 %collective-permute-start.1 = (bf16[1280,1280]{1,0:T(8,128)(2,1)}, bf16[1280,1280]{1,0:T(8,128)(2,1)S(1)}, u32[]{:S(2)}, u32[]{:S(2)}) collective-permute-start(bf16[1280,1280]{1,0:T(8,128)(2,1)} %ua.1), channel_id=1, source_target_pairs={{0,8},{8,0},{16,24},{24,16},{1,9},{9,1},{17,25},{25,17},{2,10},{10... | collective-permute-start | bytes 9830408 | tf_op jit(solution)/shard_map/ppermute | solution.py:64
  0.5 16.5 %collective-permute-start.3 = (bf16[1280,1280]{1,0:T(8,128)(2,1)}, bf16[1280,1280]{1,0:T(8,128)(2,1)}, u32[]{:S(2)}, u32[]{:S(2)}) collective-permute-start(bf16[1280,1280]{1,0:T(8,128)(2,1)} %da.1), channel_id=1, source_target_pairs={{0,8},{8,0},{16,24},{24,16},{1,9},{9,1},{17,25},{25,17},{2,10},{10... | collective-permute-start | bytes 9830408 | tf_op jit(solution)/shard_map/ppermute | solution.py:64
  0.5 24.0 %collective-permute-start.5 = (bf16[640,1280]{1,0:T(8,128)(2,1)}, bf16[640,1280]{1,0:T(8,128)(2,1)}, u32[]{:S(2)}, u32[]{:S(2)}) collective-permute-start(bf16[640,1280]{1,0:T(8,128)(2,1)} %refs_0_.4), channel_id=1, source_target_pairs={{0,1},{1,0},{2,3},{3,2},{4,5},{5,4},{6,7},{7,6},{8,10},{9,11},{10,... | collective-permute-start | bytes 4915208 | tf_op jit(solution)/shard_map/ppermute | solution.py:70
  6.0 10.9 %collective-permute-start = (bf16[128,1280]{1,0:T(8,128)(2,1)}, bf16[128,1280]{1,0:T(8,128)(2,1)}, u32[]{:S(2)}, u32[]{:S(2)}) collective-permute-start(bf16[128,1280]{1,0:T(8,128)(2,1)} %get-tuple-element.27.first_ref), channel_id=1, source_target_pairs={{0,16},{8,24},{16,0},{24,8},{1,17},{9,25},{17,1},{25,9},{2,18},{10... | collective-permute-start | bytes 983048 | tf_op jit(solution)/shard_map/ppermute | solution.py:64
  7.5 17.0 %collective-permute-start.4 = (bf16[128,1280]{1,0:T(8,128)(2,1)}, bf16[128,1280]{1,0:T(8,128)(2,1)}, u32[]{:S(2)}, u32[]{:S(2)}) collective-permute-start(bf16[128,1280]{1,0:T(8,128)(2,1)} %get-tuple-element.28.second_ref), channel_id=1, source_target_pairs={{0,16},{8,24},{16,0},{24,8},{1,17},{9,25},{17,1},{25,9},{2,18},{10... | collective-permute-start | bytes 983048 | tf_op jit(solution)/shard_map/ppermute | solution.py:64
  10.2 6.7 %collective-permute-start.2 = (f32[1280]{0:T(1024)S(1)}, f32[1280]{0:T(1024)S(1)}, u32[]{:S(2)}, u32[]{:S(2)}) collective-permute-start(f32[1280]{0:T(1024)S(1)} %after.3), channel_id=1, source_target_pairs={{0,8},{8,0},{16,24},{24,16},{1,9},{9,1},{17,25},{25,17},{2,10},{10... | collective-permute-start | bytes 15368 | tf_op jit(solution)/shard_map/ppermute | solution.py:64
  17.0 35.4 %collective-permute-start.8 = (bf16[640,1280]{1,0:T(8,128)(2,1)}, bf16[640,1280]{1,0:T(8,128)(2,1)S(1)}, u32[]{:S(2)}, u32[]{:S(2)}) collective-permute-start(bf16[640,1280]{1,0:T(8,128)(2,1)} %refs_1_.5), channel_id=1, source_target_pairs={{0,1},{1,0},{2,3},{3,2},{4,5},{5,4},{6,7},{7,6},{8,10},{9,11},{10,... | collective-permute-start | bytes 4915208 | tf_op jit(solution)/shard_map/ppermute | solution.py:70
  22.5 11.0 %collective-permute-start.6 = (bf16[128,1280]{1,0:T(8,128)(2,1)S(1)}, bf16[128,1280]{1,0:T(8,128)(2,1)S(1)}, u32[]{:S(2)}, u32[]{:S(2)}) collective-permute-start(bf16[128,1280]{1,0:T(8,128)(2,1)S(1)} %get-tuple-element.36), channel_id=1, source_target_pairs={{0,16},{8,24},{16,0},{24,8},{1,17},{9,25},{17,1},{25,9},{2,18},{10... | collective-permute-start | bytes 983048 | tf_op jit(solution)/shard_map/ppermute | solution.py:64
  24.5 9.0 %copy-start.16 = (bf16[128,1280]{1,0:T(8,128)(2,1)S(1)}, bf16[128,1280]{1,0:T(8,128)(2,1)}, u32[]{:S(2)}) copy-start(bf16[128,1280]{1,0:T(8,128)(2,1)} %get-tuple-element.27.first_ref) | copy-start | bytes 983044
  24.5 9.0 %copy-start.17 = (bf16[128,1280]{1,0:T(8,128)(2,1)S(1)}, bf16[128,1280]{1,0:T(8,128)(2,1)}, u32[]{:S(2)}) copy-start(bf16[128,1280]{1,0:T(8,128)(2,1)} %get-tuple-element.28.second_ref) | copy-start | bytes 983044
  28.7 10.3 %collective-permute-start.7 = (bf16[128,1280]{1,0:T(8,128)(2,1)S(1)}, bf16[128,1280]{1,0:T(8,128)(2,1)S(1)}, u32[]{:S(2)}, u32[]{:S(2)}) collective-permute-start(bf16[128,1280]{1,0:T(8,128)(2,1)S(1)} %get-tuple-element.38), channel_id=1, source_target_pairs={{0,16},{8,24},{16,0},{24,8},{1,17},{9,25},{17,1},{25,9},{2,18},{10... | collective-permute-start | bytes 983048 | tf_op jit(solution)/shard_map/ppermute | solution.py:64
  29.1 19.5 %collective-permute-start.12 = (bf16[160,1280]{1,0:T(8,128)(2,1)S(1)}, bf16[160,1280]{1,0:T(8,128)(2,1)S(1)}, u32[]{:S(2)}, u32[]{:S(2)}) collective-permute-start(bf16[160,1280]{1,0:T(8,128)(2,1)S(1)} %get-tuple-element.43), channel_id=1, source_target_pairs={{0,2},{1,3},{2,0},{3,1},{4,6},{5,7},{6,4},{7,5},{8,9},{9,8},{10,11... | collective-permute-start | bytes 1228808 | tf_op jit(solution)/shard_map/ppermute | solution.py:70
  30.9 17.7 %collective-permute-start.11 = (bf16[128,1280]{1,0:T(8,128)(2,1)S(1)}, bf16[128,1280]{1,0:T(8,128)(2,1)S(1)}, u32[]{:S(2)}, u32[]{:S(2)}) collective-permute-start(bf16[128,1280]{1,0:T(8,128)(2,1)S(1)} %get-tuple-element.42), channel_id=1, source_target_pairs={{0,4},{1,5},{2,6},{3,7},{4,0},{5,1},{6,2},{7,3},{8,12},{9,13},{10,... | collective-permute-start | bytes 983048 | tf_op jit(solution)/shard_map/ppermute | solution.py:64
  43.6 25.3 %all-to-all-start = ((bf16[8,32,1408]{2,1,0:T(8,128)(2,1)}), bf16[8,32,1408]{2,1,0:T(8,128)(2,1)}, u32[]{:S(2)}, u32[]{:S(2)}) async-start(bf16[8,32,1408]{2,1,0:T(8,128)(2,1)} %bitcast.2), calls=%async_computation | async-start | bytes 1441792 | tf_op jit(solution)/shard_map/all_to_all | solution.py:436
  48.6 7.7 %copy-start.6 = (bf16[160,1280]{1,0:T(8,128)(2,1)}, bf16[160,1280]{1,0:T(8,128)(2,1)S(1)}, u32[]{:S(2)}) copy-start(bf16[160,1280]{1,0:T(8,128)(2,1)S(1)} %get-tuple-element.44.mine_ref) | copy-start | bytes 1228804
  48.6 7.7 %copy-start.8 = (bf16[128,1280]{1,0:T(8,128)(2,1)}, bf16[128,1280]{1,0:T(8,128)(2,1)S(1)}, u32[]{:S(2)}) copy-start(bf16[128,1280]{1,0:T(8,128)(2,1)S(1)} %get-tuple-element.46.embed_ref) | copy-start | bytes 983044
  48.6 10.9 %collective-permute-start.13 = (bf16[160,1280]{1,0:T(8,128)(2,1)S(1)}, bf16[160,1280]{1,0:T(8,128)(2,1)S(1)}, u32[]{:S(2)}, u32[]{:S(2)}) collective-permute-start(bf16[160,1280]{1,0:T(8,128)(2,1)S(1)} %get-tuple-element.44.mine_ref), channel_id=1, source_target_pairs={{0,16},{8,24},{16,0},{24,8},{1,17},{9,25},{17,1},{25,9},{2,18},{10... | collective-permute-start | bytes 1228808 | tf_op jit(solution)/shard_map/ppermute | solution.py:64
  50.2 24.5 %collective-permute-start.9 = (bf16[640,1280]{1,0:T(8,128)(2,1)}, bf16[640,1280]{1,0:T(8,128)(2,1)}, u32[]{:S(2)}, u32[]{:S(2)}) collective-permute-start(bf16[640,1280]{1,0:T(8,128)(2,1)} %get-tuple-element.40.refs_2_), channel_id=1, source_target_pairs={{0,8},{8,0},{16,24},{24,16},{1,9},{9,1},{17,25},{25,17},{2,10},{10... | collective-permute-start | bytes 4915208 | tf_op jit(solution)/shard_map/ppermute | solution.py:64
  53.4 15.6 %copy-start = (bf16[640,1280]{1,0:T(8,128)(2,1)}, bf16[640,1280]{1,0:T(8,128)(2,1)S(1)}, u32[]{:S(2)}) copy-start(bf16[640,1280]{1,0:T(8,128)(2,1)S(1)} %get-tuple-element.41.refs_3_) | copy-start | bytes 4915204
  53.4 21.3 %collective-permute-start.10 = (bf16[640,1280]{1,0:T(8,128)(2,1)S(1)}, bf16[640,1280]{1,0:T(8,128)(2,1)}, u32[]{:S(2)}, u32[]{:S(2)}) collective-permute-start(bf16[640,1280]{1,0:T(8,128)(2,1)S(1)} %get-tuple-element.41.refs_3_), channel_id=1, source_target_pairs={{0,8},{8,0},{16,24},{24,16},{1,9},{9,1},{17,25},{25,17},{2,10},{10... | collective-permute-start | bytes 4915208 | tf_op jit(solution)/shard_map/ppermute | solution.py:64
  53.4 21.1 %collective-permute-start.15 = (bf16[320,1280]{1,0:T(8,128)(2,1)}, bf16[320,1280]{1,0:T(8,128)(2,1)S(1)}, u32[]{:S(2)}, u32[]{:S(2)}) collective-permute-start(bf16[320,1280]{1,0:T(8,128)(2,1)} %get-tuple-element.45), channel_id=1, source_target_pairs={{0,2},{1,3},{2,0},{3,1},{4,6},{5,7},{6,4},{7,5},{8,9},{9,8},{10,11... | collective-permute-start | bytes 2457608 | tf_op jit(solution)/shard_map/ppermute | solution.py:70
  61.1 16.3 %collective-permute-start.14 = (bf16[320,1280]{1,0:T(8,128)(2,1)S(1)}, bf16[320,1280]{1,0:T(8,128)(2,1)}, u32[]{:S(2)}, u32[]{:S(2)}) collective-permute-start(bf16[320,1280]{1,0:T(8,128)(2,1)S(1)} %order_across.1.refs_6_.refs_0_), channel_id=1, source_target_pairs={{0,8},{8,0},{16,24},{24,16},{1,9},{9,1},{17,25},{25,17},{2,10},{10... | collective-permute-start | bytes 2457608 | tf_op jit(solution)/shard_map/ppermute | solution.py:64
  74.6 2.8 %collective-permute-start.16 = (bf16[320,1280]{1,0:T(8,128)(2,1)S(1)}, bf16[320,1280]{1,0:T(8,128)(2,1)S(1)}, u32[]{:S(2)}, u32[]{:S(2)}) collective-permute-start(bf16[320,1280]{1,0:T(8,128)(2,1)S(1)} %after.5.refs_8_.refs_2_), channel_id=1, source_target_pairs={{0,8},{8,0},{16,24},{24,16},{1,9},{9,1},{17,25},{25,17},{2,10},{10... | collective-permute-start | bytes 2457608 | tf_op jit(solution)/shard_map/ppermute | solution.py:64
  80.0 17.1 %collective-permute-start.17 = (bf16[128,1280]{1,0:T(8,128)(2,1)S(1)}, bf16[128,1280]{1,0:T(8,128)(2,1)S(1)}, u32[]{:S(2)}, u32[]{:S(2)}) collective-permute-start(bf16[128,1280]{1,0:T(8,128)(2,1)S(1)} %text_theirs_last.1), channel_id=1, source_target_pairs={{0,4},{1,5},{2,6},{3,7},{4,0},{5,1},{6,2},{7,3},{8,12},{9,13},{10,... | collective-permute-start | bytes 983048 | tf_op jit(solution)/shard_map/ppermute | solution.py:64
  (13 other events, 46.5 us)
